TPU v7x, 32 devices: a whole 2x2x4 slice. The times are simulated.
32 devices in a mesh: seq: 8 (over z, y), ch: 4 (over x, core).
Axes of the slice: x: 2, y: 2, z: 4, core: 2. Of those that a mesh axis runs over, the one named last changes fastest.
Arguments:
- frames_in: bfloat16 [16384, 1024], P('seq'), may hold values from -6 to 6
- w_in: bfloat16 [1024, 3, 1024], P(None, None, 'ch'), may hold values from -0.1875 to 0.1875
- filters: bfloat16 [16384, 1024], P('seq', 'ch'), may hold values from -1.5 to 1.5
- skip_gain: float32 [1024], P('ch'), may hold values from -1 to 1
- w_out: bfloat16 [1024, 1024], P('ch'), may hold values from -0.1875 to 0.1875
Outputs:
- mixed: bfloat16 [16384, 1024], P('seq', 'ch')
All inputs are finite; a program needn't handle non-finite values.
Results may differ from a plain program's by a relative error of at most 0.01.
Values may be sent and summed in bfloat16 or wider, within the bound.
No kernel may reach another device: no remote copies, remote signals or barrier semaphores. Data moves between devices by JAX's collectives and lax.ppermute only.
A program may use at most 128 MiB of HBM per device.

v0:
```python
import functools
import math

import jax
import jax.numpy as jnp
import numpy as np
from jax import lax
from jax.experimental import pallas as pl
from jax.experimental.pallas import tpu as pltpu
from jax.sharding import PartitionSpec as P

LANES = 128
CHUNKS = 4
BF16 = jnp.bfloat16
F32 = jnp.float32


def dot(left, right):
    return jnp.dot(left, right, preferred_element_type=F32)


def cost(flops, data):
    return pl.CostEstimate(flops=int(flops), bytes_accessed=int(data), transcendentals=0)


def params(mib):
    return pltpu.CompilerParams(vmem_limit_bytes=mib * 1024 * 1024)


def tables(rows):
    total = rows * LANES
    r = np.arange(rows, dtype=np.float64)
    l = np.arange(LANES, dtype=np.float64)
    first = 2 * np.pi * np.outer(r + 0.25, r) / rows
    twist = 2 * np.pi * np.outer(r + 0.25, l) / total
    second = 2 * np.pi * np.outer(l, l) / LANES
    a_fwd = np.concatenate([np.cos(first), -np.sin(first)], 0)
    a_inv = np.concatenate([np.cos(first).T, -np.sin(first).T], 1) / rows
    c2, s2 = np.cos(second), np.sin(second)
    b_fwd = np.block([[c2, -s2], [s2, c2]])
    b_inv = np.block([[c2, s2], [-s2, c2]]) / LANES
    as_bf = lambda v: jnp.asarray(v.astype(np.float32)).astype(BF16)
    as_f = lambda v: jnp.asarray(v.astype(np.float32))
    return (as_bf(a_fwd), as_bf(b_fwd), as_bf(b_inv), as_bf(a_inv), as_f(np.cos(twist)), as_f(np.sin(twist)))


def seq_peer(step):
    return lax.bitwise_xor(lax.axis_index("seq"), jnp.int32(step))


def filter_kernel(seq, cpc, f_ref, *rest):
    outs, (turned,) = rest[:seq], rest[seq:]
    frames, chans = f_ref.shape
    rows = frames // LANES
    group = seq * cpc
    for r in range(rows):
        turned[pl.ds(r, chans, stride=rows), :] = f_ref[pl.ds(r * LANES, LANES), :].astype(F32).T
    for d in range(seq):
        peer = seq_peer(d)
        for k in range(chans // group):
            start = pl.multiple_of((k * group + peer * cpc) * rows, 8)
            part = turned[pl.ds(start, cpc * rows), :].reshape(cpc, rows, LANES)
            outs[d][pl.ds(k * cpc, cpc)] = part.astype(BF16)


def prepare_filters(filters, seq, cpc):
    frames, chans = filters.shape
    rows = frames // LANES
    return pl.pallas_call(
        functools.partial(filter_kernel, seq, cpc),
        out_shape=[jax.ShapeDtypeStruct((chans // seq, rows, LANES), BF16)] * seq,
        scratch_shapes=[pltpu.VMEM((chans * rows, LANES), F32)],
        compiler_params=params(24),
        cost_estimate=cost(0, 8 * frames * chans),
        name="filter_blocks",
    )(filters)


def project_kernel(seq, cpc, x_ref, w_ref, gate_ref, sig_ref, *rest):
    outs, (turned,) = rest[:-1], rest[-1:]
    tile = x_ref.shape[0]
    chans = gate_ref.shape[1]
    step = pl.program_id(0)
    rows_here = tile // LANES
    rows = rows_here * pl.num_programs(0)
    x = x_ref[...]
    gate = dot(x, w_ref[0]).astype(BF16).astype(F32)
    key = dot(x, w_ref[1]).astype(BF16).astype(F32)
    value = dot(x, w_ref[2]).astype(BF16).astype(F32)
    signal = key * value
    for r in range(rows_here):
        here = slice(r * LANES, (r + 1) * LANES)
        gate_ref[r] = gate[here].T.astype(BF16)
        flipped = signal[here].T
        sig_ref[r] = flipped.astype(BF16)
        turned[pl.ds(step * rows_here + r, chans, stride=16), :] = flipped

    @pl.when(step == pl.num_programs(0) - 1)
    def _():
        group = seq * cpc
        for d in range(seq):
            peer = seq_peer(d)
            for k in range(chans // group):
                start = pl.multiple_of((k * group + peer * cpc) * 16, 8)
                part = turned[pl.ds(start, cpc * 16), :].reshape(cpc, 16, LANES)
                outs[d * (chans // group) + k][...] = part.astype(BF16)


def project(frames_in, w_in, seq, cpc):
    frames, width = frames_in.shape
    chans = w_in.shape[2]
    rows = frames // LANES
    tile = 512
    blocks = seq * (chans // (seq * cpc))
    by_row = pl.BlockSpec((tile // LANES, chans, LANES), lambda i: (i, 0, 0))
    whole = lambda *shape: pl.BlockSpec(shape, lambda i: (0,) * len(shape))
    return pl.pallas_call(
        functools.partial(project_kernel, seq, cpc),
        grid=(frames // tile,),
        in_specs=[pl.BlockSpec((tile, width), lambda i: (i, 0)), whole(3, width, chans)],
        out_specs=[by_row, by_row] + [whole(cpc, rows, LANES)] * blocks,
        out_shape=[jax.ShapeDtypeStruct((rows, chans, LANES), BF16)] * 2
        + [jax.ShapeDtypeStruct((cpc, rows, LANES), BF16)] * blocks,
        scratch_shapes=[pltpu.VMEM((chans * rows, LANES), F32)],
        compiler_params=params(40),
        cost_estimate=cost(6 * frames * width * chans, 16 * 1024 * 1024),
        name="project",
    )(frames_in, w_in)


def conv_kernel(seq, cpc, rows, *refs):
    s_refs, f_refs = refs[:seq], refs[seq : 2 * seq]
    a_fwd, b_fwd, b_inv, a_inv, tc_ref, ts_ref = refs[2 * seq : 2 * seq + 6]
    y_refs = refs[2 * seq + 6 : 3 * seq + 6]
    grid_sf, grid_y = refs[3 * seq + 6 :]
    full = rows * seq
    for d in range(seq):
        place = pl.ds(pl.multiple_of(seq_peer(d) * rows, 16), rows)
        grid_sf[:, place, :LANES] = s_refs[d][...]
        grid_sf[:, place, LANES:] = f_refs[d][...]
    for c in range(cpc):
        tc, ts = tc_ref[...], ts_ref[...]
        outer = dot(a_fwd[...], grid_sf[c])
        parts = []
        for side in (slice(0, LANES), slice(LANES, 2 * LANES)):
            re, im = outer[:full, side], outer[full:, side]
            parts.append(
                jnp.concatenate([re * tc + im * ts, im * tc - re * ts], 1).astype(BF16)
            )
        spec_s, spec_f = dot(parts[0], b_fwd[...]), dot(parts[1], b_fwd[...])
        sr, si = spec_s[:, :LANES], spec_s[:, LANES:]
        fr, fi = spec_f[:, :LANES], spec_f[:, LANES:]
        prod = jnp.concatenate([sr * fr - si * fi, sr * fi + si * fr], 1).astype(BF16)
        inner = dot(prod, b_inv[...])
        re, im = inner[:, :LANES], inner[:, LANES:]
        back = jnp.concatenate([re * tc - im * ts, im * tc + re * ts], 0).astype(BF16)
        grid_y[c] = dot(a_inv[...], back).astype(BF16)
    for d in range(seq):
        place = pl.ds(pl.multiple_of(seq_peer(d) * rows, 16), rows)
        y_refs[d][...] = grid_y[:, place, :]


def convolve(sig_blocks, filt_blocks, consts, chunk):
    seq = len(sig_blocks)
    cpc, rows, _ = sig_blocks[0].shape
    full = rows * seq
    block = lambda k: pl.BlockSpec((cpc, rows, LANES), lambda i: (k, 0, 0))
    whole = lambda v: pl.BlockSpec(v.shape, lambda i: (0,) * v.ndim)
    return pl.pallas_call(
        functools.partial(conv_kernel, seq, cpc, rows),
        grid=(1,),
        in_specs=[block(0)] * seq + [block(chunk)] * seq + [whole(v) for v in consts],
        out_specs=[block(0)] * seq,
        out_shape=[jax.ShapeDtypeStruct((cpc, rows, LANES), BF16)] * seq,
        scratch_shapes=[
            pltpu.VMEM((cpc, full, 2 * LANES), BF16),
            pltpu.VMEM((cpc, full, LANES), BF16),
        ],
        compiler_params=params(40),
        cost_estimate=cost(cpc * full * LANES * LANES * 64, cpc * full * LANES * 6),
        name="convolve",
    )(*sig_blocks, *filt_blocks, *consts)


def gate_kernel(seq, cpc, *refs):
    y_refs = refs[:seq]
    gate_ref, sig_ref, skip_ref, out_ref, grid_y = refs[seq:]
    rows, group, _ = out_ref.shape
    for d in range(seq):
        start = pl.multiple_of(seq_peer(d) * (cpc * rows), 8)
        grid_y[pl.ds(start, cpc * rows), :] = (
            y_refs[d][...].astype(F32).reshape(cpc * rows, LANES)
        )
    skip = skip_ref[...]
    for r in range(rows):
        y = grid_y[pl.ds(r, group, stride=rows), :]
        out_ref[r] = (gate_ref[r].astype(F32) * (y + skip * sig_ref[r].astype(F32))).astype(BF16)


def apply_gate(y_blocks, gate, signal, skip, chunk):
    seq = len(y_blocks)
    cpc, rows, _ = y_blocks[0].shape
    group = seq * cpc
    block = pl.BlockSpec((cpc, rows, LANES), lambda i: (0, 0, 0))
    part = pl.BlockSpec((rows, group, LANES), lambda i: (0, chunk, 0))
    return pl.pallas_call(
        functools.partial(gate_kernel, seq, cpc),
        grid=(1,),
        in_specs=[block] * seq + [part, part, pl.BlockSpec((group, 1), lambda i: (chunk, 0))],
        out_specs=pl.BlockSpec((rows, group, LANES), lambda i: (0, 0, 0)),
        out_shape=jax.ShapeDtypeStruct((rows, group, LANES), BF16),
        scratch_shapes=[pltpu.VMEM((group * rows, LANES), F32)],
        compiler_params=params(24),
        cost_estimate=cost(0, 10 * rows * group * LANES),
        name="apply_gate",
    )(*y_blocks, gate, signal, skip)


def out_weights_kernel(ways, w_ref, *outs):
    depth = w_ref.shape[1] // ways
    for d in range(ways):
        peer = lax.bitwise_xor(lax.axis_index("ch"), jnp.int32(d))
        cols = pl.ds(pl.multiple_of(peer * depth, LANES), depth)
        outs[d][...] = w_ref[:, cols].astype(F32).T.astype(BF16)


def out_weights(w_out, ways):
    chans, width = w_out.shape
    return pl.pallas_call(
        functools.partial(out_weights_kernel, ways),
        out_shape=[jax.ShapeDtypeStruct((width // ways, chans), BF16)] * ways,
        compiler_params=params(24),
        cost_estimate=cost(0, 4 * chans * width),
        name="out_weights",
    )(w_out)


def mix_kernel(ways, chunks, *refs):
    w_refs, g_refs, out_ref = refs[:ways], refs[ways:-1], refs[-1]
    rows = g_refs[0].shape[0]
    for r in range(0, rows, 2):
        total = None
        for d in range(ways):
            pieces = g_refs[d * chunks : (d + 1) * chunks]
            left = jnp.concatenate([p[r] for p in pieces], 0)
            right = jnp.concatenate([p[r + 1] for p in pieces], 0)
            term = dot(w_refs[d][...], jnp.concatenate([left, right], 1))
            total = term if total is None else total + term
        out_ref[pl.ds(r * LANES, 2 * LANES), :] = total.T.astype(BF16)


def mix(weights, gated):
    ways, chunks = len(weights), len(gated[0])
    rows, group, _ = gated[0][0].shape
    depth, chans = weights[0].shape
    step = 4
    return pl.pallas_call(
        functools.partial(mix_kernel, ways, chunks),
        grid=(rows // step,),
        in_specs=[pl.BlockSpec((depth, chans), lambda i: (0, 0))] * ways
        + [pl.BlockSpec((step, group, LANES), lambda i: (i, 0, 0))] * (ways * chunks),
        out_specs=pl.BlockSpec((step * LANES, depth), lambda i: (i, 0)),
        out_shape=jax.ShapeDtypeStruct((rows * LANES, depth), BF16),
        compiler_params=params(40),
        cost_estimate=cost(2 * rows * LANES * depth * chans * ways, 6 * 1024 * 1024),
        name="mix",
    )(*weights, *[piece for way in gated for piece in way])


def swap(value, axis, step):
    size = lax.axis_size(axis)
    return lax.ppermute(value, axis, [(i, i ^ step) for i in range(size)])


def exchange(blocks):
    return [b if d == 0 else swap(b, "seq", d) for d, b in enumerate(blocks)]


def on_device(frames_in, w_in, filters, skip_gain, w_out):
    seq, ways = lax.axis_size("seq"), lax.axis_size("ch")
    frames, width = frames_in.shape
    chans = filters.shape[1]
    cpc = chans // (seq * CHUNKS)
    consts = tables(seq * frames // LANES)
    filt = exchange(prepare_filters(filters, seq, cpc))
    weights = [
        w if d == 0 else swap(w, "ch", d) for d, w in enumerate(out_weights(w_out, ways))
    ]
    gate, signal, *sends = project(frames_in, w_in.transpose(1, 0, 2), seq, cpc)
    skip = skip_gain[:, None]
    gated = [[] for _ in range(ways)]
    sig = [exchange([sends[d * CHUNKS + k] for d in range(seq)]) for k in range(CHUNKS)]
    for k in range(CHUNKS):
        y = exchange(convolve(sig[k], filt, consts, k))
        mine = apply_gate(y, gate, signal, skip, k)
        gated[0].append(mine)
        far = swap(mine, "ch", 2)
        gated[2].append(far)
        gated[1].append(swap(mine, "ch", 1))
        gated[3].append(swap(far, "ch", 1))
    return mix(weights, gated)


def solution(mesh):
    in_specs = (P("seq", None), P(None, None, "ch"), P("seq", "ch"), P("ch"), P("ch", None))
    out_specs = P("seq", "ch")
    return jax.shard_map(
        on_device, mesh=mesh, in_specs=in_specs, out_specs=out_specs, check_vma=False
    )
```

profile of v0, /device:TPU:0, one launch (start us, length us, event | category | flops | bytes accessed | tf_op | source)
XLA Modules:
  0.0 190.2 jit_solution(9566962502019870208)
XLA Ops:
  0.0 2.2 %copy-done.2 = bf16[2048,1024]{1,0:T(8,128)(2,1)S(1)} copy-done((bf16[2048,1024]{1,0:T(8,128)(2,1)S(1)}, bf16[2048,1024]{1,0:T(8,128)(2,1)}, u32[]{:S(2)}) %copy-start.2) | copy-done | bytes 4194328
  2.2 1.4 copy-done.3
  3.6 5.0 %project.1 = (bf16[16,256,128]{2,1,0:T(8,128)(2,1)S(1)}, bf16[16,256,128]{2,1,0:T(8,128)(2,1)S(1)}, bf16[8,16,128]{2,1,0:T(8,128)(2,1)S(1)}, bf16[8,16,128]{2,1,...) custom-call(bf16[2048,1024]{1,0:T(8,128)(2,1)S(1)} %copy-done.2, ...), custom_call_target="tpu_custom_call" | custom-call | flops 3221225472 | bytes 16777216 | tf_op jit(solution)/shard_map/project/pallas_call | solution.py:117
  8.7 3.0 %collective-permute-start.3 = (bf16[8,16,128]{2,1,0:T(8,128)(2,1)S(1)}, bf16[8,16,128]{2,1,0:T(8,128)(2,1)S(1)}, u32[]{:S(2)}, u32[]{:S(2)}) collective-permute-start(bf16[8,16,128]{2,1,0:T(8,128)(2,1)S(1)} %get-tuple-element.88), channel_id=1, source_target_pairs={{0,4},{4,0},{8,12},{12,8},{16,20},{20,16},{24,28},{28,24},{1,5},{5... | collective-permute-start | bytes 98312 | tf_op jit(solution)/shard_map/ppermute | solution.py:272
  11.7 1.6 collective-permute-start.4
  13.3 3.0 %collective-permute-start.6 = (bf16[8,16,128]{2,1,0:T(8,128)(2,1)S(1)}, bf16[8,16,128]{2,1,0:T(8,128)(2,1)S(1)}, u32[]{:S(2)}, u32[]{:S(2)}) collective-permute-start(bf16[8,16,128]{2,1,0:T(8,128)(2,1)S(1)} %get-tuple-element.91), channel_id=1, source_target_pairs={{0,16},{4,20},{8,24},{12,28},{16,0},{20,4},{24,8},{28,12},{1,17},{... | collective-permute-start | bytes 98312 | tf_op jit(solution)/shard_map/ppermute | solution.py:272
  16.3 1.3 collective-permute-start.7
  17.6 3.6 %collective-permute-start.8 = (bf16[8,16,128]{2,1,0:T(8,128)(2,1)S(1)}, bf16[8,16,128]{2,1,0:T(8,128)(2,1)S(1)}, u32[]{:S(2)}, u32[]{:S(2)}) collective-permute-start(bf16[8,16,128]{2,1,0:T(8,128)(2,1)S(1)} %get-tuple-element.93), channel_id=1, source_target_pairs={{0,24},{4,28},{8,16},{12,20},{16,8},{20,12},{24,0},{28,4},{1,25},{... | collective-permute-start | bytes 98312 | tf_op jit(solution)/shard_map/ppermute | solution.py:272
  21.2 1.7 collective-permute-start.24
  22.9 1.9 collective-permute-start.26
  25.7 1.7 collective-permute-start.10
  28.1 3.4 %collective-permute-start.27 = (bf16[8,16,128]{2,1,0:T(8,128)(2,1)S(1)}, bf16[8,16,128]{2,1,0:T(8,128)(2,1)S(1)}, u32[]{:S(2)}, u32[]{:S(2)}) collective-permute-start(bf16[8,16,128]{2,1,0:T(8,128)(2,1)S(1)} %get-tuple-element.117), channel_id=1, source_target_pairs={{0,16},{4,20},{8,24},{12,28},{16,0},{20,4},{24,8},{28,12},{1,17},{... | collective-permute-start | bytes 98312 | tf_op jit(solution)/shard_map/ppermute | solution.py:272
  31.6 2.4 %collective-permute-start.29 = (bf16[8,16,128]{2,1,0:T(8,128)(2,1)S(1)}, bf16[8,16,128]{2,1,0:T(8,128)(2,1)S(1)}, u32[]{:S(2)}, u32[]{:S(2)}) collective-permute-start(bf16[8,16,128]{2,1,0:T(8,128)(2,1)S(1)} %get-tuple-element.119), channel_id=1, source_target_pairs={{0,24},{4,28},{8,16},{12,20},{16,8},{20,12},{24,0},{28,4},{1,25},{... | collective-permute-start | bytes 98312 | tf_op jit(solution)/shard_map/ppermute | solution.py:272
  33.9 2.4 %collective-permute-start.30 = (bf16[8,16,128]{2,1,0:T(8,128)(2,1)S(1)}, bf16[8,16,128]{2,1,0:T(8,128)(2,1)S(1)}, u32[]{:S(2)}, u32[]{:S(2)}) collective-permute-start(bf16[8,16,128]{2,1,0:T(8,128)(2,1)S(1)} %get-tuple-element.120), channel_id=1, source_target_pairs={{0,28},{4,24},{8,20},{12,16},{16,12},{20,8},{24,4},{28,0},{1,29},{... | collective-permute-start | bytes 98312 | tf_op jit(solution)/shard_map/ppermute | solution.py:272
  36.3 0.9 collective-permute-done.28.refs_5_
  38.5 2.1 %collective-permute-done.30.refs_7_ = bf16[8,16,128]{2,1,0:T(8,128)(2,1)S(1)} collective-permute-done((bf16[8,16,128]{2,1,0:T(8,128)(2,1)S(1)}, bf16[8,16,128]{2,1,0:T(8,128)(2,1)S(1)}, u32[]{:S(2)}, u32[]{:S(2)}) %collective-permute-start.30) | collective-permute-done | bytes 32800 | tf_op jit(solution)/shard_map/ppermute | solution.py:272
  42.1 2.1 %collective-permute-start.53 = (bf16[8,16,128]{2,1,0:T(8,128)(2,1)S(1)}, bf16[8,16,128]{2,1,0:T(8,128)(2,1)S(1)}, u32[]{:S(2)}, u32[]{:S(2)}) collective-permute-start(bf16[8,16,128]{2,1,0:T(8,128)(2,1)S(1)} %get-tuple-element.147), channel_id=1, source_target_pairs={{0,8},{4,12},{8,0},{12,4},{16,24},{20,28},{24,16},{28,20},{1,9},{5... | collective-permute-start | bytes 98312 | tf_op jit(solution)/shard_map/ppermute | solution.py:272
  44.1 1.8 collective-permute-done.40.refs_3_
  46.5 3.3 %collective-permute-start.13 = (bf16[32,16,128]{2,1,0:T(8,128)(2,1)S(1)}, bf16[32,16,128]{2,1,0:T(8,128)(2,1)S(1)}, u32[]{:S(2)}, u32[]{:S(2)}) collective-permute-start(bf16[32,16,128]{2,1,0:T(8,128)(2,1)S(1)} %get-tuple-element.99), channel_id=1, source_target_pairs={{0,16},{4,20},{8,24},{12,28},{16,0},{20,4},{24,8},{28,12},{1,17},{... | collective-permute-start | bytes 393224 | tf_op jit(solution)/shard_map/ppermute | solution.py:272
  50.3 2.2 %collective-permute-start.15 = (bf16[32,16,128]{2,1,0:T(8,128)(2,1)S(1)}, bf16[32,16,128]{2,1,0:T(8,128)(2,1)S(1)}, u32[]{:S(2)}, u32[]{:S(2)}) collective-permute-start(bf16[32,16,128]{2,1,0:T(8,128)(2,1)S(1)} %get-tuple-element.101), channel_id=1, source_target_pairs={{0,24},{4,28},{8,16},{12,20},{16,8},{20,12},{24,0},{28,4},{1,25},{... | collective-permute-start | bytes 393224 | tf_op jit(solution)/shard_map/ppermute | solution.py:272
  52.5 2.1 %collective-permute-start.16 = (bf16[32,16,128]{2,1,0:T(8,128)(2,1)S(1)}, bf16[32,16,128]{2,1,0:T(8,128)(2,1)S(1)}, u32[]{:S(2)}, u32[]{:S(2)}) collective-permute-start(bf16[32,16,128]{2,1,0:T(8,128)(2,1)S(1)} %get-tuple-element.102), channel_id=1, source_target_pairs={{0,28},{4,24},{8,20},{12,16},{16,12},{20,8},{24,4},{28,0},{1,29},{... | collective-permute-start | bytes 393224 | tf_op jit(solution)/shard_map/ppermute | solution.py:272
  55.3 5.7 %collective-permute-done.13.refs_12_ = bf16[32,16,128]{2,1,0:T(8,128)(2,1)S(1)} collective-permute-done((bf16[32,16,128]{2,1,0:T(8,128)(2,1)S(1)}, bf16[32,16,128]{2,1,0:T(8,128)(2,1)S(1)}, u32[]{:S(2)}, u32[]{:S(2)}) %collective-permute-start.13) | collective-permute-done | bytes 131104 | tf_op jit(solution)/shard_map/ppermute | solution.py:272
  61.0 3.2 %collective-permute-done.14.refs_13_ = bf16[32,16,128]{2,1,0:T(8,128)(2,1)S(1)} collective-permute-done((bf16[32,16,128]{2,1,0:T(8,128)(2,1)S(1)}, bf16[32,16,128]{2,1,0:T(8,128)(2,1)S(1)}, u32[]{:S(2)}, u32[]{:S(2)}) %collective-permute-start.14) | collective-permute-done | bytes 131104 | tf_op jit(solution)/shard_map/ppermute | solution.py:272
  64.3 2.4 %collective-permute-start.57 = (bf16[8,16,128]{2,1,0:T(8,128)(2,1)S(1)}, bf16[8,16,128]{2,1,0:T(8,128)(2,1)S(1)}, u32[]{:S(2)}, u32[]{:S(2)}) collective-permute-start(bf16[8,16,128]{2,1,0:T(8,128)(2,1)S(1)} %get-tuple-element.151), channel_id=1, source_target_pairs={{0,24},{4,28},{8,16},{12,20},{16,8},{20,12},{24,0},{28,4},{1,25},{... | collective-permute-start | bytes 98312 | tf_op jit(solution)/shard_map/ppermute | solution.py:272
  66.7 2.0 %collective-permute-start.58 = (bf16[8,16,128]{2,1,0:T(8,128)(2,1)S(1)}, bf16[8,16,128]{2,1,0:T(8,128)(2,1)S(1)}, u32[]{:S(2)}, u32[]{:S(2)}) collective-permute-start(bf16[8,16,128]{2,1,0:T(8,128)(2,1)S(1)} %get-tuple-element.152), channel_id=1, source_target_pairs={{0,28},{4,24},{8,20},{12,16},{16,12},{20,8},{24,4},{28,0},{1,29},{... | collective-permute-start | bytes 98312 | tf_op jit(solution)/shard_map/ppermute | solution.py:272
  68.7 3.9 %convolve.4 = (bf16[8,16,128]{2,1,0:T(8,128)(2,1)S(1)}, bf16[8,16,128]{2,1,0:T(8,128)(2,1)S(1)}, bf16[8,16,128]{2,1,0:T(8,128)(2,1)S(1)}, bf16[8,16,128]{2,1,0:T...) custom-call(bf16[8,16,128]{2,1,0:T(8,128)(2,1)S(1)} %get-tuple-eleme, ...), custom_call_target="tpu_custom_call" | custom-call | flops 1073741824 | bytes 786432 | tf_op jit(solution)/shard_map/convolve/pallas_call | solution.py:169
  72.6 4.5 %collective-permute-start.41 = (bf16[8,16,128]{2,1,0:T(8,128)(2,1)S(1)}, bf16[8,16,128]{2,1,0:T(8,128)(2,1)S(1)}, u32[]{:S(2)}, u32[]{:S(2)}) collective-permute-start(bf16[8,16,128]{2,1,0:T(8,128)(2,1)S(1)} %get-tuple-element.133), channel_id=1, source_target_pairs={{0,16},{4,20},{8,24},{12,28},{16,0},{20,4},{24,8},{28,12},{1,17},{... | collective-permute-start | bytes 98312 | tf_op jit(solution)/shard_map/ppermute | solution.py:272
  77.1 2.1 %collective-permute-start.43 = (bf16[8,16,128]{2,1,0:T(8,128)(2,1)S(1)}, bf16[8,16,128]{2,1,0:T(8,128)(2,1)S(1)}, u32[]{:S(2)}, u32[]{:S(2)}) collective-permute-start(bf16[8,16,128]{2,1,0:T(8,128)(2,1)S(1)} %get-tuple-element.135), channel_id=1, source_target_pairs={{0,24},{4,28},{8,16},{12,20},{16,8},{20,12},{24,0},{28,4},{1,25},{... | collective-permute-start | bytes 98312 | tf_op jit(solution)/shard_map/ppermute | solution.py:272
  79.2 2.7 %collective-permute-start.44 = (bf16[8,16,128]{2,1,0:T(8,128)(2,1)S(1)}, bf16[8,16,128]{2,1,0:T(8,128)(2,1)S(1)}, u32[]{:S(2)}, u32[]{:S(2)}) collective-permute-start(bf16[8,16,128]{2,1,0:T(8,128)(2,1)S(1)} %get-tuple-element.136), channel_id=1, source_target_pairs={{0,28},{4,24},{8,20},{12,16},{16,12},{20,8},{24,4},{28,0},{1,29},{... | collective-permute-start | bytes 98312 | tf_op jit(solution)/shard_map/ppermute | solution.py:272
  82.5 3.2 %convolve.7 = (bf16[8,16,128]{2,1,0:T(8,128)(2,1)S(1)}, bf16[8,16,128]{2,1,0:T(8,128)(2,1)S(1)}, bf16[8,16,128]{2,1,0:T(8,128)(2,1)S(1)}, bf16[8,16,128]{2,1,0:T...) custom-call(bf16[8,16,128]{2,1,0:T(8,128)(2,1)S(1)} %get-tuple-eleme, ...), custom_call_target="tpu_custom_call" | custom-call | flops 1073741824 | bytes 786432 | tf_op jit(solution)/shard_map/convolve/pallas_call | solution.py:169
  86.5 2.2 %collective-permute-start.19 = (bf16[8,16,128]{2,1,0:T(8,128)(2,1)S(1)}, bf16[8,16,128]{2,1,0:T(8,128)(2,1)S(1)}, u32[]{:S(2)}, u32[]{:S(2)}) collective-permute-start(bf16[8,16,128]{2,1,0:T(8,128)(2,1)S(1)} %get-tuple-element.106), channel_id=1, source_target_pairs={{0,12},{4,8},{8,4},{12,0},{16,28},{20,24},{24,20},{28,16},{1,13},{... | collective-permute-start | bytes 98312 | tf_op jit(solution)/shard_map/ppermute | solution.py:272
  88.7 1.1 collective-permute-start.20
  90.7 1.7 collective-permute-start.60
  92.5 1.4 collective-permute-start.61
  93.8 1.9 collective-permute-start.62
  96.6 2.2 %collective-permute-start.64 = (bf16[8,16,128]{2,1,0:T(8,128)(2,1)S(1)}, bf16[8,16,128]{2,1,0:T(8,128)(2,1)S(1)}, u32[]{:S(2)}, u32[]{:S(2)}) collective-permute-start(bf16[8,16,128]{2,1,0:T(8,128)(2,1)S(1)} %get-tuple-element.159), channel_id=1, source_target_pairs={{0,24},{4,28},{8,16},{12,20},{16,8},{20,12},{24,0},{28,4},{1,25},{... | collective-permute-start | bytes 98312 | tf_op jit(solution)/shard_map/ppermute | solution.py:272
  98.8 2.7 %collective-permute-start.65 = (bf16[8,16,128]{2,1,0:T(8,128)(2,1)S(1)}, bf16[8,16,128]{2,1,0:T(8,128)(2,1)S(1)}, u32[]{:S(2)}, u32[]{:S(2)}) collective-permute-start(bf16[8,16,128]{2,1,0:T(8,128)(2,1)S(1)} %get-tuple-element.160), channel_id=1, source_target_pairs={{0,28},{4,24},{8,20},{12,16},{16,12},{20,8},{24,4},{28,0},{1,29},{... | collective-permute-start | bytes 98312 | tf_op jit(solution)/shard_map/ppermute | solution.py:272
  101.5 3.8 %convolve.5 = (bf16[8,16,128]{2,1,0:T(8,128)(2,1)S(1)}, bf16[8,16,128]{2,1,0:T(8,128)(2,1)}, bf16[8,16,128]{2,1,0:T(8,128)(2,1)}, bf16[8,16,128]{2,1,0:T(8,128)(...) custom-call(bf16[8,16,128]{2,1,0:T(8,128)(2,1)S(1)} %get-tuple-eleme, ...), custom_call_target="tpu_custom_call" | custom-call | flops 1073741824 | bytes 786432 | tf_op jit(solution)/shard_map/convolve/pallas_call | solution.py:169
  108.5 2.1 %collective-permute-start.22 = (bf16[8,16,128]{2,1,0:T(8,128)(2,1)}, bf16[8,16,128]{2,1,0:T(8,128)(2,1)S(1)}, u32[]{:S(2)}, u32[]{:S(2)}) collective-permute-start(bf16[8,16,128]{2,1,0:T(8,128)(2,1)} %get-tuple-element.109), channel_id=1, source_target_pairs={{0,24},{4,28},{8,16},{12,20},{16,8},{20,12},{24,0},{28,4},{1,25},{... | collective-permute-start | bytes 98312 | tf_op jit(solution)/shard_map/ppermute | solution.py:272
  110.5 2.7 %collective-permute-start.23 = (bf16[8,16,128]{2,1,0:T(8,128)(2,1)}, bf16[8,16,128]{2,1,0:T(8,128)(2,1)S(1)}, u32[]{:S(2)}, u32[]{:S(2)}) collective-permute-start(bf16[8,16,128]{2,1,0:T(8,128)(2,1)} %get-tuple-element.110), channel_id=1, source_target_pairs={{0,28},{4,24},{8,20},{12,16},{16,12},{20,8},{24,4},{28,0},{1,29},{... | collective-permute-start | bytes 98312 | tf_op jit(solution)/shard_map/ppermute | solution.py:272
  115.0 2.3 %collective-permute-start.33 = (bf16[8,16,128]{2,1,0:T(8,128)(2,1)}, bf16[8,16,128]{2,1,0:T(8,128)(2,1)S(1)}, u32[]{:S(2)}, u32[]{:S(2)}) collective-permute-start(bf16[8,16,128]{2,1,0:T(8,128)(2,1)} %copy-done.36), channel_id=1, source_target_pairs={{0,12},{4,8},{8,4},{12,0},{16,28},{20,24},{24,20},{28,16},{1,13},{... | collective-permute-start | bytes 98312 | tf_op jit(solution)/shard_map/ppermute | solution.py:272
  117.3 1.0 collective-permute-start.34
  118.3 1.9 collective-permute-start.35
  120.2 1.5 collective-permute-start.73
  138.5 3.3 %convolve.6 = (bf16[8,16,128]{2,1,0:T(8,128)(2,1)S(1)}, bf16[8,16,128]{2,1,0:T(8,128)(2,1)S(1)}, bf16[8,16,128]{2,1,0:T(8,128)(2,1)S(1)}, bf16[8,16,128]{2,1,0:T...) custom-call(bf16[8,16,128]{2,1,0:T(8,128)(2,1)S(1)} %copy-done.50, ...), custom_call_target="tpu_custom_call" | custom-call | flops 1073741824 | bytes 786432 | tf_op jit(solution)/shard_map/convolve/pallas_call | solution.py:169
  141.9 2.1 %collective-permute-start.36 = (bf16[8,16,128]{2,1,0:T(8,128)(2,1)S(1)}, bf16[8,16,128]{2,1,0:T(8,128)(2,1)S(1)}, u32[]{:S(2)}, u32[]{:S(2)}) collective-permute-start(bf16[8,16,128]{2,1,0:T(8,128)(2,1)S(1)} %copy-done.33), channel_id=1, source_target_pairs={{0,24},{4,28},{8,16},{12,20},{16,8},{20,12},{24,0},{28,4},{1,25},{... | collective-permute-start | bytes 98312 | tf_op jit(solution)/shard_map/ppermute | solution.py:272
  144.0 2.7 %collective-permute-start.37 = (bf16[8,16,128]{2,1,0:T(8,128)(2,1)S(1)}, bf16[8,16,128]{2,1,0:T(8,128)(2,1)S(1)}, u32[]{:S(2)}, u32[]{:S(2)}) collective-permute-start(bf16[8,16,128]{2,1,0:T(8,128)(2,1)S(1)} %copy-done.31), channel_id=1, source_target_pairs={{0,28},{4,24},{8,20},{12,16},{16,12},{20,8},{24,4},{28,0},{1,29},{... | collective-permute-start | bytes 98312 | tf_op jit(solution)/shard_map/ppermute | solution.py:272
  147.7 3.3 %collective-permute-done.37.refs_7_ = bf16[8,16,128]{2,1,0:T(8,128)(2,1)S(1)} collective-permute-done((bf16[8,16,128]{2,1,0:T(8,128)(2,1)S(1)}, bf16[8,16,128]{2,1,0:T(8,128)(2,1)S(1)}, u32[]{:S(2)}, u32[]{:S(2)}) %collective-permute-start.37) | collective-permute-done | bytes 32800 | tf_op jit(solution)/shard_map/ppermute | solution.py:272
  151.0 3.0 %collective-permute-start.48 = (bf16[8,16,128]{2,1,0:T(8,128)(2,1)S(1)}, bf16[8,16,128]{2,1,0:T(8,128)(2,1)S(1)}, u32[]{:S(2)}, u32[]{:S(2)}) collective-permute-start(bf16[8,16,128]{2,1,0:T(8,128)(2,1)S(1)} %get-tuple-element.141), channel_id=1, source_target_pairs={{0,16},{4,20},{8,24},{12,28},{16,0},{20,4},{24,8},{28,12},{1,17},{... | collective-permute-start | bytes 98312 | tf_op jit(solution)/shard_map/ppermute | solution.py:272
  154.0 1.8 collective-permute-done.47.refs_3_
  155.8 1.5 collective-permute-start.50
  157.3 2.2 %collective-permute-start.51 = (bf16[8,16,128]{2,1,0:T(8,128)(2,1)S(1)}, bf16[8,16,128]{2,1,0:T(8,128)(2,1)S(1)}, u32[]{:S(2)}, u32[]{:S(2)}) collective-permute-start(bf16[8,16,128]{2,1,0:T(8,128)(2,1)S(1)} %get-tuple-element.144), channel_id=1, source_target_pairs={{0,28},{4,24},{8,20},{12,16},{16,12},{20,8},{24,4},{28,0},{1,29},{... | collective-permute-start | bytes 98312 | tf_op jit(solution)/shard_map/ppermute | solution.py:272
  159.8 1.7 collective-permute-done.50.refs_6_
  162.0 1.9 collective-permute-done.51.refs_7_
  165.4 1.0 collective-permute-done.1.refs_2_
  166.8 3.0 %collective-permute-done.2.refs_3_ = bf16[256,256]{1,0:T(8,128)(2,1)S(1)} collective-permute-done((bf16[256,256]{1,0:T(8,128)(2,1)S(1)}, bf16[256,256]{1,0:T(8,128)(2,1)S(1)}, u32[]{:S(2)}, u32[]{:S(2)}) %collective-permute-start.2) | collective-permute-done | bytes 131104 | tf_op jit(solution)/shard_map/ppermute | solution.py:272
  170.2 1.7 collective-permute-start.70
  171.9 2.5 %collective-permute-done.72.refs_14_ = bf16[16,64,128]{2,1,0:T(8,128)(2,1)S(1)} collective-permute-done((bf16[16,64,128]{2,1,0:T(8,128)(2,1)S(1)}, bf16[16,64,128]{2,1,0:T(8,128)(2,1)S(1)}, u32[]{:S(2)}, u32[]{:S(2)}) %collective-permute-start.72) | collective-permute-done | bytes 262176 | tf_op jit(solution)/shard_map/ppermute | solution.py:272
  174.4 1.1 collective-permute-start.66
  175.5 4.5 %collective-permute-done.71.refs_13_ = bf16[16,64,128]{2,1,0:T(8,128)(2,1)S(1)} collective-permute-done((bf16[16,64,128]{2,1,0:T(8,128)(2,1)S(1)}, bf16[16,64,128]{2,1,0:T(8,128)(2,1)S(1)}, u32[]{:S(2)}, u32[]{:S(2)}) %collective-permute-start.71) | collective-permute-done | bytes 262176 | tf_op jit(solution)/shard_map/ppermute | solution.py:272
  180.0 1.1 collective-permute-start.76
  181.1 4.5 %collective-permute-done.70.refs_12_ = bf16[16,64,128]{2,1,0:T(8,128)(2,1)S(1)} collective-permute-done((bf16[16,64,128]{2,1,0:T(8,128)(2,1)S(1)}, bf16[16,64,128]{2,1,0:T(8,128)(2,1)S(1)}, u32[]{:S(2)}, u32[]{:S(2)}) %collective-permute-start.70) | collective-permute-done | bytes 262176 | tf_op jit(solution)/shard_map/ppermute | solution.py:272
  186.0 1.2 collective-permute-done.74.refs_16_
  187.2 3.0 %mix.1 = bf16[2048,256]{1,0:T(8,128)(2,1)} custom-call(bf16[256,256]{1,0:T(8,128)(2,1)S(1)} %get-tuple-element.83.refs_0_, bf16[256,256]{1,0:T(8,128)(2,1)S(1)} %collective-permute-done.refs_1_, bf16[256,256]{1,0:T(8,128)(2,1)S(1)} %collective-permute-done.1.refs_2_, bf16[256,256]{1,0:T(8,128)(2,1)S(1)} %collective-permute-done.2.refs_3_, ...), custom_call_target="tpu_custom_call" | custom-call | flops 1073741824 | bytes 6291456 | tf_op jit(solution)/shard_map/mix/pallas_call | solution.py:257
  (209 shorter events, 35.8 us)
Async XLA Ops:
  8.7 8.9 %collective-permute-start.3 = (bf16[8,16,128]{2,1,0:T(8,128)(2,1)S(1)}, bf16[8,16,128]{2,1,0:T(8,128)(2,1)S(1)}, u32[]{:S(2)}, u32[]{:S(2)}) collective-permute-start(bf16[8,16,128]{2,1,0:T(8,128)(2,1)S(1)} %get-tuple-element.88), channel_id=1, source_target_pairs={{0,4},{4,0},{8,12},{12,8},{16,20},{20,16},{24,28},{28,24},{1,5},{5... | collective-permute-start | bytes 98312 | tf_op jit(solution)/shard_map/ppermute | solution.py:272
  11.7 9.5 %collective-permute-start.4 = (bf16[8,16,128]{2,1,0:T(8,128)(2,1)S(1)}, bf16[8,16,128]{2,1,0:T(8,128)(2,1)S(1)}, u32[]{:S(2)}, u32[]{:S(2)}) collective-permute-start(bf16[8,16,128]{2,1,0:T(8,128)(2,1)S(1)} %get-tuple-element.89), channel_id=1, source_target_pairs={{0,8},{4,12},{8,0},{12,4},{16,24},{20,28},{24,16},{28,20},{1,9},{5... | collective-permute-start | bytes 98312 | tf_op jit(solution)/shard_map/ppermute | solution.py:272
  13.3 7.9 %collective-permute-start.5 = (bf16[8,16,128]{2,1,0:T(8,128)(2,1)S(1)}, bf16[8,16,128]{2,1,0:T(8,128)(2,1)S(1)}, u32[]{:S(2)}, u32[]{:S(2)}) collective-permute-start(bf16[8,16,128]{2,1,0:T(8,128)(2,1)S(1)} %get-tuple-element.90), channel_id=1, source_target_pairs={{0,12},{4,8},{8,4},{12,0},{16,28},{20,24},{24,20},{28,16},{1,13},{... | collective-permute-start | bytes 98312 | tf_op jit(solution)/shard_map/ppermute | solution.py:272
  13.3 9.6 %collective-permute-start.6 = (bf16[8,16,128]{2,1,0:T(8,128)(2,1)S(1)}, bf16[8,16,128]{2,1,0:T(8,128)(2,1)S(1)}, u32[]{:S(2)}, u32[]{:S(2)}) collective-permute-start(bf16[8,16,128]{2,1,0:T(8,128)(2,1)S(1)} %get-tuple-element.91), channel_id=1, source_target_pairs={{0,16},{4,20},{8,24},{12,28},{16,0},{20,4},{24,8},{28,12},{1,17},{... | collective-permute-start | bytes 98312 | tf_op jit(solution)/shard_map/ppermute | solution.py:272
  16.3 6.6 %collective-permute-start.7 = (bf16[8,16,128]{2,1,0:T(8,128)(2,1)S(1)}, bf16[8,16,128]{2,1,0:T(8,128)(2,1)S(1)}, u32[]{:S(2)}, u32[]{:S(2)}) collective-permute-start(bf16[8,16,128]{2,1,0:T(8,128)(2,1)S(1)} %get-tuple-element.92), channel_id=1, source_target_pairs={{0,20},{4,16},{8,28},{12,24},{16,4},{20,0},{24,12},{28,8},{1,21},{... | collective-permute-start | bytes 98312 | tf_op jit(solution)/shard_map/ppermute | solution.py:272
  17.6 8.1 %collective-permute-start.8 = (bf16[8,16,128]{2,1,0:T(8,128)(2,1)S(1)}, bf16[8,16,128]{2,1,0:T(8,128)(2,1)S(1)}, u32[]{:S(2)}, u32[]{:S(2)}) collective-permute-start(bf16[8,16,128]{2,1,0:T(8,128)(2,1)S(1)} %get-tuple-element.93), channel_id=1, source_target_pairs={{0,24},{4,28},{8,16},{12,20},{16,8},{20,12},{24,0},{28,4},{1,25},{... | collective-permute-start | bytes 98312 | tf_op jit(solution)/shard_map/ppermute | solution.py:272
  21.2 6.9 %collective-permute-start.9 = (bf16[8,16,128]{2,1,0:T(8,128)(2,1)S(1)}, bf16[8,16,128]{2,1,0:T(8,128)(2,1)S(1)}, u32[]{:S(2)}, u32[]{:S(2)}) collective-permute-start(bf16[8,16,128]{2,1,0:T(8,128)(2,1)S(1)} %get-tuple-element.94), channel_id=1, source_target_pairs={{0,28},{4,24},{8,20},{12,16},{16,12},{20,8},{24,4},{28,0},{1,29},{... | collective-permute-start | bytes 98312 | tf_op jit(solution)/shard_map/ppermute | solution.py:272
  21.2 6.9 %collective-permute-start.24 = (bf16[8,16,128]{2,1,0:T(8,128)(2,1)S(1)}, bf16[8,16,128]{2,1,0:T(8,128)(2,1)S(1)}, u32[]{:S(2)}, u32[]{:S(2)}) collective-permute-start(bf16[8,16,128]{2,1,0:T(8,128)(2,1)S(1)} %get-tuple-element.114), channel_id=1, source_target_pairs={{0,4},{4,0},{8,12},{12,8},{16,20},{20,16},{24,28},{28,24},{1,5},{5... | collective-permute-start | bytes 98312 | tf_op jit(solution)/shard_map/ppermute | solution.py:272
  22.9 8.7 %collective-permute-start.25 = (bf16[8,16,128]{2,1,0:T(8,128)(2,1)S(1)}, bf16[8,16,128]{2,1,0:T(8,128)(2,1)S(1)}, u32[]{:S(2)}, u32[]{:S(2)}) collective-permute-start(bf16[8,16,128]{2,1,0:T(8,128)(2,1)S(1)} %get-tuple-element.115), channel_id=1, source_target_pairs={{0,8},{4,12},{8,0},{12,4},{16,24},{20,28},{24,16},{28,20},{1,9},{5... | collective-permute-start | bytes 98312 | tf_op jit(solution)/shard_map/ppermute | solution.py:272
  22.9 8.7 %collective-permute-start.26 = (bf16[8,16,128]{2,1,0:T(8,128)(2,1)S(1)}, bf16[8,16,128]{2,1,0:T(8,128)(2,1)S(1)}, u32[]{:S(2)}, u32[]{:S(2)}) collective-permute-start(bf16[8,16,128]{2,1,0:T(8,128)(2,1)S(1)} %get-tuple-element.116), channel_id=1, source_target_pairs={{0,12},{4,8},{8,4},{12,0},{16,28},{20,24},{24,20},{28,16},{1,13},{... | collective-permute-start | bytes 98312 | tf_op jit(solution)/shard_map/ppermute | solution.py:272
  25.7 24.6 %collective-permute-start.10 = (bf16[32,16,128]{2,1,0:T(8,128)(2,1)S(1)}, bf16[32,16,128]{2,1,0:T(8,128)(2,1)S(1)}, u32[]{:S(2)}, u32[]{:S(2)}) collective-permute-start(bf16[32,16,128]{2,1,0:T(8,128)(2,1)S(1)} %get-tuple-element.96), channel_id=1, source_target_pairs={{0,4},{4,0},{8,12},{12,8},{16,20},{20,16},{24,28},{28,24},{1,5},{5... | collective-permute-start | bytes 393224 | tf_op jit(solution)/shard_map/ppermute | solution.py:272
  28.1 24.4 %collective-permute-start.11 = (bf16[32,16,128]{2,1,0:T(8,128)(2,1)S(1)}, bf16[32,16,128]{2,1,0:T(8,128)(2,1)S(1)}, u32[]{:S(2)}, u32[]{:S(2)}) collective-permute-start(bf16[32,16,128]{2,1,0:T(8,128)(2,1)S(1)} %get-tuple-element.97), channel_id=1, source_target_pairs={{0,8},{4,12},{8,0},{12,4},{16,24},{20,28},{24,16},{28,20},{1,9},{5... | collective-permute-start | bytes 393224 | tf_op jit(solution)/shard_map/ppermute | solution.py:272
  28.1 5.8 %collective-permute-start.27 = (bf16[8,16,128]{2,1,0:T(8,128)(2,1)S(1)}, bf16[8,16,128]{2,1,0:T(8,128)(2,1)S(1)}, u32[]{:S(2)}, u32[]{:S(2)}) collective-permute-start(bf16[8,16,128]{2,1,0:T(8,128)(2,1)S(1)} %get-tuple-element.117), channel_id=1, source_target_pairs={{0,16},{4,20},{8,24},{12,28},{16,0},{20,4},{24,8},{28,12},{1,17},{... | collective-permute-start | bytes 98312 | tf_op jit(solution)/shard_map/ppermute | solution.py:272
  31.6 6.2 %collective-permute-start.29 = (bf16[8,16,128]{2,1,0:T(8,128)(2,1)S(1)}, bf16[8,16,128]{2,1,0:T(8,128)(2,1)S(1)}, u32[]{:S(2)}, u32[]{:S(2)}) collective-permute-start(bf16[8,16,128]{2,1,0:T(8,128)(2,1)S(1)} %get-tuple-element.119), channel_id=1, source_target_pairs={{0,24},{4,28},{8,16},{12,20},{16,8},{20,12},{24,0},{28,4},{1,25},{... | collective-permute-start | bytes 98312 | tf_op jit(solution)/shard_map/ppermute | solution.py:272
  33.9 6.7 %collective-permute-start.30 = (bf16[8,16,128]{2,1,0:T(8,128)(2,1)S(1)}, bf16[8,16,128]{2,1,0:T(8,128)(2,1)S(1)}, u32[]{:S(2)}, u32[]{:S(2)}) collective-permute-start(bf16[8,16,128]{2,1,0:T(8,128)(2,1)S(1)} %get-tuple-element.120), channel_id=1, source_target_pairs={{0,28},{4,24},{8,20},{12,16},{16,12},{20,8},{24,4},{28,0},{1,29},{... | collective-permute-start | bytes 98312 | tf_op jit(solution)/shard_map/ppermute | solution.py:272
  42.1 7.7 %collective-permute-start.53 = (bf16[8,16,128]{2,1,0:T(8,128)(2,1)S(1)}, bf16[8,16,128]{2,1,0:T(8,128)(2,1)S(1)}, u32[]{:S(2)}, u32[]{:S(2)}) collective-permute-start(bf16[8,16,128]{2,1,0:T(8,128)(2,1)S(1)} %get-tuple-element.147), channel_id=1, source_target_pairs={{0,8},{4,12},{8,0},{12,4},{16,24},{20,28},{24,16},{28,20},{1,9},{5... | collective-permute-start | bytes 98312 | tf_op jit(solution)/shard_map/ppermute | solution.py:272
  46.5 8.5 %collective-permute-start.12 = (bf16[32,16,128]{2,1,0:T(8,128)(2,1)S(1)}, bf16[32,16,128]{2,1,0:T(8,128)(2,1)S(1)}, u32[]{:S(2)}, u32[]{:S(2)}) collective-permute-start(bf16[32,16,128]{2,1,0:T(8,128)(2,1)S(1)} %get-tuple-element.98), channel_id=1, source_target_pairs={{0,12},{4,8},{8,4},{12,0},{16,28},{20,24},{24,20},{28,16},{1,13},{... | collective-permute-start | bytes 393224 | tf_op jit(solution)/shard_map/ppermute | solution.py:272
  46.5 14.5 %collective-permute-start.13 = (bf16[32,16,128]{2,1,0:T(8,128)(2,1)S(1)}, bf16[32,16,128]{2,1,0:T(8,128)(2,1)S(1)}, u32[]{:S(2)}, u32[]{:S(2)}) collective-permute-start(bf16[32,16,128]{2,1,0:T(8,128)(2,1)S(1)} %get-tuple-element.99), channel_id=1, source_target_pairs={{0,16},{4,20},{8,24},{12,28},{16,0},{20,4},{24,8},{28,12},{1,17},{... | collective-permute-start | bytes 393224 | tf_op jit(solution)/shard_map/ppermute | solution.py:272
  49.8 14.4 %collective-permute-start.14 = (bf16[32,16,128]{2,1,0:T(8,128)(2,1)S(1)}, bf16[32,16,128]{2,1,0:T(8,128)(2,1)S(1)}, u32[]{:S(2)}, u32[]{:S(2)}) collective-permute-start(bf16[32,16,128]{2,1,0:T(8,128)(2,1)S(1)} %get-tuple-element.100), channel_id=1, source_target_pairs={{0,20},{4,16},{8,28},{12,24},{16,4},{20,0},{24,12},{28,8},{1,21},{... | collective-permute-start | bytes 393224 | tf_op jit(solution)/shard_map/ppermute | solution.py:272
  50.3 14.0 %collective-permute-start.15 = (bf16[32,16,128]{2,1,0:T(8,128)(2,1)S(1)}, bf16[32,16,128]{2,1,0:T(8,128)(2,1)S(1)}, u32[]{:S(2)}, u32[]{:S(2)}) collective-permute-start(bf16[32,16,128]{2,1,0:T(8,128)(2,1)S(1)} %get-tuple-element.101), channel_id=1, source_target_pairs={{0,24},{4,28},{8,16},{12,20},{16,8},{20,12},{24,0},{28,4},{1,25},{... | collective-permute-start | bytes 393224 | tf_op jit(solution)/shard_map/ppermute | solution.py:272
  52.5 14.2 %collective-permute-start.16 = (bf16[32,16,128]{2,1,0:T(8,128)(2,1)S(1)}, bf16[32,16,128]{2,1,0:T(8,128)(2,1)S(1)}, u32[]{:S(2)}, u32[]{:S(2)}) collective-permute-start(bf16[32,16,128]{2,1,0:T(8,128)(2,1)S(1)} %get-tuple-element.102), channel_id=1, source_target_pairs={{0,28},{4,24},{8,20},{12,16},{16,12},{20,8},{24,4},{28,0},{1,29},{... | collective-permute-start | bytes 393224 | tf_op jit(solution)/shard_map/ppermute | solution.py:272
  55.1 17.5 %collective-permute-start.54 = (bf16[8,16,128]{2,1,0:T(8,128)(2,1)S(1)}, bf16[8,16,128]{2,1,0:T(8,128)(2,1)S(1)}, u32[]{:S(2)}, u32[]{:S(2)}) collective-permute-start(bf16[8,16,128]{2,1,0:T(8,128)(2,1)S(1)} %get-tuple-element.148), channel_id=1, source_target_pairs={{0,12},{4,8},{8,4},{12,0},{16,28},{20,24},{24,20},{28,16},{1,13},{... | collective-permute-start | bytes 98312 | tf_op jit(solution)/shard_map/ppermute | solution.py:272
  61.0 16.1 %collective-permute-start.55 = (bf16[8,16,128]{2,1,0:T(8,128)(2,1)S(1)}, bf16[8,16,128]{2,1,0:T(8,128)(2,1)S(1)}, u32[]{:S(2)}, u32[]{:S(2)}) collective-permute-start(bf16[8,16,128]{2,1,0:T(8,128)(2,1)S(1)} %get-tuple-element.149), channel_id=1, source_target_pairs={{0,16},{4,20},{8,24},{12,28},{16,0},{20,4},{24,8},{28,12},{1,17},{... | collective-permute-start | bytes 98312 | tf_op jit(solution)/shard_map/ppermute | solution.py:272
  64.2 12.9 %collective-permute-start.56 = (bf16[8,16,128]{2,1,0:T(8,128)(2,1)S(1)}, bf16[8,16,128]{2,1,0:T(8,128)(2,1)S(1)}, u32[]{:S(2)}, u32[]{:S(2)}) collective-permute-start(bf16[8,16,128]{2,1,0:T(8,128)(2,1)S(1)} %get-tuple-element.150), channel_id=1, source_target_pairs={{0,20},{4,16},{8,28},{12,24},{16,4},{20,0},{24,12},{28,8},{1,21},{... | collective-permute-start | bytes 98312 | tf_op jit(solution)/shard_map/ppermute | solution.py:272
  64.3 14.9 %collective-permute-start.57 = (bf16[8,16,128]{2,1,0:T(8,128)(2,1)S(1)}, bf16[8,16,128]{2,1,0:T(8,128)(2,1)S(1)}, u32[]{:S(2)}, u32[]{:S(2)}) collective-permute-start(bf16[8,16,128]{2,1,0:T(8,128)(2,1)S(1)} %get-tuple-element.151), channel_id=1, source_target_pairs={{0,24},{4,28},{8,16},{12,20},{16,8},{20,12},{24,0},{28,4},{1,25},{... | collective-permute-start | bytes 98312 | tf_op jit(solution)/shard_map/ppermute | solution.py:272
  66.7 15.2 %collective-permute-start.58 = (bf16[8,16,128]{2,1,0:T(8,128)(2,1)S(1)}, bf16[8,16,128]{2,1,0:T(8,128)(2,1)S(1)}, u32[]{:S(2)}, u32[]{:S(2)}) collective-permute-start(bf16[8,16,128]{2,1,0:T(8,128)(2,1)S(1)} %get-tuple-element.152), channel_id=1, source_target_pairs={{0,28},{4,24},{8,20},{12,16},{16,12},{20,8},{24,4},{28,0},{1,29},{... | collective-permute-start | bytes 98312 | tf_op jit(solution)/shard_map/ppermute | solution.py:272
  72.6 13.1 %collective-permute-start.41 = (bf16[8,16,128]{2,1,0:T(8,128)(2,1)S(1)}, bf16[8,16,128]{2,1,0:T(8,128)(2,1)S(1)}, u32[]{:S(2)}, u32[]{:S(2)}) collective-permute-start(bf16[8,16,128]{2,1,0:T(8,128)(2,1)S(1)} %get-tuple-element.133), channel_id=1, source_target_pairs={{0,16},{4,20},{8,24},{12,28},{16,0},{20,4},{24,8},{28,12},{1,17},{... | collective-permute-start | bytes 98312 | tf_op jit(solution)/shard_map/ppermute | solution.py:272
  77.1 9.4 %collective-permute-start.42 = (bf16[8,16,128]{2,1,0:T(8,128)(2,1)S(1)}, bf16[8,16,128]{2,1,0:T(8,128)(2,1)S(1)}, u32[]{:S(2)}, u32[]{:S(2)}) collective-permute-start(bf16[8,16,128]{2,1,0:T(8,128)(2,1)S(1)} %get-tuple-element.134), channel_id=1, source_target_pairs={{0,20},{4,16},{8,28},{12,24},{16,4},{20,0},{24,12},{28,8},{1,21},{... | collective-permute-start | bytes 98312 | tf_op jit(solution)/shard_map/ppermute | solution.py:272
  77.1 11.6 %collective-permute-start.43 = (bf16[8,16,128]{2,1,0:T(8,128)(2,1)S(1)}, bf16[8,16,128]{2,1,0:T(8,128)(2,1)S(1)}, u32[]{:S(2)}, u32[]{:S(2)}) collective-permute-start(bf16[8,16,128]{2,1,0:T(8,128)(2,1)S(1)} %get-tuple-element.135), channel_id=1, source_target_pairs={{0,24},{4,28},{8,16},{12,20},{16,8},{20,12},{24,0},{28,4},{1,25},{... | collective-permute-start | bytes 98312 | tf_op jit(solution)/shard_map/ppermute | solution.py:272
  79.2 10.5 %collective-permute-start.44 = (bf16[8,16,128]{2,1,0:T(8,128)(2,1)S(1)}, bf16[8,16,128]{2,1,0:T(8,128)(2,1)S(1)}, u32[]{:S(2)}, u32[]{:S(2)}) collective-permute-start(bf16[8,16,128]{2,1,0:T(8,128)(2,1)S(1)} %get-tuple-element.136), channel_id=1, source_target_pairs={{0,28},{4,24},{8,20},{12,16},{16,12},{20,8},{24,4},{28,0},{1,29},{... | collective-permute-start | bytes 98312 | tf_op jit(solution)/shard_map/ppermute | solution.py:272
  81.9 8.8 %collective-permute-start.17 = (bf16[8,16,128]{2,1,0:T(8,128)(2,1)S(1)}, bf16[8,16,128]{2,1,0:T(8,128)(2,1)S(1)}, u32[]{:S(2)}, u32[]{:S(2)}) collective-permute-start(bf16[8,16,128]{2,1,0:T(8,128)(2,1)S(1)} %get-tuple-element.104), channel_id=1, source_target_pairs={{0,4},{4,0},{8,12},{12,8},{16,20},{20,16},{24,28},{28,24},{1,5},{5... | collective-permute-start | bytes 98312 | tf_op jit(solution)/shard_map/ppermute | solution.py:272
  85.7 6.8 %collective-permute-start.18 = (bf16[8,16,128]{2,1,0:T(8,128)(2,1)S(1)}, bf16[8,16,128]{2,1,0:T(8,128)(2,1)S(1)}, u32[]{:S(2)}, u32[]{:S(2)}) collective-permute-start(bf16[8,16,128]{2,1,0:T(8,128)(2,1)S(1)} %get-tuple-element.105), channel_id=1, source_target_pairs={{0,8},{4,12},{8,0},{12,4},{16,24},{20,28},{24,16},{28,20},{1,9},{5... | collective-permute-start | bytes 98312 | tf_op jit(solution)/shard_map/ppermute | solution.py:272
  86.5 7.4 %collective-permute-start.19 = (bf16[8,16,128]{2,1,0:T(8,128)(2,1)S(1)}, bf16[8,16,128]{2,1,0:T(8,128)(2,1)S(1)}, u32[]{:S(2)}, u32[]{:S(2)}) collective-permute-start(bf16[8,16,128]{2,1,0:T(8,128)(2,1)S(1)} %get-tuple-element.106), channel_id=1, source_target_pairs={{0,12},{4,8},{8,4},{12,0},{16,28},{20,24},{24,20},{28,16},{1,13},{... | collective-permute-start | bytes 98312 | tf_op jit(solution)/shard_map/ppermute | solution.py:272
  88.7 7.0 %collective-permute-start.20 = (bf16[8,16,128]{2,1,0:T(8,128)(2,1)S(1)}, bf16[8,16,128]{2,1,0:T(8,128)(2,1)S(1)}, u32[]{:S(2)}, u32[]{:S(2)}) collective-permute-start(bf16[8,16,128]{2,1,0:T(8,128)(2,1)S(1)} %get-tuple-element.107), channel_id=1, source_target_pairs={{0,16},{4,20},{8,24},{12,28},{16,0},{20,4},{24,8},{28,12},{1,17},{... | collective-permute-start | bytes 98312 | tf_op jit(solution)/shard_map/ppermute | solution.py:272
  90.3 6.3 %collective-permute-start.59 = (bf16[8,16,128]{2,1,0:T(8,128)(2,1)S(1)}, bf16[8,16,128]{2,1,0:T(8,128)(2,1)S(1)}, u32[]{:S(2)}, u32[]{:S(2)}) collective-permute-start(bf16[8,16,128]{2,1,0:T(8,128)(2,1)S(1)} %get-tuple-element.154), channel_id=1, source_target_pairs={{0,4},{4,0},{8,12},{12,8},{16,20},{20,16},{24,28},{28,24},{1,5},{5... | collective-permute-start | bytes 98312 | tf_op jit(solution)/shard_map/ppermute | solution.py:272
  90.7 8.1 %collective-permute-start.60 = (bf16[8,16,128]{2,1,0:T(8,128)(2,1)S(1)}, bf16[8,16,128]{2,1,0:T(8,128)(2,1)S(1)}, u32[]{:S(2)}, u32[]{:S(2)}) collective-permute-start(bf16[8,16,128]{2,1,0:T(8,128)(2,1)S(1)} %get-tuple-element.155), channel_id=1, source_target_pairs={{0,8},{4,12},{8,0},{12,4},{16,24},{20,28},{24,16},{28,20},{1,9},{5... | collective-permute-start | bytes 98312 | tf_op jit(solution)/shard_map/ppermute | solution.py:272
  92.5 15.9 %collective-permute-start.61 = (bf16[8,16,128]{2,1,0:T(8,128)(2,1)S(1)}, bf16[8,16,128]{2,1,0:T(8,128)(2,1)S(1)}, u32[]{:S(2)}, u32[]{:S(2)}) collective-permute-start(bf16[8,16,128]{2,1,0:T(8,128)(2,1)S(1)} %get-tuple-element.156), channel_id=1, source_target_pairs={{0,12},{4,8},{8,4},{12,0},{16,28},{20,24},{24,20},{28,16},{1,13},{... | collective-permute-start | bytes 98312 | tf_op jit(solution)/shard_map/ppermute | solution.py:272
  93.8 14.6 %collective-permute-start.62 = (bf16[8,16,128]{2,1,0:T(8,128)(2,1)S(1)}, bf16[8,16,128]{2,1,0:T(8,128)(2,1)S(1)}, u32[]{:S(2)}, u32[]{:S(2)}) collective-permute-start(bf16[8,16,128]{2,1,0:T(8,128)(2,1)S(1)} %get-tuple-element.157), channel_id=1, source_target_pairs={{0,16},{4,20},{8,24},{12,28},{16,0},{20,4},{24,8},{28,12},{1,17},{... | collective-permute-start | bytes 98312 | tf_op jit(solution)/shard_map/ppermute | solution.py:272
  95.7 14.8 %collective-permute-start.63 = (bf16[8,16,128]{2,1,0:T(8,128)(2,1)S(1)}, bf16[8,16,128]{2,1,0:T(8,128)(2,1)S(1)}, u32[]{:S(2)}, u32[]{:S(2)}) collective-permute-start(bf16[8,16,128]{2,1,0:T(8,128)(2,1)S(1)} %get-tuple-element.158), channel_id=1, source_target_pairs={{0,20},{4,16},{8,28},{12,24},{16,4},{20,0},{24,12},{28,8},{1,21},{... | collective-permute-start | bytes 98312 | tf_op jit(solution)/shard_map/ppermute | solution.py:272
  96.6 16.6 %collective-permute-start.64 = (bf16[8,16,128]{2,1,0:T(8,128)(2,1)S(1)}, bf16[8,16,128]{2,1,0:T(8,128)(2,1)S(1)}, u32[]{:S(2)}, u32[]{:S(2)}) collective-permute-start(bf16[8,16,128]{2,1,0:T(8,128)(2,1)S(1)} %get-tuple-element.159), channel_id=1, source_target_pairs={{0,24},{4,28},{8,16},{12,20},{16,8},{20,12},{24,0},{28,4},{1,25},{... | collective-permute-start | bytes 98312 | tf_op jit(solution)/shard_map/ppermute | solution.py:272
  98.8 15.0 %collective-permute-start.65 = (bf16[8,16,128]{2,1,0:T(8,128)(2,1)S(1)}, bf16[8,16,128]{2,1,0:T(8,128)(2,1)S(1)}, u32[]{:S(2)}, u32[]{:S(2)}) collective-permute-start(bf16[8,16,128]{2,1,0:T(8,128)(2,1)S(1)} %get-tuple-element.160), channel_id=1, source_target_pairs={{0,28},{4,24},{8,20},{12,16},{16,12},{20,8},{24,4},{28,0},{1,29},{... | collective-permute-start | bytes 98312 | tf_op jit(solution)/shard_map/ppermute | solution.py:272
  108.4 6.6 %collective-permute-start.21 = (bf16[8,16,128]{2,1,0:T(8,128)(2,1)}, bf16[8,16,128]{2,1,0:T(8,128)(2,1)S(1)}, u32[]{:S(2)}, u32[]{:S(2)}) collective-permute-start(bf16[8,16,128]{2,1,0:T(8,128)(2,1)} %get-tuple-element.108), channel_id=1, source_target_pairs={{0,20},{4,16},{8,28},{12,24},{16,4},{20,0},{24,12},{28,8},{1,21},{... | collective-permute-start | bytes 98312 | tf_op jit(solution)/shard_map/ppermute | solution.py:272
  108.5 8.8 %collective-permute-start.22 = (bf16[8,16,128]{2,1,0:T(8,128)(2,1)}, bf16[8,16,128]{2,1,0:T(8,128)(2,1)S(1)}, u32[]{:S(2)}, u32[]{:S(2)}) collective-permute-start(bf16[8,16,128]{2,1,0:T(8,128)(2,1)} %get-tuple-element.109), channel_id=1, source_target_pairs={{0,24},{4,28},{8,16},{12,20},{16,8},{20,12},{24,0},{28,4},{1,25},{... | collective-permute-start | bytes 98312 | tf_op jit(solution)/shard_map/ppermute | solution.py:272
  110.5 7.8 %collective-permute-start.23 = (bf16[8,16,128]{2,1,0:T(8,128)(2,1)}, bf16[8,16,128]{2,1,0:T(8,128)(2,1)S(1)}, u32[]{:S(2)}, u32[]{:S(2)}) collective-permute-start(bf16[8,16,128]{2,1,0:T(8,128)(2,1)} %get-tuple-element.110), channel_id=1, source_target_pairs={{0,28},{4,24},{8,20},{12,16},{16,12},{20,8},{24,4},{28,0},{1,29},{... | collective-permute-start | bytes 98312 | tf_op jit(solution)/shard_map/ppermute | solution.py:272
  113.2 7.0 %collective-permute-start.31 = (bf16[8,16,128]{2,1,0:T(8,128)(2,1)}, bf16[8,16,128]{2,1,0:T(8,128)(2,1)S(1)}, u32[]{:S(2)}, u32[]{:S(2)}) collective-permute-start(bf16[8,16,128]{2,1,0:T(8,128)(2,1)} %get-tuple-element.122), channel_id=1, source_target_pairs={{0,4},{4,0},{8,12},{12,8},{16,20},{20,16},{24,28},{28,24},{1,5},{5... | collective-permute-start | bytes 98312 | tf_op jit(solution)/shard_map/ppermute | solution.py:272
  113.8 7.9 %collective-permute-start.32 = (bf16[8,16,128]{2,1,0:T(8,128)(2,1)}, bf16[8,16,128]{2,1,0:T(8,128)(2,1)S(1)}, u32[]{:S(2)}, u32[]{:S(2)}) collective-permute-start(bf16[8,16,128]{2,1,0:T(8,128)(2,1)} %get-tuple-element.123), channel_id=1, source_target_pairs={{0,8},{4,12},{8,0},{12,4},{16,24},{20,28},{24,16},{28,20},{1,9},{5... | collective-permute-start | bytes 98312 | tf_op jit(solution)/shard_map/ppermute | solution.py:272
  115.0 26.9 %collective-permute-start.33 = (bf16[8,16,128]{2,1,0:T(8,128)(2,1)}, bf16[8,16,128]{2,1,0:T(8,128)(2,1)S(1)}, u32[]{:S(2)}, u32[]{:S(2)}) collective-permute-start(bf16[8,16,128]{2,1,0:T(8,128)(2,1)} %copy-done.36), channel_id=1, source_target_pairs={{0,12},{4,8},{8,4},{12,0},{16,28},{20,24},{24,20},{28,16},{1,13},{... | collective-permute-start | bytes 98312 | tf_op jit(solution)/shard_map/ppermute | solution.py:272
  117.3 26.7 %collective-permute-start.34 = (bf16[8,16,128]{2,1,0:T(8,128)(2,1)}, bf16[8,16,128]{2,1,0:T(8,128)(2,1)S(1)}, u32[]{:S(2)}, u32[]{:S(2)}) collective-permute-start(bf16[8,16,128]{2,1,0:T(8,128)(2,1)} %copy-done.35), channel_id=1, source_target_pairs={{0,16},{4,20},{8,24},{12,28},{16,0},{20,4},{24,8},{28,12},{1,17},{... | collective-permute-start | bytes 98312 | tf_op jit(solution)/shard_map/ppermute | solution.py:272
  118.3 28.4 %collective-permute-start.35 = (bf16[8,16,128]{2,1,0:T(8,128)(2,1)}, bf16[8,16,128]{2,1,0:T(8,128)(2,1)S(1)}, u32[]{:S(2)}, u32[]{:S(2)}) collective-permute-start(bf16[8,16,128]{2,1,0:T(8,128)(2,1)} %copy-done.34), channel_id=1, source_target_pairs={{0,20},{4,16},{8,28},{12,24},{16,4},{20,0},{24,12},{28,8},{1,21},{... | collective-permute-start | bytes 98312 | tf_op jit(solution)/shard_map/ppermute | solution.py:272
  120.2 50.0 %collective-permute-start.73 = (bf16[16,64,128]{2,1,0:T(8,128)(2,1)S(1)}, bf16[16,64,128]{2,1,0:T(8,128)(2,1)S(1)}, u32[]{:S(2)}, u32[]{:S(2)}) collective-permute-start(bf16[16,64,128]{2,1,0:T(8,128)(2,1)S(1)} %apply_gate.7.refs_7_), channel_id=1, source_target_pairs={{0,2},{1,3},{2,0},{3,1},{4,6},{5,7},{6,4},{7,5},{8,10},{9,11},{10,... | collective-permute-start | bytes 786440 | tf_op jit(solution)/shard_map/ppermute | solution.py:272
  121.7 48.5 %collective-permute-start.69 = (bf16[16,64,128]{2,1,0:T(8,128)(2,1)S(1)}, bf16[16,64,128]{2,1,0:T(8,128)(2,1)S(1)}, u32[]{:S(2)}, u32[]{:S(2)}) collective-permute-start(bf16[16,64,128]{2,1,0:T(8,128)(2,1)S(1)} %apply_gate.7.refs_7_), channel_id=1, source_target_pairs={{0,1},{1,0},{2,3},{3,2},{4,5},{5,4},{6,7},{7,6},{8,9},{9,8},{10,11... | collective-permute-start | bytes 786440 | tf_op jit(solution)/shard_map/ppermute | solution.py:272
  144.0 7.0 %collective-permute-start.37 = (bf16[8,16,128]{2,1,0:T(8,128)(2,1)S(1)}, bf16[8,16,128]{2,1,0:T(8,128)(2,1)S(1)}, u32[]{:S(2)}, u32[]{:S(2)}) collective-permute-start(bf16[8,16,128]{2,1,0:T(8,128)(2,1)S(1)} %copy-done.31), channel_id=1, source_target_pairs={{0,28},{4,24},{8,20},{12,16},{16,12},{20,8},{24,4},{28,0},{1,29},{... | collective-permute-start | bytes 98312 | tf_op jit(solution)/shard_map/ppermute | solution.py:272
  147.7 6.3 %collective-permute-start.46 = (bf16[8,16,128]{2,1,0:T(8,128)(2,1)S(1)}, bf16[8,16,128]{2,1,0:T(8,128)(2,1)S(1)}, u32[]{:S(2)}, u32[]{:S(2)}) collective-permute-start(bf16[8,16,128]{2,1,0:T(8,128)(2,1)S(1)} %get-tuple-element.139), channel_id=1, source_target_pairs={{0,8},{4,12},{8,0},{12,4},{16,24},{20,28},{24,16},{28,20},{1,9},{5... | collective-permute-start | bytes 98312 | tf_op jit(solution)/shard_map/ppermute | solution.py:272
  151.0 6.4 %collective-permute-start.48 = (bf16[8,16,128]{2,1,0:T(8,128)(2,1)S(1)}, bf16[8,16,128]{2,1,0:T(8,128)(2,1)S(1)}, u32[]{:S(2)}, u32[]{:S(2)}) collective-permute-start(bf16[8,16,128]{2,1,0:T(8,128)(2,1)S(1)} %get-tuple-element.141), channel_id=1, source_target_pairs={{0,16},{4,20},{8,24},{12,28},{16,0},{20,4},{24,8},{28,12},{1,17},{... | collective-permute-start | bytes 98312 | tf_op jit(solution)/shard_map/ppermute | solution.py:272
  157.3 6.6 %collective-permute-start.51 = (bf16[8,16,128]{2,1,0:T(8,128)(2,1)S(1)}, bf16[8,16,128]{2,1,0:T(8,128)(2,1)S(1)}, u32[]{:S(2)}, u32[]{:S(2)}) collective-permute-start(bf16[8,16,128]{2,1,0:T(8,128)(2,1)S(1)} %get-tuple-element.144), channel_id=1, source_target_pairs={{0,28},{4,24},{8,20},{12,16},{16,12},{20,8},{24,4},{28,0},{1,29},{... | collective-permute-start | bytes 98312 | tf_op jit(solution)/shard_map/ppermute | solution.py:272
  163.9 5.9 %collective-permute-start.2 = (bf16[256,256]{1,0:T(8,128)(2,1)S(1)}, bf16[256,256]{1,0:T(8,128)(2,1)S(1)}, u32[]{:S(2)}, u32[]{:S(2)}) collective-permute-start(bf16[256,256]{1,0:T(8,128)(2,1)S(1)} %get-tuple-element.86), channel_id=1, source_target_pairs={{0,3},{1,2},{2,1},{3,0},{4,7},{5,6},{6,5},{7,4},{8,11},{9,10},{10,... | collective-permute-start | bytes 393224 | tf_op jit(solution)/shard_map/ppermute | solution.py:272
  164.8 9.6 %collective-permute-start.72 = (bf16[16,64,128]{2,1,0:T(8,128)(2,1)S(1)}, bf16[16,64,128]{2,1,0:T(8,128)(2,1)S(1)}, u32[]{:S(2)}, u32[]{:S(2)}) collective-permute-start(bf16[16,64,128]{2,1,0:T(8,128)(2,1)S(1)} %apply_gate.6.refs_6_), channel_id=1, source_target_pairs={{0,2},{1,3},{2,0},{3,1},{4,6},{5,7},{6,4},{7,5},{8,10},{9,11},{10,... | collective-permute-start | bytes 786440 | tf_op jit(solution)/shard_map/ppermute | solution.py:272
  166.5 9.0 %collective-permute-start.68 = (bf16[16,64,128]{2,1,0:T(8,128)(2,1)S(1)}, bf16[16,64,128]{2,1,0:T(8,128)(2,1)S(1)}, u32[]{:S(2)}, u32[]{:S(2)}) collective-permute-start(bf16[16,64,128]{2,1,0:T(8,128)(2,1)S(1)} %apply_gate.6.refs_6_), channel_id=1, source_target_pairs={{0,1},{1,0},{2,3},{3,2},{4,5},{5,4},{6,7},{7,6},{8,9},{9,8},{10,11... | collective-permute-start | bytes 786440 | tf_op jit(solution)/shard_map/ppermute | solution.py:272
  169.8 10.2 %collective-permute-start.71 = (bf16[16,64,128]{2,1,0:T(8,128)(2,1)S(1)}, bf16[16,64,128]{2,1,0:T(8,128)(2,1)S(1)}, u32[]{:S(2)}, u32[]{:S(2)}) collective-permute-start(bf16[16,64,128]{2,1,0:T(8,128)(2,1)S(1)} %apply_gate.5.refs_5_), channel_id=1, source_target_pairs={{0,2},{1,3},{2,0},{3,1},{4,6},{5,7},{6,4},{7,5},{8,10},{9,11},{10,... | collective-permute-start | bytes 786440 | tf_op jit(solution)/shard_map/ppermute | solution.py:272
  170.2 10.9 %collective-permute-start.67 = (bf16[16,64,128]{2,1,0:T(8,128)(2,1)S(1)}, bf16[16,64,128]{2,1,0:T(8,128)(2,1)S(1)}, u32[]{:S(2)}, u32[]{:S(2)}) collective-permute-start(bf16[16,64,128]{2,1,0:T(8,128)(2,1)S(1)} %apply_gate.5.refs_5_), channel_id=1, source_target_pairs={{0,1},{1,0},{2,3},{3,2},{4,5},{5,4},{6,7},{7,6},{8,9},{9,8},{10,11... | collective-permute-start | bytes 786440 | tf_op jit(solution)/shard_map/ppermute | solution.py:272
  170.2 15.4 %collective-permute-start.70 = (bf16[16,64,128]{2,1,0:T(8,128)(2,1)S(1)}, bf16[16,64,128]{2,1,0:T(8,128)(2,1)S(1)}, u32[]{:S(2)}, u32[]{:S(2)}) collective-permute-start(bf16[16,64,128]{2,1,0:T(8,128)(2,1)S(1)} %apply_gate.4.refs_4_), channel_id=1, source_target_pairs={{0,2},{1,3},{2,0},{3,1},{4,6},{5,7},{6,4},{7,5},{8,10},{9,11},{10,... | collective-permute-start | bytes 786440 | tf_op jit(solution)/shard_map/ppermute | solution.py:272
  174.4 11.6 %collective-permute-start.66 = (bf16[16,64,128]{2,1,0:T(8,128)(2,1)S(1)}, bf16[16,64,128]{2,1,0:T(8,128)(2,1)S(1)}, u32[]{:S(2)}, u32[]{:S(2)}) collective-permute-start(bf16[16,64,128]{2,1,0:T(8,128)(2,1)S(1)} %apply_gate.4.refs_4_), channel_id=1, source_target_pairs={{0,1},{1,0},{2,3},{3,2},{4,5},{5,4},{6,7},{7,6},{8,9},{9,8},{10,11... | collective-permute-start | bytes 786440 | tf_op jit(solution)/shard_map/ppermute | solution.py:272
  175.5 10.4 %collective-permute-start.77 = (bf16[16,64,128]{2,1,0:T(8,128)(2,1)S(1)}, bf16[16,64,128]{2,1,0:T(8,128)(2,1)S(1)}, u32[]{:S(2)}, u32[]{:S(2)}) collective-permute-start(bf16[16,64,128]{2,1,0:T(8,128)(2,1)S(1)} %collective-permute-done.73.refs_15_), channel_id=1, source_target_pairs={{0,1},{1,0},{2,3},{3,2},{4,5},{5,4},{6,7},{7,6},{8,9},{9,8},{10,11... | collective-permute-start | bytes 786440 | tf_op jit(solution)/shard_map/ppermute | solution.py:272
  180.0 6.0 %collective-permute-start.76 = (bf16[16,64,128]{2,1,0:T(8,128)(2,1)S(1)}, bf16[16,64,128]{2,1,0:T(8,128)(2,1)S(1)}, u32[]{:S(2)}, u32[]{:S(2)}) collective-permute-start(bf16[16,64,128]{2,1,0:T(8,128)(2,1)S(1)} %collective-permute-done.72.refs_14_), channel_id=1, source_target_pairs={{0,1},{1,0},{2,3},{3,2},{4,5},{5,4},{6,7},{7,6},{8,9},{9,8},{10,11... | collective-permute-start | bytes 786440 | tf_op jit(solution)/shard_map/ppermute | solution.py:272
  (66 other events, 1138.1 us)
where the time goes:
time: 191 us; the launch traced here: 190 us
  starting transfers between devices  99.3 us (52%)
  waiting for transfers between devices  41.1 us (22%)
  local copies, waits for them, and re-layouts  24.9 us (13%)
  Pallas kernels  24.5 us (13%)
    ppermute x78, starting transfers between devices, swap(): return lax.ppermute(value, axis, [(i, i ^ step) for i in range(size)])  99.3 us
    ppermute x78, waiting for transfers between devices, swap(): return lax.ppermute(value, axis, [(i, i ^ step) for i in range(size)])  41.1 us
    unnamed x104, local copies, waits for them, and re-layouts  24.7 us
    pallas_call x4, Pallas kernels, convolve(): pl.pallas_call(functools.partial(conv_kernel, seq, cpc, rows), grid=(1,),...  14.2 us
    pallas_call x1, Pallas kernels, project(): pl.pallas_call(functools.partial(project_kernel, seq, cpc), grid=(frames...  5.03 us
  transfers between devices with their start and end apart: 78, of which 19 were waited for; matrix products, arithmetic and copies ran while one was open for 0% of the time, Pallas kernels for 9%

commit v1 on v0

v1 whole, which is shorter than its diff:
```python
import functools
import math

import jax
import jax.numpy as jnp
import numpy as np
from jax import lax
from jax.experimental import pallas as pl
from jax.experimental.pallas import tpu as pltpu
from jax.sharding import PartitionSpec as P

LANES = 128
SMALL = 16
SHARES = (16, 16)
BF16 = jnp.bfloat16
F32 = jnp.float32


def dot(left, right):
    return jnp.dot(left, right, preferred_element_type=F32)


def cost(flops, data):
    return pl.CostEstimate(flops=int(flops), bytes_accessed=int(data), transcendentals=0)


def params(mib):
    return pltpu.CompilerParams(vmem_limit_bytes=mib * 1024 * 1024)


def tables(rows):
    total = rows * LANES
    r = np.arange(rows, dtype=np.float64)
    l = np.arange(LANES, dtype=np.float64)
    first = 2 * np.pi * np.outer(r + 0.25, r) / rows
    twist = 2 * np.pi * np.outer(r + 0.25, l) / total
    second = 2 * np.pi * np.outer(l, l) / LANES
    a_fwd = np.concatenate([np.cos(first), -np.sin(first)], 0)
    a_inv = np.concatenate([np.cos(first).T, -np.sin(first).T], 1) / rows
    c2, s2 = np.cos(second), np.sin(second)
    b_fwd = np.block([[c2, -s2], [s2, c2]])
    b_inv = np.block([[c2, s2], [-s2, c2]]) / LANES
    as_bf = lambda v: jnp.asarray(v.astype(np.float32)).astype(BF16)
    as_f = lambda v: jnp.asarray(v.astype(np.float32))
    return (as_bf(a_fwd), as_bf(b_fwd), as_bf(b_inv), as_bf(a_inv), as_f(np.cos(twist)), as_f(np.sin(twist)))


def seq_peer(step):
    return lax.bitwise_xor(lax.axis_index("seq"), jnp.int32(step))


def block_shapes(seq, cpc, rows):
    return [jax.ShapeDtypeStruct((cpc, rows, LANES), BF16)] * seq


def whole(shape):
    return pl.BlockSpec(tuple(shape), lambda i: (0,) * len(shape))


def tie(value, *after):
    return lax.optimization_barrier((value, *after))[0]


def cut_blocks(turned, outs, cpcs, rows):
    seq = len(outs)
    for d in range(seq):
        peer, start, used = seq_peer(d), 0, 0
        for cpc in cpcs:
            first = pl.multiple_of((start + peer * cpc) * rows, 8)
            part = turned[pl.ds(first, cpc * rows), :]
            outs[d][pl.ds(used, cpc)] = part.reshape(cpc, rows, LANES).astype(BF16)
            start += seq * cpc
            used += cpc


def filter_kernel(seq, cpcs, f_ref, out, turned):
    frames, chans = f_ref.shape
    rows = frames // LANES
    for r in range(rows):
        turned[pl.ds(r, chans, stride=rows), :] = f_ref[pl.ds(r * LANES, LANES), :].astype(F32).T
    start, used = 0, 0
    for cpc in cpcs:
        part = turned[pl.ds(start * rows, seq * cpc * rows), :].reshape(seq, cpc, rows, LANES)
        out[:, pl.ds(used, cpc)] = part.astype(BF16)
        start += seq * cpc
        used += cpc


def prepare_filters(filters, seq, cpcs):
    frames, chans = filters.shape
    rows = frames // LANES
    return pl.pallas_call(
        functools.partial(filter_kernel, seq, cpcs),
        out_shape=jax.ShapeDtypeStruct((seq, chans // seq, rows, LANES), BF16),
        scratch_shapes=[pltpu.VMEM((chans * rows, LANES), F32)],
        compiler_params=params(12),
        cost_estimate=cost(0, 8 * frames * chans),
        name="filter_blocks",
    )(filters)


def project_kernel(seq, cpcs, x_ref, w_ref, _, *refs):
    n = len(cpcs)
    gates, sigs, sends, turned = refs[:n], refs[n : 2 * n], refs[2 * n : -1], refs[-1]
    tile = x_ref.shape[0]
    chans = w_ref.shape[2]
    step = pl.program_id(0)
    rows_here = tile // LANES
    rows = turned.shape[0] // chans
    x = x_ref[...]
    gate = dot(x, w_ref[0]).astype(BF16).astype(F32)
    key = dot(x, w_ref[1]).astype(BF16).astype(F32)
    value = dot(x, w_ref[2]).astype(BF16).astype(F32)
    signal = key * value
    for r in range(rows_here):
        here = slice(r * LANES, (r + 1) * LANES)
        turned_gate, flipped = gate[here].T, signal[here].T
        start = 0
        for k, cpc in enumerate(cpcs):
            span = slice(start, start + seq * cpc)
            gates[k][r] = turned_gate[span].astype(BF16)
            sigs[k][r] = flipped[span].astype(BF16)
            start += seq * cpc
        turned[pl.ds(step * rows_here + r, chans, stride=rows), :] = flipped

    @pl.when(step == pl.num_programs(0) - 1)
    def _():
        cut_blocks(turned, sends, cpcs, rows)


def project(frames_in, w_in, ready, seq, cpcs):
    frames, width = frames_in.shape
    chans = w_in.shape[2]
    rows = frames // LANES
    tile = 512
    send_shapes = block_shapes(seq, sum(cpcs), rows)
    out = pl.pallas_call(
        functools.partial(project_kernel, seq, cpcs),
        grid=(frames // tile,),
        in_specs=[
            pl.BlockSpec((tile, width), lambda i: (i, 0)),
            whole(w_in.shape),
            pl.BlockSpec(memory_space=pl.ANY),
        ],
        out_specs=[
            pl.BlockSpec((tile // LANES, seq * cpc, LANES), lambda i: (i, 0, 0)) for cpc in cpcs
        ]
        * 2
        + [whole(v.shape) for v in send_shapes],
        out_shape=[jax.ShapeDtypeStruct((rows, seq * cpc, LANES), BF16) for cpc in cpcs] * 2
        + send_shapes,
        scratch_shapes=[pltpu.VMEM((chans * rows, LANES), F32)],
        compiler_params=params(58),
        cost_estimate=cost(6 * frames * width * chans, 16 * 1024 * 1024),
        name="project",
    )(frames_in, w_in, ready)
    n = len(cpcs)
    return out[:n], out[n : 2 * n], out[2 * n :]


def gather_rows(grid, blocks, first, cpc):
    rows = blocks[0].shape[1]
    for d, block in enumerate(blocks):
        place = pl.ds(pl.multiple_of(seq_peer(d) * rows, 16), rows)
        grid[:, place, :] = block[pl.ds(first, cpc)]


def twisted(outer, tc, ts):
    full = outer.shape[0] // 2
    parts = []
    for side in (slice(0, LANES), slice(LANES, 2 * LANES)):
        re, im = outer[:full, side], outer[full:, side]
        parts.append(jnp.concatenate([re * tc + im * ts, im * tc - re * ts], 1).astype(BF16))
    return jnp.concatenate(parts, 0)


def forward_pair(grid, c, consts):
    a_fwd, b_fwd, tc, ts = consts
    outer = dot(a_fwd[...], jnp.concatenate([grid[c], grid[c + 1]], 1))
    return dot(twisted(outer, tc, ts), b_fwd[...])


def spectra_kernel(f_ref, a_fwd, b_fwd, tc_ref, ts_ref, out, grid):
    seq, _, rows, _ = f_ref.shape
    chans, full, _ = out.shape
    for j in range(seq):
        grid[:, j * rows : (j + 1) * rows, :] = f_ref[j]
    tc, ts = tc_ref[...], ts_ref[...]
    for c in range(0, chans, 2):
        spec = forward_pair(grid, c, (a_fwd, b_fwd, tc, ts))
        out[c] = spec[:full]
        out[c + 1] = spec[full:]


def filter_spectra(filt, consts):
    a_fwd, b_fwd, _, _, tc, ts = consts
    seq, chans, rows, _ = filt.shape
    full = rows * seq
    return pl.pallas_call(
        spectra_kernel,
        out_shape=jax.ShapeDtypeStruct((chans, full, 2 * LANES), F32),
        scratch_shapes=[pltpu.VMEM((chans, full, LANES), BF16)],
        compiler_params=params(SMALL),
        cost_estimate=cost(chans * full * LANES * LANES * 8, chans * full * LANES * 10),
        name="filter_spectra",
    )(filt, a_fwd, b_fwd, tc, ts)


def conv_kernel(seq, first, skipped, *refs):
    s_refs, rest = refs[:seq], refs[seq:]
    spec_ref, a_fwd, b_fwd, b_inv, a_inv, tc_ref, ts_ref = rest[:7]
    y_refs = rest[7 + skipped : 7 + skipped + seq]
    grid, grid_y, work = rest[7 + skipped + seq :]
    cpc, rows, _ = y_refs[0].shape
    full = rows * seq
    gather_rows(grid, s_refs, first, cpc)
    tc, ts = tc_ref[...], ts_ref[...]
    pairs = [(c, pl.ds(c * full, 2 * full)) for c in range(0, cpc, 2)]
    for c, here in pairs:
        outer = dot(a_fwd[...], jnp.concatenate([grid[c], grid[c + 1]], 1))
        work[here, :] = twisted(outer, tc, ts)
    for c, here in pairs:
        mine = dot(work[here, :], b_fwd[...])
        other = spec_ref[pl.ds(first + c, 2)].reshape(2 * full, 2 * LANES)
        sr, si, fr, fi = mine[:, :LANES], mine[:, LANES:], other[:, :LANES], other[:, LANES:]
        work[here, :] = jnp.concatenate([sr * fr - si * fi, sr * fi + si * fr], 1).astype(BF16)
    for c, here in pairs:
        inner = dot(work[here, :], b_inv[...])
        for i in range(2):
            re, im = inner[i * full : (i + 1) * full, :LANES], inner[i * full : (i + 1) * full, LANES:]
            back = jnp.concatenate([re * tc - im * ts, im * tc + re * ts], 1)
            work[pl.ds((c + i) * full, full), :] = back.astype(BF16)
    for c, here in pairs:
        back = work[here, :]
        re = jnp.concatenate([back[:full, :LANES], back[full:, :LANES]], 1)
        im = jnp.concatenate([back[:full, LANES:], back[full:, LANES:]], 1)
        y = dot(a_inv[...], jnp.concatenate([re, im], 0)).astype(BF16)
        grid_y[c] = y[:, :LANES]
        grid_y[c + 1] = y[:, LANES:]
    for d in range(seq):
        place = pl.ds(pl.multiple_of(seq_peer(d) * rows, 16), rows)
        y_refs[d][...] = grid_y[:, place, :]


def convolve(sig, spec, consts, first, cpc, ready):
    seq = len(sig)
    rows = sig[0].shape[1]
    full = rows * seq
    anywhere = [pl.BlockSpec(memory_space=pl.ANY)] * len(ready)
    ins = (*sig, spec, *consts)
    return pl.pallas_call(
        functools.partial(conv_kernel, seq, first, len(ready)),
        in_specs=[pl.BlockSpec(memory_space=pltpu.VMEM)] * len(ins) + anywhere,
        out_shape=block_shapes(seq, cpc, rows),
        scratch_shapes=[pltpu.VMEM((cpc, full, LANES), BF16)] * 2
        + [pltpu.VMEM((cpc * full, 2 * LANES), BF16)],
        compiler_params=params(SMALL),
        cost_estimate=cost(cpc * full * LANES * LANES * 16, cpc * full * LANES * 12),
        name="convolve",
    )(*ins, *ready)


def gate_kernel(seq, first_chan, *refs):
    gate_ref, sig_ref, skip_ref, out_ref, grid_y = refs[seq:]
    rows, group, _ = out_ref.shape
    part = group // seq * rows
    for d in range(seq):
        start = pl.multiple_of(seq_peer(d) * part, 8)
        grid_y[pl.ds(start, part), :] = refs[d][...].astype(F32).reshape(part, LANES)
    skip = jnp.broadcast_to(skip_ref[...], (LANES, skip_ref.shape[1])).T[
        first_chan : first_chan + group, :1
    ]
    for r in range(rows):
        y = grid_y[pl.ds(r, group, stride=rows), :]
        out_ref[r] = (gate_ref[r].astype(F32) * (y + skip * sig_ref[r].astype(F32))).astype(BF16)


def apply_gate(y, gate, signal, skip, first_chan):
    seq = len(y)
    rows, group, _ = gate.shape
    return pl.pallas_call(
        functools.partial(gate_kernel, seq, first_chan),
        out_shape=jax.ShapeDtypeStruct(gate.shape, BF16),
        scratch_shapes=[pltpu.VMEM((group * rows, LANES), F32)],
        compiler_params=params(SMALL),
        cost_estimate=cost(0, 10 * rows * group * LANES),
        name="apply_gate",
    )(*y, gate, signal, skip)


def out_weights_kernel(ways, w_ref, *outs):
    depth = w_ref.shape[1] // ways
    for d in range(ways):
        peer = lax.bitwise_xor(lax.axis_index("ch"), jnp.int32(d))
        cols = pl.ds(pl.multiple_of(peer * depth, LANES), depth)
        outs[d][...] = w_ref[:, cols].astype(F32).T.astype(BF16)


def out_weights(w_out, ways):
    chans, width = w_out.shape
    return pl.pallas_call(
        functools.partial(out_weights_kernel, ways),
        out_shape=[jax.ShapeDtypeStruct((width // ways, chans), BF16)] * ways,
        compiler_params=params(12),
        cost_estimate=cost(0, 4 * chans * width),
        name="out_weights",
    )(w_out)


def partial_mix(w_refs, g_refs, start, r):
    total = None
    for w_ref, g_ref in zip(w_refs, g_refs):
        rows = slice(start, start + g_ref.shape[1])
        term = dot(w_ref[:, rows], jnp.concatenate([g_ref[r], g_ref[r + 1]], 1))
        total = term if total is None else total + term
    return total


def mix_first_kernel(ways, start, *refs):
    w_refs, g_refs, out_ref = refs[:ways], refs[ways : 2 * ways], refs[-1]
    for r in range(0, g_refs[0].shape[0], 2):
        out_ref[r // 2] = partial_mix(w_refs, g_refs, start, r)


def mix_first(weights, gated, start):
    ways = len(weights)
    rows, group, _ = gated[0].shape
    depth = weights[0].shape[0]
    return pl.pallas_call(
        functools.partial(mix_first_kernel, ways, start),
        out_shape=jax.ShapeDtypeStruct((rows // 2, depth, 2 * LANES), F32),
        compiler_params=params(SMALL),
        cost_estimate=cost(2 * rows * LANES * depth * group * ways, 4 * 1024 * 1024),
        name="mix_first",
    )(*weights, *gated)


def mix_last_kernel(ways, start, *refs):
    w_refs, g_refs = refs[:ways], refs[ways : 2 * ways]
    before, out_ref, held, sems = refs[2 * ways :]
    copies = []
    for r in range(0, g_refs[0].shape[0], 2):
        total = before[r // 2] + partial_mix(w_refs, g_refs, start, r)
        span = pl.ds(r * LANES, 2 * LANES)
        held[span, :] = total.T.astype(BF16)
        copies.append(pltpu.make_async_copy(held.at[span], out_ref.at[span], sems.at[r // 2]))
        copies[-1].start()
    for copy in copies:
        copy.wait()


def mix_last(weights, gated, before, start):
    ways = len(weights)
    rows, group, _ = gated[0].shape
    depth = weights[0].shape[0]
    out = (rows * LANES, depth)
    return pl.pallas_call(
        functools.partial(mix_last_kernel, ways, start),
        out_shape=jax.ShapeDtypeStruct(out, BF16),
        out_specs=pl.BlockSpec(memory_space=pl.ANY),
        scratch_shapes=[pltpu.VMEM(out, BF16), pltpu.SemaphoreType.DMA((rows // 2,))],
        compiler_params=params(SMALL),
        cost_estimate=cost(2 * rows * LANES * depth * group * ways, 6 * 1024 * 1024),
        name="mix_last",
    )(*weights, *gated, before)


def swap(value, axis, step):
    size = lax.axis_size(axis)
    return lax.ppermute(value, axis, [(i, i ^ step) for i in range(size)])


def exchange(blocks):
    return [b if d == 0 else swap(b, "seq", d) for d, b in enumerate(blocks)]


def on_device(frames_in, w_in, filters, skip_gain, w_out):
    seq, ways = lax.axis_size("seq"), lax.axis_size("ch")
    frames, width = frames_in.shape
    chans = filters.shape[1]
    cpcs = [chans * share // (seq * 32) for share in SHARES]
    consts = tables(seq * frames // LANES)
    filt_sends = prepare_filters(filters, seq, cpcs)
    filt = lax.all_to_all(filt_sends, "seq", split_axis=0, concat_axis=0, tiled=True)
    weights = [
        w if d == 0 else swap(w, "ch", d) for d, w in enumerate(out_weights(w_out, ways))
    ]
    gates, sigs, sends = project(frames_in, w_in.transpose(1, 0, 2), filt_sends, seq, cpcs)
    sig = exchange(sends)
    spec = filter_spectra(filt, consts)
    first, start, before, total = 0, 0, [], None
    for k, cpc in enumerate(cpcs):
        y = convolve(sig, spec, consts, first, cpc, [*weights, *before])
        before = [y[0]]
        y = exchange(y)
        mine = apply_gate(y, gates[k], sigs[k], skip_gain[None, :], start)
        far = swap(mine, "ch", 2)
        gated = [mine, swap(mine, "ch", 1), far, swap(far, "ch", 1)]
        if k == 0:
            total = mix_first(weights, gated, start)
        else:
            total = mix_last(weights, gated, total, start)
        first += cpc
        start += seq * cpc
    return total


def solution(mesh):
    in_specs = (P("seq", None), P(None, None, "ch"), P("seq", "ch"), P("ch"), P("ch", None))
    out_specs = P("seq", "ch")
    return jax.shard_map(
        on_device, mesh=mesh, in_specs=in_specs, out_specs=out_specs, check_vma=False
    )
```

time: 191 us -> 111 us (0.58)
  starting transfers between devices: 99.3 us -> 53.5 us
  local copies, waits for them, and re-layouts: 24.9 us -> 1.28 us
  Pallas kernels: 24.5 us -> 19.3 us
  waiting for transfers between devices: 41.1 us -> 36.9 us
    ppermute x78 -> x30, starting transfers between devices: 99.3 us -> 46.2 us  [swap(): return lax.ppermute(value, axis, [(i, i ^ step) for i in range(size)])]
    unnamed x104 -> x28, local copies, waits for them, and re-layouts: 24.7 us -> 1.28 us
    ppermute x78 -> x30, waiting for transfers between devices: 41.1 us -> 24.2 us  [swap(): return lax.ppermute(value, axis, [(i, i ^ step) for i in range(size)])]
    all_to_all x0 -> x1, waiting for transfers between devices: none -> 12.6 us  [on_device(): lax.all_to_all(filt_sends, 'seq', split_axis=0, concat_axis=0, tiled=True)]
    all_to_all x0 -> x1, starting transfers between devices: none -> 7.28 us  [on_device(): lax.all_to_all(filt_sends, 'seq', split_axis=0, concat_axis=0, tiled=True)]
    pallas_call x11 -> x9, Pallas kernels: 24.3 us -> 19.1 us  [the longest x1 8.26 us: project(): pl.pallas_call(functools.partial(project_kernel, seq, cpcs), grid=(frames...]
  transfers between devices with their start and end apart: 78 -> 31, of which waited for: 19 -> 9; matrix products, arithmetic and copies ran while one was open for 0% -> 0% of each run, Pallas kernels for 9% -> 13%
where the time goes in v1:
time: 111 us
  starting transfers between devices  53.5 us (48%)
  waiting for transfers between devices  36.9 us (33%)
  Pallas kernels  19.3 us (17%)
  local copies, waits for them, and re-layouts  1.28 us (1%)
    ppermute x30, starting transfers between devices, swap(): return lax.ppermute(value, axis, [(i, i ^ step) for i in range(size)])  46.2 us
    ppermute x30, waiting for transfers between devices, swap(): return lax.ppermute(value, axis, [(i, i ^ step) for i in range(size)])  24.2 us
    all_to_all x1, waiting for transfers between devices, on_device(): lax.all_to_all(filt_sends, 'seq', split_axis=0, concat_axis=0, tiled=True)  12.6 us
    pallas_call x1, Pallas kernels, project(): pl.pallas_call(functools.partial(project_kernel, seq, cpcs), grid=(frames...  8.26 us
    all_to_all x1, starting transfers between devices, on_device(): lax.all_to_all(filt_sends, 'seq', split_axis=0, concat_axis=0, tiled=True)  7.28 us
    pallas_call x2, Pallas kernels, convolve(): pl.pallas_call(functools.partial(conv_kernel, seq, first, len(ready)), in...  2.79 us
  transfers between devices with their start and end apart: 31, of which 9 were waited for; matrix products, arithmetic and copies ran while one was open for 0% of the time, Pallas kernels for 13%

profile of v1, /device:TPU:0, one launch (start us, length us, event | category | flops | bytes accessed | tf_op | source)
XLA Modules:
  0.0 111.2 jit_solution(14874477258047121948)
XLA Ops:
  0.0 1.2 %copy-done.1 = bf16[2048,256]{1,0:T(8,128)(2,1)S(1)} copy-done((bf16[2048,256]{1,0:T(8,128)(2,1)S(1)}, bf16[2048,256]{1,0:T(8,128)(2,1)}, u32[]{:S(2)}) %copy-start.1) | copy-done | bytes 1048600
  1.2 1.9 %filter_blocks.1._ = bf16[8,32,16,128]{3,2,1,0:T(8,128)(2,1)} custom-call(bf16[2048,256]{1,0:T(8,128)(2,1)S(1)} %copy-done.1), custom_call_target="tpu_custom_call" | custom-call | bytes 4194304 | tf_op jit(solution)/shard_map/filter_blocks/pallas_call | solution.py:92
  3.1 7.3 %all-to-all-start = ((bf16[8,32,16,128]{3,2,1,0:T(8,128)(2,1)}), bf16[8,32,16,128]{3,2,1,0:T(8,128)(2,1)S(1)}, u32[]{:S(2)}, u32[]{:S(2)}) async-start(bf16[8,32,16,128]{3,2,1,0:T(8,128)(2,1)} %filter_blocks.1._), calls=%async_computation | async-start | bytes 2097152 | tf_op jit(solution)/shard_map/all_to_all | solution.py:384
  10.4 0.2 out_weights.1
  10.6 0.1 collective-permute-start
  10.7 1.6 %collective-permute-start.1 = (bf16[256,256]{1,0:T(8,128)(2,1)S(1)}, bf16[256,256]{1,0:T(8,128)(2,1)S(1)}, u32[]{:S(2)}, u32[]{:S(2)}) collective-permute-start(bf16[256,256]{1,0:T(8,128)(2,1)S(1)} %get-tuple-element.39), channel_id=1, source_target_pairs={{0,2},{1,3},{2,0},{3,1},{4,6},{5,7},{6,4},{7,5},{8,10},{9,11},{10,... | collective-permute-start | bytes 393224 | tf_op jit(solution)/shard_map/ppermute | solution.py:370
  12.2 0.3 collective-permute-start.2
  12.5 8.3 %project.1 = (bf16[16,128,128]{2,1,0:T(8,128)(2,1)}, bf16[16,128,128]{2,1,0:T(8,128)(2,1)}, bf16[16,128,128]{2,1,0:T(8,128)(2,1)}, bf16[16,128,128]{2,1,0:T(8,12...) custom-call(bf16[2048,1024]{1,0:T(8,128)(2,1)} %x_ref.1, ...), custom_call_target="tpu_custom_call" | custom-call | flops 3221225472 | bytes 16777216 | tf_op jit(solution)/shard_map/project/pallas_call | solution.py:137
  20.8 0.0 copy-start.5
  20.8 0.0 copy-start.12
  20.8 2.1 %collective-permute-start.3 = (bf16[32,16,128]{2,1,0:T(8,128)(2,1)}, bf16[32,16,128]{2,1,0:T(8,128)(2,1)S(1)}, u32[]{:S(2)}, u32[]{:S(2)}) collective-permute-start(bf16[32,16,128]{2,1,0:T(8,128)(2,1)} %get-tuple-element.42), channel_id=1, source_target_pairs={{0,4},{4,0},{8,12},{12,8},{16,20},{20,16},{24,28},{28,24},{1,5},{5... | collective-permute-start | bytes 393224 | tf_op jit(solution)/shard_map/ppermute | solution.py:370
  22.9 1.5 %collective-permute-start.4 = (bf16[32,16,128]{2,1,0:T(8,128)(2,1)}, bf16[32,16,128]{2,1,0:T(8,128)(2,1)S(1)}, u32[]{:S(2)}, u32[]{:S(2)}) collective-permute-start(bf16[32,16,128]{2,1,0:T(8,128)(2,1)} %get-tuple-element.43), channel_id=1, source_target_pairs={{0,8},{4,12},{8,0},{12,4},{16,24},{20,28},{24,16},{28,20},{1,9},{5... | collective-permute-start | bytes 393224 | tf_op jit(solution)/shard_map/ppermute | solution.py:370
  24.4 0.1 collective-permute-start.5
  24.5 0.0 collective-permute-done.1.refs_17_.refs_2_
  24.5 2.8 %collective-permute-start.6 = (bf16[32,16,128]{2,1,0:T(8,128)(2,1)}, bf16[32,16,128]{2,1,0:T(8,128)(2,1)S(1)}, u32[]{:S(2)}, u32[]{:S(2)}) collective-permute-start(bf16[32,16,128]{2,1,0:T(8,128)(2,1)} %get-tuple-element.45), channel_id=1, source_target_pairs={{0,16},{4,20},{8,24},{12,28},{16,0},{20,4},{24,8},{28,12},{1,17},{... | collective-permute-start | bytes 393224 | tf_op jit(solution)/shard_map/ppermute | solution.py:370
  27.3 0.0 collective-permute-done.2.refs_18_.refs_3_
  27.3 1.5 %collective-permute-start.7 = (bf16[32,16,128]{2,1,0:T(8,128)(2,1)}, bf16[32,16,128]{2,1,0:T(8,128)(2,1)S(1)}, u32[]{:S(2)}, u32[]{:S(2)}) collective-permute-start(bf16[32,16,128]{2,1,0:T(8,128)(2,1)} %get-tuple-element.46), channel_id=1, source_target_pairs={{0,20},{4,16},{8,28},{12,24},{16,4},{20,0},{24,12},{28,8},{1,21},{... | collective-permute-start | bytes 393224 | tf_op jit(solution)/shard_map/ppermute | solution.py:370
  28.8 0.2 collective-permute-done.3.refs_1_
  29.0 4.4 %collective-permute-start.8 = (bf16[32,16,128]{2,1,0:T(8,128)(2,1)}, bf16[32,16,128]{2,1,0:T(8,128)(2,1)S(1)}, u32[]{:S(2)}, u32[]{:S(2)}) collective-permute-start(bf16[32,16,128]{2,1,0:T(8,128)(2,1)} %get-tuple-element.47), channel_id=1, source_target_pairs={{0,24},{4,28},{8,16},{12,20},{16,8},{20,12},{24,0},{28,4},{1,25},{... | collective-permute-start | bytes 393224 | tf_op jit(solution)/shard_map/ppermute | solution.py:370
  33.5 2.7 %collective-permute-start.9 = (bf16[32,16,128]{2,1,0:T(8,128)(2,1)}, bf16[32,16,128]{2,1,0:T(8,128)(2,1)S(1)}, u32[]{:S(2)}, u32[]{:S(2)}) collective-permute-start(bf16[32,16,128]{2,1,0:T(8,128)(2,1)} %get-tuple-element.48), channel_id=1, source_target_pairs={{0,28},{4,24},{8,20},{12,16},{16,12},{20,8},{24,4},{28,0},{1,29},{... | collective-permute-start | bytes 393224 | tf_op jit(solution)/shard_map/ppermute | solution.py:370
  36.2 12.6 %all-to-all-done.f_ref = bf16[8,32,16,128]{3,2,1,0:T(8,128)(2,1)S(1)} async-done(((bf16[8,32,16,128]{3,2,1,0:T(8,128)(2,1)}), bf16[8,32,16,128]{3,2,1,0:T(8,128)(2,1)S(1)}, u32[]{:S(2)}, u32[]{:S(2)}) %all-to-all-start) | async-done | bytes 1048608 | tf_op jit(solution)/shard_map/all_to_all | solution.py:384
  48.9 1.4 %filter_spectra.1.refs_8_ = f32[32,128,256]{2,1,0:T(8,128)S(1)} custom-call(bf16[8,32,16,128]{3,2,1,0:T(8,128)(2,1)S(1)} %all-to-all-done.f_ref, bf16[256,128]{1,0:T(8,128)(2,1)S(1)} %copy-done.2, bf16[256,256]{1,0:T(8,128)(2,1)S(1)} %copy-done, f32[128,128]{1,0:T(8,128)S(1)} %copy-done.4, f32[128,128]{1,0:T(8,128)S(1)} %copy-done.3), custom_call_target="tpu_custom_call" | custom-call | flops 536870912 | bytes 5242880 | tf_op jit(solution)/shard_map/filter_spectra/pallas_call | solution.py:199
  50.3 1.4 %collective-permute-done.6.refs_4_ = bf16[32,16,128]{2,1,0:T(8,128)(2,1)S(1)} collective-permute-done((bf16[32,16,128]{2,1,0:T(8,128)(2,1)}, bf16[32,16,128]{2,1,0:T(8,128)(2,1)S(1)}, u32[]{:S(2)}, u32[]{:S(2)}) %collective-permute-start.6) | collective-permute-done | bytes 131104 | tf_op jit(solution)/shard_map/ppermute | solution.py:370
  51.6 3.3 %collective-permute-done.7.refs_5_ = bf16[32,16,128]{2,1,0:T(8,128)(2,1)S(1)} collective-permute-done((bf16[32,16,128]{2,1,0:T(8,128)(2,1)}, bf16[32,16,128]{2,1,0:T(8,128)(2,1)S(1)}, u32[]{:S(2)}, u32[]{:S(2)}) %collective-permute-start.7) | collective-permute-done | bytes 131104 | tf_op jit(solution)/shard_map/ppermute | solution.py:370
  54.9 0.0 collective-permute-done.8.refs_6_
  54.9 0.0 collective-permute-done.9.refs_7_
  54.9 1.4 %convolve.2 = (bf16[16,16,128]{2,1,0:T(8,128)(2,1)S(1)}, bf16[16,16,128]{2,1,0:T(8,128)(2,1)S(1)}, bf16[16,16,128]{2,1,0:T(8,128)(2,1)S(1)}, bf16[16,16,128]{2,1...) custom-call(bf16[32,16,128]{2,1,0:T(8,128)(2,1)S(1)} %copy-done.6, ...), custom_call_target="tpu_custom_call" | custom-call | flops 536870912 | bytes 3145728 | tf_op jit(solution)/shard_map/convolve/pallas_call | solution.py:251
  56.4 0.0 copy-start.13
  56.4 1.1 collective-permute-start.20
  57.5 4.7 %collective-permute-start.21 = (bf16[16,16,128]{2,1,0:T(8,128)(2,1)S(1)}, bf16[16,16,128]{2,1,0:T(8,128)(2,1)S(1)}, u32[]{:S(2)}, u32[]{:S(2)}) collective-permute-start(bf16[16,16,128]{2,1,0:T(8,128)(2,1)S(1)} %get-tuple-element.61), channel_id=1, source_target_pairs={{0,8},{4,12},{8,0},{12,4},{16,24},{20,28},{24,16},{28,20},{1,9},{5... | collective-permute-start | bytes 196616 | tf_op jit(solution)/shard_map/ppermute | solution.py:370
  62.2 0.8 collective-permute-start.22
  63.0 2.0 %collective-permute-start.23 = (bf16[16,16,128]{2,1,0:T(8,128)(2,1)S(1)}, bf16[16,16,128]{2,1,0:T(8,128)(2,1)S(1)}, u32[]{:S(2)}, u32[]{:S(2)}) collective-permute-start(bf16[16,16,128]{2,1,0:T(8,128)(2,1)S(1)} %get-tuple-element.63), channel_id=1, source_target_pairs={{0,16},{4,20},{8,24},{12,28},{16,0},{20,4},{24,8},{28,12},{1,17},{... | collective-permute-start | bytes 196616 | tf_op jit(solution)/shard_map/ppermute | solution.py:370
  65.0 1.0 collective-permute-start.24
  66.0 1.4 %convolve.3 = (bf16[16,16,128]{2,1,0:T(8,128)(2,1)S(1)}, bf16[16,16,128]{2,1,0:T(8,128)(2,1)S(1)}, bf16[16,16,128]{2,1,0:T(8,128)(2,1)S(1)}, bf16[16,16,128]{2,1...) custom-call(bf16[32,16,128]{2,1,0:T(8,128)(2,1)S(1)} %copy-done.6, ...), custom_call_target="tpu_custom_call" | custom-call | flops 536870912 | bytes 3145728 | tf_op jit(solution)/shard_map/convolve/pallas_call | solution.py:251
  67.4 0.0 collective-permute-done.20.refs_1_
  67.4 1.5 %collective-permute-start.25 = (bf16[16,16,128]{2,1,0:T(8,128)(2,1)S(1)}, bf16[16,16,128]{2,1,0:T(8,128)(2,1)S(1)}, u32[]{:S(2)}, u32[]{:S(2)}) collective-permute-start(bf16[16,16,128]{2,1,0:T(8,128)(2,1)S(1)} %get-tuple-element.65), channel_id=1, source_target_pairs={{0,24},{4,28},{8,16},{12,20},{16,8},{20,12},{24,0},{28,4},{1,25},{... | collective-permute-start | bytes 196616 | tf_op jit(solution)/shard_map/ppermute | solution.py:370
  69.0 3.2 %collective-permute-start.26 = (bf16[16,16,128]{2,1,0:T(8,128)(2,1)S(1)}, bf16[16,16,128]{2,1,0:T(8,128)(2,1)S(1)}, u32[]{:S(2)}, u32[]{:S(2)}) collective-permute-start(bf16[16,16,128]{2,1,0:T(8,128)(2,1)S(1)} %get-tuple-element.66), channel_id=1, source_target_pairs={{0,28},{4,24},{8,20},{12,16},{16,12},{20,8},{24,4},{28,0},{1,29},{... | collective-permute-start | bytes 196616 | tf_op jit(solution)/shard_map/ppermute | solution.py:370
  72.1 0.7 collective-permute-start.10
  72.8 0.0 collective-permute-done.23.refs_4_
  72.8 0.2 collective-permute-start.11
  73.0 0.0 collective-permute-done.24.refs_5_
  73.0 2.6 %collective-permute-start.12 = (bf16[16,16,128]{2,1,0:T(8,128)(2,1)S(1)}, bf16[16,16,128]{2,1,0:T(8,128)(2,1)S(1)}, u32[]{:S(2)}, u32[]{:S(2)}) collective-permute-start(bf16[16,16,128]{2,1,0:T(8,128)(2,1)S(1)} %get-tuple-element.53), channel_id=1, source_target_pairs={{0,12},{4,8},{8,4},{12,0},{16,28},{20,24},{24,20},{28,16},{1,13},{... | collective-permute-start | bytes 196616 | tf_op jit(solution)/shard_map/ppermute | solution.py:370
  75.6 0.0 collective-permute-done.25.refs_6_
  75.6 2.3 %collective-permute-start.13 = (bf16[16,16,128]{2,1,0:T(8,128)(2,1)S(1)}, bf16[16,16,128]{2,1,0:T(8,128)(2,1)S(1)}, u32[]{:S(2)}, u32[]{:S(2)}) collective-permute-start(bf16[16,16,128]{2,1,0:T(8,128)(2,1)S(1)} %get-tuple-element.54), channel_id=1, source_target_pairs={{0,16},{4,20},{8,24},{12,28},{16,0},{20,4},{24,8},{28,12},{1,17},{... | collective-permute-start | bytes 196616 | tf_op jit(solution)/shard_map/ppermute | solution.py:370
  78.0 0.0 collective-permute-done.26.refs_7_
  78.0 2.5 %collective-permute-start.14 = (bf16[16,16,128]{2,1,0:T(8,128)(2,1)S(1)}, bf16[16,16,128]{2,1,0:T(8,128)(2,1)S(1)}, u32[]{:S(2)}, u32[]{:S(2)}) collective-permute-start(bf16[16,16,128]{2,1,0:T(8,128)(2,1)S(1)} %get-tuple-element.55), channel_id=1, source_target_pairs={{0,20},{4,16},{8,28},{12,24},{16,4},{20,0},{24,12},{28,8},{1,21},{... | collective-permute-start | bytes 196616 | tf_op jit(solution)/shard_map/ppermute | solution.py:370
  80.5 2.1 %collective-permute-start.15 = (bf16[16,16,128]{2,1,0:T(8,128)(2,1)S(1)}, bf16[16,16,128]{2,1,0:T(8,128)(2,1)S(1)}, u32[]{:S(2)}, u32[]{:S(2)}) collective-permute-start(bf16[16,16,128]{2,1,0:T(8,128)(2,1)S(1)} %get-tuple-element.56), channel_id=1, source_target_pairs={{0,24},{4,28},{8,16},{12,20},{16,8},{20,12},{24,0},{28,4},{1,25},{... | collective-permute-start | bytes 196616 | tf_op jit(solution)/shard_map/ppermute | solution.py:370
  82.6 0.0 collective-permute-done.11.refs_2_
  82.6 0.8 collective-permute-start.16
  83.4 0.7 apply_gate.3.refs_4_
  84.1 1.6 %collective-permute-start.28 = (bf16[16,128,128]{2,1,0:T(8,128)(2,1)S(1)}, bf16[16,128,128]{2,1,0:T(8,128)(2,1)S(1)}, u32[]{:S(2)}, u32[]{:S(2)}) collective-permute-start(bf16[16,128,128]{2,1,0:T(8,128)(2,1)S(1)} %apply_gate.3.refs_4_), channel_id=1, source_target_pairs={{0,2},{1,3},{2,0},{3,1},{4,6},{5,7},{6,4},{7,5},{8,10},{9,11},{10,... | collective-permute-start | bytes 1572872 | tf_op jit(solution)/shard_map/ppermute | solution.py:370
  85.7 1.5 %collective-permute-done.14.refs_5_ = bf16[16,16,128]{2,1,0:T(8,128)(2,1)S(1)} collective-permute-done((bf16[16,16,128]{2,1,0:T(8,128)(2,1)S(1)}, bf16[16,16,128]{2,1,0:T(8,128)(2,1)S(1)}, u32[]{:S(2)}, u32[]{:S(2)}) %collective-permute-start.14) | collective-permute-done | bytes 65568 | tf_op jit(solution)/shard_map/ppermute | solution.py:370
  87.2 0.0 collective-permute-done.15.refs_6_
  87.2 2.4 %collective-permute-done.16.refs_7_ = bf16[16,16,128]{2,1,0:T(8,128)(2,1)S(1)} collective-permute-done((bf16[16,16,128]{2,1,0:T(8,128)(2,1)S(1)}, bf16[16,16,128]{2,1,0:T(8,128)(2,1)S(1)}, u32[]{:S(2)}, u32[]{:S(2)}) %collective-permute-start.16) | collective-permute-done | bytes 65568 | tf_op jit(solution)/shard_map/ppermute | solution.py:370
  89.5 0.7 apply_gate.2.refs_4_
  90.3 1.6 %collective-permute-start.18 = (bf16[16,128,128]{2,1,0:T(8,128)(2,1)S(1)}, bf16[16,128,128]{2,1,0:T(8,128)(2,1)S(1)}, u32[]{:S(2)}, u32[]{:S(2)}) collective-permute-start(bf16[16,128,128]{2,1,0:T(8,128)(2,1)S(1)} %apply_gate.2.refs_4_), channel_id=1, source_target_pairs={{0,2},{1,3},{2,0},{3,1},{4,6},{5,7},{6,4},{7,5},{8,10},{9,11},{10,... | collective-permute-start | bytes 1572872 | tf_op jit(solution)/shard_map/ppermute | solution.py:370
  91.8 0.0 collective-permute-start.27
  91.9 7.2 %collective-permute-done.28.refs_6_ = bf16[16,128,128]{2,1,0:T(8,128)(2,1)S(1)} collective-permute-done((bf16[16,128,128]{2,1,0:T(8,128)(2,1)S(1)}, bf16[16,128,128]{2,1,0:T(8,128)(2,1)S(1)}, u32[]{:S(2)}, u32[]{:S(2)}) %collective-permute-start.28) | collective-permute-done | bytes 524320 | tf_op jit(solution)/shard_map/ppermute | solution.py:370
  99.1 0.5 collective-permute-start.17
  99.6 7.6 %collective-permute-done.18.refs_6_ = bf16[16,128,128]{2,1,0:T(8,128)(2,1)S(1)} collective-permute-done((bf16[16,128,128]{2,1,0:T(8,128)(2,1)S(1)}, bf16[16,128,128]{2,1,0:T(8,128)(2,1)S(1)}, u32[]{:S(2)}, u32[]{:S(2)}) %collective-permute-start.18) | collective-permute-done | bytes 524320 | tf_op jit(solution)/shard_map/ppermute | solution.py:370
  107.2 0.0 collective-permute-start.19
  107.2 1.2 %mix_first.1.refs_8_ = f32[8,256,256]{2,1,0:T(8,128)S(1)} custom-call(bf16[256,256]{1,0:T(8,128)(2,1)S(1)} %get-tuple-element.37.refs_15_.refs_0_, bf16[256,256]{1,0:T(8,128)(2,1)S(1)} %collective-permute-done.refs_16_.refs_1_, bf16[256,256]{1,0:T(8,128)(2,1)S(1)} %collective-permute-done.1.refs_17_.refs_2_, ...), custom_call_target="tpu_custom_call" | custom-call | flops 536870912 | bytes 4194304 | tf_op jit(solution)/shard_map/mix_first/pallas_call | solution.py:329
  108.4 0.7 collective-permute-done.19.refs_7_
  109.1 2.1 %mix_last.1 = bf16[2048,256]{1,0:T(8,128)(2,1)} custom-call(bf16[256,256]{1,0:T(8,128)(2,1)S(1)} %get-tuple-element.37.refs_15_.refs_0_, bf16[256,256]{1,0:T(8,128)(2,1)S(1)} %collective-permute-done.refs_16_.refs_1_, bf16[256,256]{1,0:T(8,128)(2,1)S(1)} %collective-permute-done.1.refs_17_.refs_2_, ...), custom_call_target="tpu_custom_call" | custom-call | flops 536870912 | bytes 6291456 | tf_op jit(solution)/shard_map/mix_last/pallas_call | solution.py:357
  (36 shorter events, 0.1 us)
Async XLA Ops:
  0.0 1.2 %copy-start.1 = (bf16[2048,256]{1,0:T(8,128)(2,1)S(1)}, bf16[2048,256]{1,0:T(8,128)(2,1)}, u32[]{:S(2)}) copy-start(bf16[2048,256]{1,0:T(8,128)(2,1)} %f_ref.1) | copy-start | bytes 3145732
  1.2 9.1 %copy-start.7 = (bf16[256,1024]{1,0:T(8,128)(2,1)S(1)}, bf16[256,1024]{1,0:T(8,128)(2,1)}, u32[]{:S(2)}) copy-start(bf16[256,1024]{1,0:T(8,128)(2,1)} %w_ref.1) | copy-start | bytes 1572868
  3.1 45.7 %all-to-all-start = ((bf16[8,32,16,128]{3,2,1,0:T(8,128)(2,1)}), bf16[8,32,16,128]{3,2,1,0:T(8,128)(2,1)S(1)}, u32[]{:S(2)}, u32[]{:S(2)}) async-start(bf16[8,32,16,128]{3,2,1,0:T(8,128)(2,1)} %filter_blocks.1._), calls=%async_computation | async-start | bytes 2097152 | tf_op jit(solution)/shard_map/all_to_all | solution.py:384
  10.6 13.8 %collective-permute-start = (bf16[256,256]{1,0:T(8,128)(2,1)S(1)}, bf16[256,256]{1,0:T(8,128)(2,1)S(1)}, u32[]{:S(2)}, u32[]{:S(2)}) collective-permute-start(bf16[256,256]{1,0:T(8,128)(2,1)S(1)} %get-tuple-element.38), channel_id=1, source_target_pairs={{0,1},{1,0},{2,3},{3,2},{4,5},{5,4},{6,7},{7,6},{8,9},{9,8},{10,11... | collective-permute-start | bytes 393224 | tf_op jit(solution)/shard_map/ppermute | solution.py:370
  10.7 13.8 %collective-permute-start.1 = (bf16[256,256]{1,0:T(8,128)(2,1)S(1)}, bf16[256,256]{1,0:T(8,128)(2,1)S(1)}, u32[]{:S(2)}, u32[]{:S(2)}) collective-permute-start(bf16[256,256]{1,0:T(8,128)(2,1)S(1)} %get-tuple-element.39), channel_id=1, source_target_pairs={{0,2},{1,3},{2,0},{3,1},{4,6},{5,7},{6,4},{7,5},{8,10},{9,11},{10,... | collective-permute-start | bytes 393224 | tf_op jit(solution)/shard_map/ppermute | solution.py:370
  12.2 15.1 %collective-permute-start.2 = (bf16[256,256]{1,0:T(8,128)(2,1)S(1)}, bf16[256,256]{1,0:T(8,128)(2,1)S(1)}, u32[]{:S(2)}, u32[]{:S(2)}) collective-permute-start(bf16[256,256]{1,0:T(8,128)(2,1)S(1)} %get-tuple-element.40), channel_id=1, source_target_pairs={{0,3},{1,2},{2,1},{3,0},{4,7},{5,6},{6,5},{7,4},{8,11},{9,10},{10,... | collective-permute-start | bytes 393224 | tf_op jit(solution)/shard_map/ppermute | solution.py:370
  12.5 36.3 %copy-start = (bf16[256,256]{1,0:T(8,128)(2,1)S(1)}, bf16[256,256]{1,0:T(8,128)(2,1)}, u32[]{:S(2)}) copy-start(bf16[256,256]{1,0:T(8,128)(2,1)} %constant.19.b_fwd.refs_10_) | copy-start | bytes 393220
  12.5 36.3 %copy-start.2 = (bf16[256,128]{1,0:T(8,128)(2,1)S(1)}, bf16[256,128]{1,0:T(8,128)(2,1)}, u32[]{:S(2)}) copy-start(bf16[256,128]{1,0:T(8,128)(2,1)} %constant.18.a_fwd.refs_9_) | copy-start | bytes 196612
  12.5 36.3 %copy-start.3 = (f32[128,128]{1,0:T(8,128)S(1)}, f32[128,128]{1,0:T(8,128)}, u32[]{:S(2)}) copy-start(f32[128,128]{1,0:T(8,128)} %constant.17.clone.ts_ref.refs_14_) | copy-start | bytes 196612
  12.5 36.3 %copy-start.4 = (f32[128,128]{1,0:T(8,128)S(1)}, f32[128,128]{1,0:T(8,128)}, u32[]{:S(2)}) copy-start(f32[128,128]{1,0:T(8,128)} %constant.16.clone.tc_ref.refs_13_) | copy-start | bytes 196612
  20.8 34.1 %copy-start.5 = (bf16[256,256]{1,0:T(8,128)(2,1)S(1)}, bf16[256,256]{1,0:T(8,128)(2,1)}, u32[]{:S(2)}) copy-start(bf16[256,256]{1,0:T(8,128)(2,1)} %constant.20.refs_11_) | copy-start | bytes 393220
  20.8 34.1 %copy-start.6 = (bf16[32,16,128]{2,1,0:T(8,128)(2,1)S(1)}, bf16[32,16,128]{2,1,0:T(8,128)(2,1)}, u32[]{:S(2)}) copy-start(bf16[32,16,128]{2,1,0:T(8,128)(2,1)} %get-tuple-element.41.refs_0_) | copy-start | bytes 393220
  20.8 34.1 %copy-start.12 = (bf16[128,256]{1,0:T(8,128)(2,1)S(1)}, bf16[128,256]{1,0:T(8,128)(2,1)}, u32[]{:S(2)}) copy-start(bf16[128,256]{1,0:T(8,128)(2,1)} %constant.21.refs_12_) | copy-start | bytes 196612
  20.8 8.2 %collective-permute-start.3 = (bf16[32,16,128]{2,1,0:T(8,128)(2,1)}, bf16[32,16,128]{2,1,0:T(8,128)(2,1)S(1)}, u32[]{:S(2)}, u32[]{:S(2)}) collective-permute-start(bf16[32,16,128]{2,1,0:T(8,128)(2,1)} %get-tuple-element.42), channel_id=1, source_target_pairs={{0,4},{4,0},{8,12},{12,8},{16,20},{20,16},{24,28},{28,24},{1,5},{5... | collective-permute-start | bytes 393224 | tf_op jit(solution)/shard_map/ppermute | solution.py:370
  22.9 10.5 %collective-permute-start.4 = (bf16[32,16,128]{2,1,0:T(8,128)(2,1)}, bf16[32,16,128]{2,1,0:T(8,128)(2,1)S(1)}, u32[]{:S(2)}, u32[]{:S(2)}) collective-permute-start(bf16[32,16,128]{2,1,0:T(8,128)(2,1)} %get-tuple-element.43), channel_id=1, source_target_pairs={{0,8},{4,12},{8,0},{12,4},{16,24},{20,28},{24,16},{28,20},{1,9},{5... | collective-permute-start | bytes 393224 | tf_op jit(solution)/shard_map/ppermute | solution.py:370
  24.4 25.9 %collective-permute-start.5 = (bf16[32,16,128]{2,1,0:T(8,128)(2,1)}, bf16[32,16,128]{2,1,0:T(8,128)(2,1)S(1)}, u32[]{:S(2)}, u32[]{:S(2)}) collective-permute-start(bf16[32,16,128]{2,1,0:T(8,128)(2,1)} %get-tuple-element.44), channel_id=1, source_target_pairs={{0,12},{4,8},{8,4},{12,0},{16,28},{20,24},{24,20},{28,16},{1,13},{... | collective-permute-start | bytes 393224 | tf_op jit(solution)/shard_map/ppermute | solution.py:370
  24.5 27.2 %collective-permute-start.6 = (bf16[32,16,128]{2,1,0:T(8,128)(2,1)}, bf16[32,16,128]{2,1,0:T(8,128)(2,1)S(1)}, u32[]{:S(2)}, u32[]{:S(2)}) collective-permute-start(bf16[32,16,128]{2,1,0:T(8,128)(2,1)} %get-tuple-element.45), channel_id=1, source_target_pairs={{0,16},{4,20},{8,24},{12,28},{16,0},{20,4},{24,8},{28,12},{1,17},{... | collective-permute-start | bytes 393224 | tf_op jit(solution)/shard_map/ppermute | solution.py:370
  27.3 27.6 %collective-permute-start.7 = (bf16[32,16,128]{2,1,0:T(8,128)(2,1)}, bf16[32,16,128]{2,1,0:T(8,128)(2,1)S(1)}, u32[]{:S(2)}, u32[]{:S(2)}) collective-permute-start(bf16[32,16,128]{2,1,0:T(8,128)(2,1)} %get-tuple-element.46), channel_id=1, source_target_pairs={{0,20},{4,16},{8,28},{12,24},{16,4},{20,0},{24,12},{28,8},{1,21},{... | collective-permute-start | bytes 393224 | tf_op jit(solution)/shard_map/ppermute | solution.py:370
  29.0 25.9 %collective-permute-start.8 = (bf16[32,16,128]{2,1,0:T(8,128)(2,1)}, bf16[32,16,128]{2,1,0:T(8,128)(2,1)S(1)}, u32[]{:S(2)}, u32[]{:S(2)}) collective-permute-start(bf16[32,16,128]{2,1,0:T(8,128)(2,1)} %get-tuple-element.47), channel_id=1, source_target_pairs={{0,24},{4,28},{8,16},{12,20},{16,8},{20,12},{24,0},{28,4},{1,25},{... | collective-permute-start | bytes 393224 | tf_op jit(solution)/shard_map/ppermute | solution.py:370
  33.5 21.4 %collective-permute-start.9 = (bf16[32,16,128]{2,1,0:T(8,128)(2,1)}, bf16[32,16,128]{2,1,0:T(8,128)(2,1)S(1)}, u32[]{:S(2)}, u32[]{:S(2)}) collective-permute-start(bf16[32,16,128]{2,1,0:T(8,128)(2,1)} %get-tuple-element.48), channel_id=1, source_target_pairs={{0,28},{4,24},{8,20},{12,16},{16,12},{20,8},{24,4},{28,0},{1,29},{... | collective-permute-start | bytes 393224 | tf_op jit(solution)/shard_map/ppermute | solution.py:370
  56.3 27.1 %copy-start.10 = (bf16[16,128,128]{2,1,0:T(8,128)(2,1)S(1)}, bf16[16,128,128]{2,1,0:T(8,128)(2,1)}, u32[]{:S(2)}) copy-start(bf16[16,128,128]{2,1,0:T(8,128)(2,1)} %get-tuple-element.67.refs_8_) | copy-start | bytes 1572868
  56.4 27.0 %copy-start.11 = (bf16[16,128,128]{2,1,0:T(8,128)(2,1)S(1)}, bf16[16,128,128]{2,1,0:T(8,128)(2,1)}, u32[]{:S(2)}) copy-start(bf16[16,128,128]{2,1,0:T(8,128)(2,1)} %get-tuple-element.68.refs_9_) | copy-start | bytes 1572868
  56.4 27.0 %copy-start.13 = (f32[256]{0:T(256)S(1)}, f32[256]{0:T(256)}, u32[]{:S(2)}) copy-start(f32[256]{0:T(256)} %param.14) | copy-start | bytes 3076
  56.4 11.1 %collective-permute-start.20 = (bf16[16,16,128]{2,1,0:T(8,128)(2,1)S(1)}, bf16[16,16,128]{2,1,0:T(8,128)(2,1)S(1)}, u32[]{:S(2)}, u32[]{:S(2)}) collective-permute-start(bf16[16,16,128]{2,1,0:T(8,128)(2,1)S(1)} %get-tuple-element.60), channel_id=1, source_target_pairs={{0,4},{4,0},{8,12},{12,8},{16,20},{20,16},{24,28},{28,24},{1,5},{5... | collective-permute-start | bytes 196616 | tf_op jit(solution)/shard_map/ppermute | solution.py:370
  57.5 11.5 %collective-permute-start.21 = (bf16[16,16,128]{2,1,0:T(8,128)(2,1)S(1)}, bf16[16,16,128]{2,1,0:T(8,128)(2,1)S(1)}, u32[]{:S(2)}, u32[]{:S(2)}) collective-permute-start(bf16[16,16,128]{2,1,0:T(8,128)(2,1)S(1)} %get-tuple-element.61), channel_id=1, source_target_pairs={{0,8},{4,12},{8,0},{12,4},{16,24},{20,28},{24,16},{28,20},{1,9},{5... | collective-permute-start | bytes 196616 | tf_op jit(solution)/shard_map/ppermute | solution.py:370
  62.2 9.9 %collective-permute-start.22 = (bf16[16,16,128]{2,1,0:T(8,128)(2,1)S(1)}, bf16[16,16,128]{2,1,0:T(8,128)(2,1)S(1)}, u32[]{:S(2)}, u32[]{:S(2)}) collective-permute-start(bf16[16,16,128]{2,1,0:T(8,128)(2,1)S(1)} %get-tuple-element.62), channel_id=1, source_target_pairs={{0,12},{4,8},{8,4},{12,0},{16,28},{20,24},{24,20},{28,16},{1,13},{... | collective-permute-start | bytes 196616 | tf_op jit(solution)/shard_map/ppermute | solution.py:370
  63.0 9.8 %collective-permute-start.23 = (bf16[16,16,128]{2,1,0:T(8,128)(2,1)S(1)}, bf16[16,16,128]{2,1,0:T(8,128)(2,1)S(1)}, u32[]{:S(2)}, u32[]{:S(2)}) collective-permute-start(bf16[16,16,128]{2,1,0:T(8,128)(2,1)S(1)} %get-tuple-element.63), channel_id=1, source_target_pairs={{0,16},{4,20},{8,24},{12,28},{16,0},{20,4},{24,8},{28,12},{1,17},{... | collective-permute-start | bytes 196616 | tf_op jit(solution)/shard_map/ppermute | solution.py:370
  65.0 8.0 %collective-permute-start.24 = (bf16[16,16,128]{2,1,0:T(8,128)(2,1)S(1)}, bf16[16,16,128]{2,1,0:T(8,128)(2,1)S(1)}, u32[]{:S(2)}, u32[]{:S(2)}) collective-permute-start(bf16[16,16,128]{2,1,0:T(8,128)(2,1)S(1)} %get-tuple-element.64), channel_id=1, source_target_pairs={{0,20},{4,16},{8,28},{12,24},{16,4},{20,0},{24,12},{28,8},{1,21},{... | collective-permute-start | bytes 196616 | tf_op jit(solution)/shard_map/ppermute | solution.py:370
  66.0 23.5 %copy-start.8 = (bf16[16,128,128]{2,1,0:T(8,128)(2,1)S(1)}, bf16[16,128,128]{2,1,0:T(8,128)(2,1)}, u32[]{:S(2)}) copy-start(bf16[16,128,128]{2,1,0:T(8,128)(2,1)} %get-tuple-element.58.refs_8_) | copy-start | bytes 1572868
  66.0 23.5 %copy-start.9 = (bf16[16,128,128]{2,1,0:T(8,128)(2,1)S(1)}, bf16[16,128,128]{2,1,0:T(8,128)(2,1)}, u32[]{:S(2)}) copy-start(bf16[16,128,128]{2,1,0:T(8,128)(2,1)} %get-tuple-element.59.refs_9_) | copy-start | bytes 1572868
  67.4 8.2 %collective-permute-start.25 = (bf16[16,16,128]{2,1,0:T(8,128)(2,1)S(1)}, bf16[16,16,128]{2,1,0:T(8,128)(2,1)S(1)}, u32[]{:S(2)}, u32[]{:S(2)}) collective-permute-start(bf16[16,16,128]{2,1,0:T(8,128)(2,1)S(1)} %get-tuple-element.65), channel_id=1, source_target_pairs={{0,24},{4,28},{8,16},{12,20},{16,8},{20,12},{24,0},{28,4},{1,25},{... | collective-permute-start | bytes 196616 | tf_op jit(solution)/shard_map/ppermute | solution.py:370
  69.0 9.0 %collective-permute-start.26 = (bf16[16,16,128]{2,1,0:T(8,128)(2,1)S(1)}, bf16[16,16,128]{2,1,0:T(8,128)(2,1)S(1)}, u32[]{:S(2)}, u32[]{:S(2)}) collective-permute-start(bf16[16,16,128]{2,1,0:T(8,128)(2,1)S(1)} %get-tuple-element.66), channel_id=1, source_target_pairs={{0,28},{4,24},{8,20},{12,16},{16,12},{20,8},{24,4},{28,0},{1,29},{... | collective-permute-start | bytes 196616 | tf_op jit(solution)/shard_map/ppermute | solution.py:370
  72.1 8.3 %collective-permute-start.10 = (bf16[16,16,128]{2,1,0:T(8,128)(2,1)S(1)}, bf16[16,16,128]{2,1,0:T(8,128)(2,1)S(1)}, u32[]{:S(2)}, u32[]{:S(2)}) collective-permute-start(bf16[16,16,128]{2,1,0:T(8,128)(2,1)S(1)} %get-tuple-element.51), channel_id=1, source_target_pairs={{0,4},{4,0},{8,12},{12,8},{16,20},{20,16},{24,28},{28,24},{1,5},{5... | collective-permute-start | bytes 196616 | tf_op jit(solution)/shard_map/ppermute | solution.py:370
  72.8 9.8 %collective-permute-start.11 = (bf16[16,16,128]{2,1,0:T(8,128)(2,1)S(1)}, bf16[16,16,128]{2,1,0:T(8,128)(2,1)S(1)}, u32[]{:S(2)}, u32[]{:S(2)}) collective-permute-start(bf16[16,16,128]{2,1,0:T(8,128)(2,1)S(1)} %get-tuple-element.52), channel_id=1, source_target_pairs={{0,8},{4,12},{8,0},{12,4},{16,24},{20,28},{24,16},{28,20},{1,9},{5... | collective-permute-start | bytes 196616 | tf_op jit(solution)/shard_map/ppermute | solution.py:370
  73.0 11.1 %collective-permute-start.12 = (bf16[16,16,128]{2,1,0:T(8,128)(2,1)S(1)}, bf16[16,16,128]{2,1,0:T(8,128)(2,1)S(1)}, u32[]{:S(2)}, u32[]{:S(2)}) collective-permute-start(bf16[16,16,128]{2,1,0:T(8,128)(2,1)S(1)} %get-tuple-element.53), channel_id=1, source_target_pairs={{0,12},{4,8},{8,4},{12,0},{16,28},{20,24},{24,20},{28,16},{1,13},{... | collective-permute-start | bytes 196616 | tf_op jit(solution)/shard_map/ppermute | solution.py:370
  75.6 10.0 %collective-permute-start.13 = (bf16[16,16,128]{2,1,0:T(8,128)(2,1)S(1)}, bf16[16,16,128]{2,1,0:T(8,128)(2,1)S(1)}, u32[]{:S(2)}, u32[]{:S(2)}) collective-permute-start(bf16[16,16,128]{2,1,0:T(8,128)(2,1)S(1)} %get-tuple-element.54), channel_id=1, source_target_pairs={{0,16},{4,20},{8,24},{12,28},{16,0},{20,4},{24,8},{28,12},{1,17},{... | collective-permute-start | bytes 196616 | tf_op jit(solution)/shard_map/ppermute | solution.py:370
  78.0 9.2 %collective-permute-start.14 = (bf16[16,16,128]{2,1,0:T(8,128)(2,1)S(1)}, bf16[16,16,128]{2,1,0:T(8,128)(2,1)S(1)}, u32[]{:S(2)}, u32[]{:S(2)}) collective-permute-start(bf16[16,16,128]{2,1,0:T(8,128)(2,1)S(1)} %get-tuple-element.55), channel_id=1, source_target_pairs={{0,20},{4,16},{8,28},{12,24},{16,4},{20,0},{24,12},{28,8},{1,21},{... | collective-permute-start | bytes 196616 | tf_op jit(solution)/shard_map/ppermute | solution.py:370
  80.5 6.7 %collective-permute-start.15 = (bf16[16,16,128]{2,1,0:T(8,128)(2,1)S(1)}, bf16[16,16,128]{2,1,0:T(8,128)(2,1)S(1)}, u32[]{:S(2)}, u32[]{:S(2)}) collective-permute-start(bf16[16,16,128]{2,1,0:T(8,128)(2,1)S(1)} %get-tuple-element.56), channel_id=1, source_target_pairs={{0,24},{4,28},{8,16},{12,20},{16,8},{20,12},{24,0},{28,4},{1,25},{... | collective-permute-start | bytes 196616 | tf_op jit(solution)/shard_map/ppermute | solution.py:370
  82.6 7.0 %collective-permute-start.16 = (bf16[16,16,128]{2,1,0:T(8,128)(2,1)S(1)}, bf16[16,16,128]{2,1,0:T(8,128)(2,1)S(1)}, u32[]{:S(2)}, u32[]{:S(2)}) collective-permute-start(bf16[16,16,128]{2,1,0:T(8,128)(2,1)S(1)} %get-tuple-element.57), channel_id=1, source_target_pairs={{0,28},{4,24},{8,20},{12,16},{16,12},{20,8},{24,4},{28,0},{1,29},{... | collective-permute-start | bytes 196616 | tf_op jit(solution)/shard_map/ppermute | solution.py:370
  84.1 14.9 %collective-permute-start.28 = (bf16[16,128,128]{2,1,0:T(8,128)(2,1)S(1)}, bf16[16,128,128]{2,1,0:T(8,128)(2,1)S(1)}, u32[]{:S(2)}, u32[]{:S(2)}) collective-permute-start(bf16[16,128,128]{2,1,0:T(8,128)(2,1)S(1)} %apply_gate.3.refs_4_), channel_id=1, source_target_pairs={{0,2},{1,3},{2,0},{3,1},{4,6},{5,7},{6,4},{7,5},{8,10},{9,11},{10,... | collective-permute-start | bytes 1572872 | tf_op jit(solution)/shard_map/ppermute | solution.py:370
  90.3 16.9 %collective-permute-start.18 = (bf16[16,128,128]{2,1,0:T(8,128)(2,1)S(1)}, bf16[16,128,128]{2,1,0:T(8,128)(2,1)S(1)}, u32[]{:S(2)}, u32[]{:S(2)}) collective-permute-start(bf16[16,128,128]{2,1,0:T(8,128)(2,1)S(1)} %apply_gate.2.refs_4_), channel_id=1, source_target_pairs={{0,2},{1,3},{2,0},{3,1},{4,6},{5,7},{6,4},{7,5},{8,10},{9,11},{10,... | collective-permute-start | bytes 1572872 | tf_op jit(solution)/shard_map/ppermute | solution.py:370
  91.8 15.3 %collective-permute-start.27 = (bf16[16,128,128]{2,1,0:T(8,128)(2,1)S(1)}, bf16[16,128,128]{2,1,0:T(8,128)(2,1)S(1)}, u32[]{:S(2)}, u32[]{:S(2)}) collective-permute-start(bf16[16,128,128]{2,1,0:T(8,128)(2,1)S(1)} %apply_gate.3.refs_4_), channel_id=1, source_target_pairs={{0,1},{1,0},{2,3},{3,2},{4,5},{5,4},{6,7},{7,6},{8,9},{9,8},{10,11... | collective-permute-start | bytes 1572872 | tf_op jit(solution)/shard_map/ppermute | solution.py:370
  99.1 8.1 %collective-permute-start.29 = (bf16[16,128,128]{2,1,0:T(8,128)(2,1)S(1)}, bf16[16,128,128]{2,1,0:T(8,128)(2,1)S(1)}, u32[]{:S(2)}, u32[]{:S(2)}) collective-permute-start(bf16[16,128,128]{2,1,0:T(8,128)(2,1)S(1)} %collective-permute-done.28.refs_6_), channel_id=1, source_target_pairs={{0,1},{1,0},{2,3},{3,2},{4,5},{5,4},{6,7},{7,6},{8,9},{9,8},{10,11... | collective-permute-start | bytes 1572872 | tf_op jit(solution)/shard_map/ppermute | solution.py:370
  99.1 9.4 %collective-permute-start.17 = (bf16[16,128,128]{2,1,0:T(8,128)(2,1)S(1)}, bf16[16,128,128]{2,1,0:T(8,128)(2,1)S(1)}, u32[]{:S(2)}, u32[]{:S(2)}) collective-permute-start(bf16[16,128,128]{2,1,0:T(8,128)(2,1)S(1)} %apply_gate.2.refs_4_), channel_id=1, source_target_pairs={{0,1},{1,0},{2,3},{3,2},{4,5},{5,4},{6,7},{7,6},{8,9},{9,8},{10,11... | collective-permute-start | bytes 1572872 | tf_op jit(solution)/shard_map/ppermute | solution.py:370
  107.2 1.9 %collective-permute-start.19 = (bf16[16,128,128]{2,1,0:T(8,128)(2,1)S(1)}, bf16[16,128,128]{2,1,0:T(8,128)(2,1)S(1)}, u32[]{:S(2)}, u32[]{:S(2)}) collective-permute-start(bf16[16,128,128]{2,1,0:T(8,128)(2,1)S(1)} %collective-permute-done.18.refs_6_), channel_id=1, source_target_pairs={{0,1},{1,0},{2,3},{3,2},{4,5},{5,4},{6,7},{7,6},{8,9},{9,8},{10,11... | collective-permute-start | bytes 1572872 | tf_op jit(solution)/shard_map/ppermute | solution.py:370

commit v2 on v1

v2 whole, which is shorter than its diff:
```python
import functools
import math

import jax
import jax.numpy as jnp
import numpy as np
from jax import lax
from jax.experimental import pallas as pl
from jax.experimental.pallas import tpu as pltpu
from jax.sharding import PartitionSpec as P

LANES = 128
GROUPS = ((0,1),(4,5,2,3),(6,7))
NEAR = (1, 2, 3)
SMALL = 16
LANES = 128
SMALL = 16
BF16 = jnp.bfloat16
F32 = jnp.float32


def dot(left, right):
    return jnp.dot(left, right, preferred_element_type=F32)


def cost(flops, data):
    return pl.CostEstimate(flops=int(flops), bytes_accessed=int(data), transcendentals=0)


def params(mib):
    return pltpu.CompilerParams(vmem_limit_bytes=mib * 1024 * 1024)


def tables(rows):
    total = rows * LANES
    r = np.arange(rows, dtype=np.float64)
    l = np.arange(LANES, dtype=np.float64)
    first = 2 * np.pi * np.outer(r + 0.25, r) / rows
    twist = 2 * np.pi * np.outer(r + 0.25, l) / total
    second = 2 * np.pi * np.outer(l, l) / LANES
    a_fwd = np.concatenate([np.cos(first), -np.sin(first)], 0)
    a_inv = np.concatenate([np.cos(first).T, -np.sin(first).T], 1) / rows
    c2, s2 = np.cos(second), np.sin(second)
    b_fwd = np.block([[c2, -s2], [s2, c2]])
    b_inv = np.block([[c2, s2], [-s2, c2]]) / LANES
    as_bf = lambda v: jnp.asarray(v.astype(np.float32)).astype(BF16)
    as_f = lambda v: jnp.asarray(v.astype(np.float32))
    return (as_bf(a_fwd), as_bf(b_fwd), as_bf(b_inv), as_bf(a_inv), as_f(np.cos(twist)), as_f(np.sin(twist)))


def seq_peer(step):
    return lax.bitwise_xor(lax.axis_index("seq"), jnp.int32(step))


def block_shapes(seq, cpc, rows):
    return [jax.ShapeDtypeStruct((cpc, rows, LANES), BF16)] * seq


def whole(shape):
    return pl.BlockSpec(tuple(shape), lambda i: (0,) * len(shape))


def tie(value, *after):
    return lax.optimization_barrier((value, *after))[0]


def cut_block(turned, peer, cpd, rows):
    first = pl.multiple_of(peer * (cpd * rows), 8)
    return turned[pl.ds(first, cpd * rows), :].reshape(cpd, rows, LANES).astype(BF16)


def filter_kernel(seq, f_ref, out, turned):
    frames, chans = f_ref.shape
    rows = frames // LANES
    for r in range(rows):
        turned[pl.ds(r, chans, stride=rows), :] = f_ref[pl.ds(r * LANES, LANES), :].astype(F32).T
    for j in range(seq):
        out[j] = cut_block(turned, j, chans // seq, rows)


def prepare_filters(filters, seq):
    frames, chans = filters.shape
    rows = frames // LANES
    return pl.pallas_call(
        functools.partial(filter_kernel, seq),
        out_shape=jax.ShapeDtypeStruct((seq, chans // seq, rows, LANES), BF16),
        scratch_shapes=[pltpu.VMEM((chans * rows, LANES), F32)],
        compiler_params=params(12),
        cost_estimate=cost(0, 8 * frames * chans),
        name="filter_blocks",
    )(filters)


def project_kernel(seq, x_ref, w_ref, _, gates, *refs):
    sends, turned, turned_gate = refs[:seq], refs[seq], refs[seq + 1]
    tile = x_ref.shape[0]
    chans = w_ref.shape[2]
    step = pl.program_id(0)
    rows_here = tile // LANES
    rows = turned.shape[0] // chans
    x = x_ref[...]
    gate = dot(x, w_ref[0]).astype(BF16).astype(F32)
    key = dot(x, w_ref[1]).astype(BF16).astype(F32)
    value = dot(x, w_ref[2]).astype(BF16).astype(F32)
    signal = key * value
    for r in range(rows_here):
        here = slice(r * LANES, (r + 1) * LANES)
        place = pl.ds(step * rows_here + r, chans, stride=rows)
        turned[place, :] = signal[here].T
        turned_gate[place, :] = gate[here].T

    @pl.when(step == pl.num_programs(0) - 1)
    def _():
        for d in range(seq):
            peer = seq_peer(d)
            sends[d][...] = cut_block(turned, peer, chans // seq, rows)
            gates[d] = cut_block(turned_gate, peer, chans // seq, rows)


def project(frames_in, w_in, ready, seq):
    frames, width = frames_in.shape
    chans = w_in.shape[2]
    rows = frames // LANES
    tile = 512
    cpd = chans // seq
    out_shape = [jax.ShapeDtypeStruct((seq, cpd, rows, LANES), BF16)]
    out_shape += block_shapes(seq, cpd, rows)
    gates, *sends = pl.pallas_call(
        functools.partial(project_kernel, seq),
        grid=(frames // tile,),
        in_specs=[
            pl.BlockSpec((tile, width), lambda i: (i, 0)),
            whole(w_in.shape),
            pl.BlockSpec(memory_space=pl.ANY),
        ],
        out_specs=[whole(v.shape) for v in out_shape],
        out_shape=out_shape,
        scratch_shapes=[pltpu.VMEM((chans * rows, LANES), F32)] * 2,
        compiler_params=params(58),
        cost_estimate=cost(6 * frames * width * chans, 16 * 1024 * 1024),
        name="project",
    )(frames_in, w_in, ready)
    return gates, sends


def gather_rows(grid, blocks):
    rows = blocks[0].shape[1]
    for d, block in enumerate(blocks):
        place = pl.ds(pl.multiple_of(seq_peer(d) * rows, 16), rows)
        grid[:, place, :] = block[...]


def twisted(outer, tc, ts):
    full = outer.shape[0] // 2
    parts = []
    for side in (slice(0, LANES), slice(LANES, 2 * LANES)):
        re, im = outer[:full, side], outer[full:, side]
        parts.append(jnp.concatenate([re * tc + im * ts, im * tc - re * ts], 1).astype(BF16))
    return jnp.concatenate(parts, 0)


def forward_pair(grid, c, consts):
    a_fwd, b_fwd, tc, ts = consts
    outer = dot(a_fwd[...], jnp.concatenate([grid[c], grid[c + 1]], 1))
    return dot(twisted(outer, tc, ts), b_fwd[...])


def spectra_kernel(f_ref, a_fwd, b_fwd, tc_ref, ts_ref, out, grid):
    seq, _, rows, _ = f_ref.shape
    chans, full, _ = out.shape
    for j in range(seq):
        grid[:, j * rows : (j + 1) * rows, :] = f_ref[j]
    tc, ts = tc_ref[...], ts_ref[...]
    for c in range(0, chans, 2):
        spec = forward_pair(grid, c, (a_fwd, b_fwd, tc, ts))
        out[c] = spec[:full]
        out[c + 1] = spec[full:]


def filter_spectra(filt, consts):
    a_fwd, b_fwd, _, _, tc, ts = consts
    seq, chans, rows, _ = filt.shape
    full = rows * seq
    return pl.pallas_call(
        spectra_kernel,
        out_shape=jax.ShapeDtypeStruct((chans, full, 2 * LANES), F32),
        scratch_shapes=[pltpu.VMEM((chans, full, LANES), BF16)],
        compiler_params=params(SMALL),
        cost_estimate=cost(chans * full * LANES * LANES * 8, chans * full * LANES * 10),
        name="filter_spectra",
    )(filt, a_fwd, b_fwd, tc, ts)


def conv_kernel(seq, skipped, *refs):
    s_refs, rest = refs[:seq], refs[seq:]
    spec_ref, a_fwd, b_fwd, b_inv, a_inv, tc_ref, ts_ref = rest[:7]
    y_refs = rest[7 + skipped : 7 + skipped + seq]
    grid, grid_y, work = rest[7 + skipped + seq :]
    cpc, rows, _ = y_refs[0].shape
    full = rows * seq
    gather_rows(grid, s_refs)
    tc, ts = tc_ref[...], ts_ref[...]
    pairs = [(c, pl.ds(c * full, 2 * full)) for c in range(0, cpc, 2)]
    for c, here in pairs:
        outer = dot(a_fwd[...], jnp.concatenate([grid[c], grid[c + 1]], 1))
        work[here, :] = twisted(outer, tc, ts)
    for c, here in pairs:
        mine = dot(work[here, :], b_fwd[...])
        other = spec_ref[pl.ds(c, 2)].reshape(2 * full, 2 * LANES)
        sr, si, fr, fi = mine[:, :LANES], mine[:, LANES:], other[:, :LANES], other[:, LANES:]
        work[here, :] = jnp.concatenate([sr * fr - si * fi, sr * fi + si * fr], 1).astype(BF16)
    for c, here in pairs:
        inner = dot(work[here, :], b_inv[...])
        for i in range(2):
            re, im = inner[i * full : (i + 1) * full, :LANES], inner[i * full : (i + 1) * full, LANES:]
            back = jnp.concatenate([re * tc - im * ts, im * tc + re * ts], 1)
            work[pl.ds((c + i) * full, full), :] = back.astype(BF16)
    for c, here in pairs:
        back = work[here, :]
        re = jnp.concatenate([back[:full, :LANES], back[full:, :LANES]], 1)
        im = jnp.concatenate([back[:full, LANES:], back[full:, LANES:]], 1)
        y = dot(a_inv[...], jnp.concatenate([re, im], 0)).astype(BF16)
        grid_y[c] = y[:, :LANES]
        grid_y[c + 1] = y[:, LANES:]
    for d in range(seq):
        place = pl.ds(pl.multiple_of(seq_peer(d) * rows, 16), rows)
        y_refs[d][...] = grid_y[:, place, :]


def convolve(sig, spec, consts, ready):
    seq = len(sig)
    cpc, rows, _ = sig[0].shape
    full = rows * seq
    anywhere = [pl.BlockSpec(memory_space=pl.ANY)] * len(ready)
    ins = (*sig, spec, *consts)
    return pl.pallas_call(
        functools.partial(conv_kernel, seq, len(ready)),
        in_specs=[pl.BlockSpec(memory_space=pltpu.VMEM)] * len(ins) + anywhere,
        out_shape=block_shapes(seq, cpc, rows),
        scratch_shapes=[pltpu.VMEM((cpc, full, LANES), BF16)] * 2
        + [pltpu.VMEM((cpc * full, 2 * LANES), BF16)],
        compiler_params=params(SMALL),
        cost_estimate=cost(cpc * full * LANES * LANES * 16, cpc * full * LANES * 12),
        name="convolve",
    )(*ins, *ready)


def gate_kernel(group, gates, skips, *refs):
    n = len(group)
    y_refs, sig_refs = refs[:n], refs[n : 2 * n]
    out_ref, turned = refs[2 * n :]
    rows, chans, _ = out_ref.shape
    block = chans // n * rows
    for i, d in enumerate(group):
        inner = y_refs[i][...].astype(F32) + skips[d][:, None, :] * sig_refs[i][...].astype(F32)
        value = gates[d].astype(F32) * inner
        turned[pl.ds(i * block, block), :] = value.reshape(block, LANES)
    for r in range(rows):
        out_ref[r] = turned[pl.ds(r, chans, stride=rows), :].astype(BF16)


def apply_gate(group, y, gates, signal, skips):
    cpd, rows, _ = y[0].shape
    chans = len(group) * cpd
    return pl.pallas_call(
        functools.partial(gate_kernel, group),
        out_shape=jax.ShapeDtypeStruct((rows, chans, LANES), BF16),
        scratch_shapes=[pltpu.VMEM((chans * rows, LANES), F32)],
        compiler_params=params(SMALL),
        cost_estimate=cost(0, 10 * rows * chans * LANES),
        name="apply_gate",
    )(gates, skips, *[y[d] for d in group], *[signal[d] for d in group])


def out_weights_kernel(ways, order, w_ref, skip_ref, *refs):
    outs, skips, held, turned = refs[:ways], refs[ways], refs[ways + 1], refs[ways + 2]
    depth = w_ref.shape[1] // ways
    seq, cpd, _ = skips.shape
    held[...] = w_ref[...].astype(F32)
    turned[...] = jnp.broadcast_to(skip_ref[...], (LANES, skip_ref.shape[1])).T
    for d in range(seq):
        skips[d] = turned[pl.ds(pl.multiple_of(seq_peer(d) * cpd, 8), cpd), :]
    for d in range(ways):
        peer = lax.bitwise_xor(lax.axis_index("ch"), jnp.int32(d))
        cols = pl.ds(pl.multiple_of(peer * depth, LANES), depth)
        parts = [
            held[pl.ds(pl.multiple_of(seq_peer(e) * cpd, 8), cpd), cols] for e in order
        ]
        outs[d][...] = jnp.concatenate(parts, 0).T.astype(BF16)


def out_weights(w_out, skip_gain, ways, seq, order):
    chans, width = w_out.shape
    *weights, skips = pl.pallas_call(
        functools.partial(out_weights_kernel, ways, order),
        out_shape=[jax.ShapeDtypeStruct((width // ways, chans), BF16)] * ways
        + [jax.ShapeDtypeStruct((seq, chans // seq, LANES), F32)],
        scratch_shapes=[pltpu.VMEM((chans, width), F32), pltpu.VMEM((chans, LANES), F32)],
        compiler_params=params(SMALL),
        cost_estimate=cost(0, 4 * chans * width),
        name="out_weights",
    )(w_out, skip_gain[None, :])
    return weights, skips


def partial_mix(ways, r):
    total = None
    for w_ref, pieces in ways:
        left = jnp.concatenate([piece[r] for piece in pieces], 0)
        right = jnp.concatenate([piece[r + 1] for piece in pieces], 0)
        term = dot(w_ref[...], jnp.concatenate([left, right], 1))
        total = term if total is None else total + term
    return total


def pair_ways(refs, n):
    return [(refs[i], refs[2 + i * n : 2 + (i + 1) * n]) for i in range(2)]


def mix_early_kernel(n, *refs):
    out_ref = refs[-1]
    for r in range(0, refs[2].shape[0], 2):
        out_ref[r // 2] = partial_mix(pair_ways(refs, n), r)


def mix_early(weights, gated):
    n = len(gated[0])
    rows = gated[0][0].shape[0]
    depth, chans = weights[0].shape
    return pl.pallas_call(
        functools.partial(mix_early_kernel, n),
        out_shape=jax.ShapeDtypeStruct((rows // 2, depth, 2 * LANES), F32),
        compiler_params=params(SMALL),
        cost_estimate=cost(4 * rows * LANES * depth * chans, 4 * 1024 * 1024),
        name="mix_early",
    )(*weights, *gated[0], *gated[1])


def mix_last_kernel(n, *refs):
    before, out_ref, held, sems = refs[2 + 2 * n :]
    copies = []
    for r in range(0, refs[2].shape[0], 2):
        total = before[r // 2] + partial_mix(pair_ways(refs, n), r)
        span = pl.ds(r * LANES, 2 * LANES)
        held[span, :] = total.T.astype(BF16)
        copies.append(pltpu.make_async_copy(held.at[span], out_ref.at[span], sems.at[r // 2]))
        copies[-1].start()
    for copy in copies:
        copy.wait()


def mix_last(weights, gated, before):
    n = len(gated[0])
    rows = gated[0][0].shape[0]
    depth, chans = weights[0].shape
    out = (rows * LANES, depth)
    return pl.pallas_call(
        functools.partial(mix_last_kernel, n),
        out_shape=jax.ShapeDtypeStruct(out, BF16),
        out_specs=pl.BlockSpec(memory_space=pl.ANY),
        scratch_shapes=[pltpu.VMEM(out, BF16), pltpu.SemaphoreType.DMA((rows // 2,))],
        compiler_params=params(SMALL),
        cost_estimate=cost(4 * rows * LANES * depth * chans, 4 * 1024 * 1024),
        name="mix_last",
    )(*weights, *gated[0], *gated[1], before)


def swap(value, axis, step):
    size = lax.axis_size(axis)
    return lax.ppermute(value, axis, [(i, i ^ step) for i in range(size)])


def on_device(frames_in, w_in, filters, skip_gain, w_out):
    seq, ways = lax.axis_size("seq"), lax.axis_size("ch")
    frames, width = frames_in.shape
    chans = filters.shape[1]
    cpd = chans // seq
    consts = tables(seq * frames // LANES)
    filt_sends = prepare_filters(filters, seq)
    filt = lax.all_to_all(filt_sends, "seq", split_axis=0, concat_axis=0, tiled=True)
    unit = max(seq // 8, 1)
    groups = [[d * unit + i for d in g for i in range(unit)] for g in GROUPS]
    order = [d for g in groups for d in g]
    weights, skips = out_weights(w_out, skip_gain, ways, seq, order)
    weights = [w if d == 0 else swap(w, "ch", d) for d, w in enumerate(weights)]
    gates, sends = project(frames_in, w_in.transpose(1, 0, 2), filt_sends, seq)
    sig = [s if d == 0 else swap(s, "seq", d) for d, s in enumerate(sends)]
    y = convolve(sig, filter_spectra(filt, consts), consts, [*weights, skips])
    back = {d: y[0] if d == 0 else swap(y[d], "seq", d) for d in range(seq)}
    mine = [apply_gate(g, back, gates, sends, skips) for g in groups]
    far = [swap(m, "ch", 2) for m in mine]
    near = [swap(m, "ch", 1) for m in mine]
    far = [f if f is far[-1] else tie(f, mine[-1]) for f in far]
    firsts = [swap(f, "ch", 1) for f in far[:-1]]
    total = mix_early(weights[:2], [mine, near])
    last = tie(far[-1], total, *firsts)
    return mix_last(weights[2:], [far[:-1] + [last], firsts + [swap(last, "ch", 1)]], total)


def solution(mesh):
    in_specs = (P("seq", None), P(None, None, "ch"), P("seq", "ch"), P("ch"), P("ch", None))
    out_specs = P("seq", "ch")
    return jax.shard_map(
        on_device, mesh=mesh, in_specs=in_specs, out_specs=out_specs, check_vma=False
    )
```

time: 111 us -> 105 us (0.946)
  starting transfers between devices: 53.5 us -> 42.2 us
  waiting for transfers between devices: 36.9 us -> 42.4 us
    ppermute x30 -> x26, starting transfers between devices: 46.2 us -> 34.9 us  [swap(): return lax.ppermute(value, axis, [(i, i ^ step) for i in range(size)])]
    ppermute x30 -> x26, waiting for transfers between devices: 24.2 us -> 29.7 us  [swap(): return lax.ppermute(value, axis, [(i, i ^ step) for i in range(size)])]
  transfers between devices with their start and end apart: 31 -> 27, of which waited for: 9 -> 13; matrix products, arithmetic and copies ran while one was open for 0% -> 0% of each run, Pallas kernels for 13% -> 11%
where the time goes in v2:
time: 105 us; the launch traced here: 104 us
  waiting for transfers between devices  42.4 us (40%)
  starting transfers between devices  42.2 us (40%)
  Pallas kernels  18.3 us (17%)
  local copies, waits for them, and re-layouts  1.29 us (1%)
    ppermute x26, starting transfers between devices, swap(): return lax.ppermute(value, axis, [(i, i ^ step) for i in range(size)])  34.9 us
    ppermute x26, waiting for transfers between devices, swap(): return lax.ppermute(value, axis, [(i, i ^ step) for i in range(size)])  29.7 us
    all_to_all x1, waiting for transfers between devices, on_device(): lax.all_to_all(filt_sends, 'seq', split_axis=0, concat_axis=0, tiled=True)  12.6 us
    pallas_call x1, Pallas kernels, project(): pl.pallas_call(functools.partial(project_kernel, seq), grid=(frames // ti...  8.77 us
    all_to_all x1, starting transfers between devices, on_device(): lax.all_to_all(filt_sends, 'seq', split_axis=0, concat_axis=0, tiled=True)  7.28 us
    pallas_call x1, Pallas kernels, convolve(): pl.pallas_call(functools.partial(conv_kernel, seq, len(ready)), in_specs=...  2.51 us
  transfers between devices with their start and end apart: 27, of which 13 were waited for; matrix products, arithmetic and copies ran while one was open for 0% of the time, Pallas kernels for 11%

profile of v2, /device:TPU:0, one launch (start us, length us, event | category | flops | bytes accessed | tf_op | source)
XLA Modules:
  0.0 104.4 jit_solution(13986421508591695241)
XLA Ops:
  0.0 1.2 %copy-done.1 = bf16[2048,256]{1,0:T(8,128)(2,1)S(1)} copy-done((bf16[2048,256]{1,0:T(8,128)(2,1)S(1)}, bf16[2048,256]{1,0:T(8,128)(2,1)}, u32[]{:S(2)}) %copy-start.1) | copy-done | bytes 1048600
  1.2 1.9 %filter_blocks.1._ = bf16[8,32,16,128]{3,2,1,0:T(8,128)(2,1)} custom-call(bf16[2048,256]{1,0:T(8,128)(2,1)S(1)} %copy-done.1), custom_call_target="tpu_custom_call" | custom-call | bytes 4194304 | tf_op jit(solution)/shard_map/filter_blocks/pallas_call | solution.py:84
  3.1 7.3 %all-to-all-start = ((bf16[8,32,16,128]{3,2,1,0:T(8,128)(2,1)}), bf16[8,32,16,128]{3,2,1,0:T(8,128)(2,1)S(1)}, u32[]{:S(2)}, u32[]{:S(2)}) async-start(bf16[8,32,16,128]{3,2,1,0:T(8,128)(2,1)} %filter_blocks.1._), calls=%async_computation | async-start | bytes 2097152 | tf_op jit(solution)/shard_map/all_to_all | solution.py:380
  10.4 0.3 out_weights.1
  10.7 1.6 %collective-permute-start = (bf16[256,256]{1,0:T(8,128)(2,1)S(1)}, bf16[256,256]{1,0:T(8,128)(2,1)S(1)}, u32[]{:S(2)}, u32[]{:S(2)}) collective-permute-start(bf16[256,256]{1,0:T(8,128)(2,1)S(1)} %get-tuple-element.30), channel_id=1, source_target_pairs={{0,2},{1,3},{2,0},{3,1},{4,6},{5,7},{6,4},{7,5},{8,10},{9,11},{10,... | collective-permute-start | bytes 393224 | tf_op jit(solution)/shard_map/ppermute | solution.py:370
  12.2 0.0 collective-permute-start.1
  12.2 0.6 collective-permute-start.9
  12.9 8.8 %project.1 = (bf16[8,32,16,128]{3,2,1,0:T(8,128)(2,1)}, bf16[32,16,128]{2,1,0:T(8,128)(2,1)}, bf16[32,16,128]{2,1,0:T(8,128)(2,1)}, bf16[32,16,128]{2,1,0:T(8,12...) custom-call(bf16[2048,1024]{1,0:T(8,128)(2,1)} %x_ref.1, ...), custom_call_target="tpu_custom_call" | custom-call | flops 3221225472 | bytes 16777216 | tf_op jit(solution)/shard_map/project/pallas_call | solution.py:128
  21.7 2.1 %collective-permute-start.2 = (bf16[32,16,128]{2,1,0:T(8,128)(2,1)}, bf16[32,16,128]{2,1,0:T(8,128)(2,1)S(1)}, u32[]{:S(2)}, u32[]{:S(2)}) collective-permute-start(bf16[32,16,128]{2,1,0:T(8,128)(2,1)} %get-tuple-element.35.refs_3_), channel_id=1, source_target_pairs={{0,4},{4,0},{8,12},{12,8},{16,20},{20,16},{24,28},{28,24},{1,5},{5... | collective-permute-start | bytes 393224 | tf_op jit(solution)/shard_map/ppermute | solution.py:370
  23.8 1.5 %collective-permute-start.3 = (bf16[32,16,128]{2,1,0:T(8,128)(2,1)}, bf16[32,16,128]{2,1,0:T(8,128)(2,1)S(1)}, u32[]{:S(2)}, u32[]{:S(2)}) collective-permute-start(bf16[32,16,128]{2,1,0:T(8,128)(2,1)} %get-tuple-element.36.refs_6_), channel_id=1, source_target_pairs={{0,8},{4,12},{8,0},{12,4},{16,24},{20,28},{24,16},{28,20},{1,9},{5... | collective-permute-start | bytes 393224 | tf_op jit(solution)/shard_map/ppermute | solution.py:370
  25.2 0.0 collective-permute-done.refs_17_.refs_0_
  25.2 0.1 collective-permute-start.4
  25.3 0.0 collective-permute-done.1.refs_18_.refs_1_
  25.3 2.8 %collective-permute-start.5 = (bf16[32,16,128]{2,1,0:T(8,128)(2,1)}, bf16[32,16,128]{2,1,0:T(8,128)(2,1)S(1)}, u32[]{:S(2)}, u32[]{:S(2)}) collective-permute-start(bf16[32,16,128]{2,1,0:T(8,128)(2,1)} %get-tuple-element.38.refs_4_), channel_id=1, source_target_pairs={{0,16},{4,20},{8,24},{12,28},{16,0},{20,4},{24,8},{28,12},{1,17},{... | collective-permute-start | bytes 393224 | tf_op jit(solution)/shard_map/ppermute | solution.py:370
  28.1 0.0 collective-permute-done.9.refs_16_.refs_1_
  28.2 1.5 %collective-permute-start.6 = (bf16[32,16,128]{2,1,0:T(8,128)(2,1)}, bf16[32,16,128]{2,1,0:T(8,128)(2,1)S(1)}, u32[]{:S(2)}, u32[]{:S(2)}) collective-permute-start(bf16[32,16,128]{2,1,0:T(8,128)(2,1)} %get-tuple-element.39.refs_5_), channel_id=1, source_target_pairs={{0,20},{4,16},{8,28},{12,24},{16,4},{20,0},{24,12},{28,8},{1,21},{... | collective-permute-start | bytes 393224 | tf_op jit(solution)/shard_map/ppermute | solution.py:370
  29.6 0.4 collective-permute-done.2.refs_1_
  30.0 3.5 %collective-permute-start.7 = (bf16[32,16,128]{2,1,0:T(8,128)(2,1)}, bf16[32,16,128]{2,1,0:T(8,128)(2,1)S(1)}, u32[]{:S(2)}, u32[]{:S(2)}) collective-permute-start(bf16[32,16,128]{2,1,0:T(8,128)(2,1)} %get-tuple-element.40.refs_2_), channel_id=1, source_target_pairs={{0,24},{4,28},{8,16},{12,20},{16,8},{20,12},{24,0},{28,4},{1,25},{... | collective-permute-start | bytes 393224 | tf_op jit(solution)/shard_map/ppermute | solution.py:370
  33.5 0.0 collective-permute-done.3.refs_2_
  33.5 2.7 %collective-permute-start.8 = (bf16[32,16,128]{2,1,0:T(8,128)(2,1)}, bf16[32,16,128]{2,1,0:T(8,128)(2,1)S(1)}, u32[]{:S(2)}, u32[]{:S(2)}) collective-permute-start(bf16[32,16,128]{2,1,0:T(8,128)(2,1)} %get-tuple-element.41.refs_3_), channel_id=1, source_target_pairs={{0,28},{4,24},{8,20},{12,16},{16,12},{20,8},{24,4},{28,0},{1,29},{... | collective-permute-start | bytes 393224 | tf_op jit(solution)/shard_map/ppermute | solution.py:370
  36.2 12.6 %all-to-all-done.f_ref = bf16[8,32,16,128]{3,2,1,0:T(8,128)(2,1)S(1)} async-done(((bf16[8,32,16,128]{3,2,1,0:T(8,128)(2,1)}), bf16[8,32,16,128]{3,2,1,0:T(8,128)(2,1)S(1)}, u32[]{:S(2)}, u32[]{:S(2)}) %all-to-all-start) | async-done | bytes 1048608 | tf_op jit(solution)/shard_map/all_to_all | solution.py:380
  48.9 1.4 %filter_spectra.1.refs_8_ = f32[32,128,256]{2,1,0:T(8,128)S(1)} custom-call(bf16[8,32,16,128]{3,2,1,0:T(8,128)(2,1)S(1)} %all-to-all-done.f_ref, bf16[256,128]{1,0:T(8,128)(2,1)S(1)} %copy-done.5, bf16[256,256]{1,0:T(8,128)(2,1)S(1)} %copy-done.2, f32[128,128]{1,0:T(8,128)S(1)} %copy-done.7, f32[128,128]{1,0:T(8,128)S(1)} %copy-done.6), custom_call_target="tpu_custom_call" | custom-call | flops 536870912 | bytes 5242880 | tf_op jit(solution)/shard_map/filter_spectra/pallas_call | solution.py:184
  50.3 0.0 collective-permute-done.4.refs_3_
  50.3 1.3 %collective-permute-done.5.refs_4_ = bf16[32,16,128]{2,1,0:T(8,128)(2,1)S(1)} collective-permute-done((bf16[32,16,128]{2,1,0:T(8,128)(2,1)}, bf16[32,16,128]{2,1,0:T(8,128)(2,1)S(1)}, u32[]{:S(2)}, u32[]{:S(2)}) %collective-permute-start.5) | collective-permute-done | bytes 131104 | tf_op jit(solution)/shard_map/ppermute | solution.py:370
  51.6 3.3 %collective-permute-done.6.refs_5_ = bf16[32,16,128]{2,1,0:T(8,128)(2,1)S(1)} collective-permute-done((bf16[32,16,128]{2,1,0:T(8,128)(2,1)}, bf16[32,16,128]{2,1,0:T(8,128)(2,1)S(1)}, u32[]{:S(2)}, u32[]{:S(2)}) %collective-permute-start.6) | collective-permute-done | bytes 131104 | tf_op jit(solution)/shard_map/ppermute | solution.py:370
  54.9 0.0 collective-permute-done.7.refs_6_
  54.9 0.0 collective-permute-done.8.refs_7_
  55.0 2.5 %convolve.1 = (bf16[32,16,128]{2,1,0:T(8,128)(2,1)S(1)}, bf16[32,16,128]{2,1,0:T(8,128)(2,1)S(1)}, bf16[32,16,128]{2,1,0:T(8,128)(2,1)S(1)}, bf16[32,16,128]{2,1...) custom-call(bf16[32,16,128]{2,1,0:T(8,128)(2,1)S(1)} %copy-done.4, ...), custom_call_target="tpu_custom_call" | custom-call | flops 1073741824 | bytes 6291456 | tf_op jit(solution)/shard_map/convolve/pallas_call | solution.py:236
  57.5 5.2 %collective-permute-start.14 = (bf16[32,16,128]{2,1,0:T(8,128)(2,1)S(1)}, bf16[32,16,128]{2,1,0:T(8,128)(2,1)S(1)}, u32[]{:S(2)}, u32[]{:S(2)}) collective-permute-start(bf16[32,16,128]{2,1,0:T(8,128)(2,1)S(1)} %get-tuple-element.49), channel_id=1, source_target_pairs={{0,16},{4,20},{8,24},{12,28},{16,0},{20,4},{24,8},{28,12},{1,17},{... | collective-permute-start | bytes 393224 | tf_op jit(solution)/shard_map/ppermute | solution.py:370
  62.7 0.0 collective-permute-start.15
  62.7 3.0 %collective-permute-start.16 = (bf16[32,16,128]{2,1,0:T(8,128)(2,1)S(1)}, bf16[32,16,128]{2,1,0:T(8,128)(2,1)S(1)}, u32[]{:S(2)}, u32[]{:S(2)}) collective-permute-start(bf16[32,16,128]{2,1,0:T(8,128)(2,1)S(1)} %get-tuple-element.51), channel_id=1, source_target_pairs={{0,8},{4,12},{8,0},{12,4},{16,24},{20,28},{24,16},{28,20},{1,9},{5... | collective-permute-start | bytes 393224 | tf_op jit(solution)/shard_map/ppermute | solution.py:370
  65.7 0.8 collective-permute-start.17
  66.5 6.2 %collective-permute-done.14.refs_0_ = bf16[32,16,128]{2,1,0:T(8,128)(2,1)S(1)} collective-permute-done((bf16[32,16,128]{2,1,0:T(8,128)(2,1)S(1)}, bf16[32,16,128]{2,1,0:T(8,128)(2,1)S(1)}, u32[]{:S(2)}, u32[]{:S(2)}) %collective-permute-start.14) | collective-permute-done | bytes 131104 | tf_op jit(solution)/shard_map/ppermute | solution.py:370
  72.7 2.0 %collective-permute-done.15.refs_1_ = bf16[32,16,128]{2,1,0:T(8,128)(2,1)S(1)} collective-permute-done((bf16[32,16,128]{2,1,0:T(8,128)(2,1)S(1)}, bf16[32,16,128]{2,1,0:T(8,128)(2,1)S(1)}, u32[]{:S(2)}, u32[]{:S(2)}) %collective-permute-start.15) | collective-permute-done | bytes 131104 | tf_op jit(solution)/shard_map/ppermute | solution.py:370
  74.6 0.0 collective-permute-done.16.refs_2_
  74.6 1.6 %collective-permute-done.17.refs_3_ = bf16[32,16,128]{2,1,0:T(8,128)(2,1)S(1)} collective-permute-done((bf16[32,16,128]{2,1,0:T(8,128)(2,1)S(1)}, bf16[32,16,128]{2,1,0:T(8,128)(2,1)S(1)}, u32[]{:S(2)}, u32[]{:S(2)}) %collective-permute-start.17) | collective-permute-done | bytes 131104 | tf_op jit(solution)/shard_map/ppermute | solution.py:370
  76.3 0.6 apply_gate.5.refs_3_
  76.9 1.6 %collective-permute-start.18 = (bf16[16,128,128]{2,1,0:T(8,128)(2,1)S(1)}, bf16[16,128,128]{2,1,0:T(8,128)(2,1)S(1)}, u32[]{:S(2)}, u32[]{:S(2)}) collective-permute-start(bf16[16,128,128]{2,1,0:T(8,128)(2,1)S(1)} %apply_gate.5.refs_3_), channel_id=1, source_target_pairs={{0,2},{1,3},{2,0},{3,1},{4,6},{5,7},{6,4},{7,5},{8,10},{9,11},{10,... | collective-permute-start | bytes 1572872 | tf_op jit(solution)/shard_map/ppermute | solution.py:370
  78.5 1.0 collective-permute-start.10
  79.5 0.7 collective-permute-start.12
  80.3 3.5 %collective-permute-start.13 = (bf16[32,16,128]{2,1,0:T(8,128)(2,1)S(1)}, bf16[32,16,128]{2,1,0:T(8,128)(2,1)S(1)}, u32[]{:S(2)}, u32[]{:S(2)}) collective-permute-start(bf16[32,16,128]{2,1,0:T(8,128)(2,1)S(1)} %get-tuple-element.47), channel_id=1, source_target_pairs={{0,28},{4,24},{8,20},{12,16},{16,12},{20,8},{24,4},{28,0},{1,29},{... | collective-permute-start | bytes 393224 | tf_op jit(solution)/shard_map/ppermute | solution.py:370
  83.8 0.0 collective-permute-start.21
  83.8 0.0 collective-permute-done.10.refs_1_
  83.8 0.3 apply_gate.3.refs_2_
  84.1 0.6 collective-permute-start.11
  84.7 1.6 %collective-permute-done.12.refs_0_ = bf16[32,16,128]{2,1,0:T(8,128)(2,1)S(1)} collective-permute-done((bf16[32,16,128]{2,1,0:T(8,128)(2,1)S(1)}, bf16[32,16,128]{2,1,0:T(8,128)(2,1)S(1)}, u32[]{:S(2)}, u32[]{:S(2)}) %collective-permute-start.12) | collective-permute-done | bytes 131104 | tf_op jit(solution)/shard_map/ppermute | solution.py:370
  86.3 1.8 %collective-permute-done.13.refs_1_ = bf16[32,16,128]{2,1,0:T(8,128)(2,1)S(1)} collective-permute-done((bf16[32,16,128]{2,1,0:T(8,128)(2,1)S(1)}, bf16[32,16,128]{2,1,0:T(8,128)(2,1)S(1)}, u32[]{:S(2)}, u32[]{:S(2)}) %collective-permute-start.13) | collective-permute-done | bytes 131104 | tf_op jit(solution)/shard_map/ppermute | solution.py:370
  88.1 0.3 apply_gate.4.refs_4_
  88.4 0.1 collective-permute-start.22
  88.5 1.4 %collective-permute-done.18.refs_3_ = bf16[16,128,128]{2,1,0:T(8,128)(2,1)S(1)} collective-permute-done((bf16[16,128,128]{2,1,0:T(8,128)(2,1)S(1)}, bf16[16,128,128]{2,1,0:T(8,128)(2,1)S(1)}, u32[]{:S(2)}, u32[]{:S(2)}) %collective-permute-start.18) | collective-permute-done | bytes 524320 | tf_op jit(solution)/shard_map/ppermute | solution.py:370
  90.0 0.0 collective-permute-start.24
  90.0 0.5 collective-permute-start.20
  90.5 3.8 %collective-permute-done.11.refs_2_ = bf16[16,64,128]{2,1,0:T(8,128)(2,1)S(1)} collective-permute-done((bf16[16,64,128]{2,1,0:T(8,128)(2,1)S(1)}, bf16[16,64,128]{2,1,0:T(8,128)(2,1)S(1)}, u32[]{:S(2)}, u32[]{:S(2)}) %collective-permute-start.11) | collective-permute-done | bytes 262176 | tf_op jit(solution)/shard_map/ppermute | solution.py:370
  94.3 1.5 %collective-permute-start.19 = (bf16[16,64,128]{2,1,0:T(8,128)(2,1)S(1)}, bf16[16,64,128]{2,1,0:T(8,128)(2,1)S(1)}, u32[]{:S(2)}, u32[]{:S(2)}) collective-permute-start(bf16[16,64,128]{2,1,0:T(8,128)(2,1)S(1)} %apply_gate.4.refs_4_), channel_id=1, source_target_pairs={{0,2},{1,3},{2,0},{3,1},{4,6},{5,7},{6,4},{7,5},{8,10},{9,11},{10,... | collective-permute-start | bytes 786440 | tf_op jit(solution)/shard_map/ppermute | solution.py:370
  95.8 0.0 collective-permute-done.22.refs_7_
  95.8 0.0 collective-permute-start.23
  95.8 0.0 collective-permute-done.20.refs_5_
  95.8 0.0 collective-permute-done.21.refs_6_
  95.8 0.7 mix_early.1.refs_8_
  96.5 4.8 %collective-permute-done.19.refs_4_ = bf16[16,64,128]{2,1,0:T(8,128)(2,1)S(1)} collective-permute-done((bf16[16,64,128]{2,1,0:T(8,128)(2,1)S(1)}, bf16[16,64,128]{2,1,0:T(8,128)(2,1)S(1)}, u32[]{:S(2)}, u32[]{:S(2)}) %collective-permute-start.19) | collective-permute-done | bytes 262176 | tf_op jit(solution)/shard_map/ppermute | solution.py:370
  101.3 0.0 collective-permute-done.23.refs_5_
  101.3 0.0 collective-permute-done.24.refs_6_
  101.3 1.5 %collective-permute-done.25.refs_7_ = bf16[16,64,128]{2,1,0:T(8,128)(2,1)S(1)} collective-permute-done((bf16[16,64,128]{2,1,0:T(8,128)(2,1)S(1)}, bf16[16,64,128]{2,1,0:T(8,128)(2,1)S(1)}, u32[]{:S(2)}, u32[]{:S(2)}) %collective-permute-start.25) | collective-permute-done | bytes 262176 | tf_op jit(solution)/shard_map/ppermute | solution.py:370
  102.8 1.6 %mix_last.1 = bf16[2048,256]{1,0:T(8,128)(2,1)} custom-call(bf16[256,256]{1,0:T(8,128)(2,1)S(1)} %collective-permute-done.refs_17_.refs_0_, bf16[256,256]{1,0:T(8,128)(2,1)S(1)} %collective-permute-done.1.refs_18_.refs_1_, bf16[16,64,128]{2,1,0:T(8,128)(2,1)S(1)} %collective-permute-done.11.refs_2_, ...), custom_call_target="tpu_custom_call" | custom-call | flops 536870912 | bytes 4194304 | tf_op jit(solution)/shard_map/mix_last/pallas_call | solution.py:357
  (36 shorter events, 0.1 us)
Async XLA Ops:
  0.0 1.2 %copy-start.1 = (bf16[2048,256]{1,0:T(8,128)(2,1)S(1)}, bf16[2048,256]{1,0:T(8,128)(2,1)}, u32[]{:S(2)}) copy-start(bf16[2048,256]{1,0:T(8,128)(2,1)} %f_ref.1) | copy-start | bytes 3145732
  1.2 9.1 %copy-start.3 = (bf16[256,1024]{1,0:T(8,128)(2,1)S(1)}, bf16[256,1024]{1,0:T(8,128)(2,1)}, u32[]{:S(2)}) copy-start(bf16[256,1024]{1,0:T(8,128)(2,1)} %w_ref.1) | copy-start | bytes 1572868
  1.2 9.2 %copy-start.17 = (f32[256]{0:T(256)S(1)}, f32[256]{0:T(256)}, u32[]{:S(2)}) copy-start(f32[256]{0:T(256)} %param.14) | copy-start | bytes 3076
  3.1 45.7 %all-to-all-start = ((bf16[8,32,16,128]{3,2,1,0:T(8,128)(2,1)}), bf16[8,32,16,128]{3,2,1,0:T(8,128)(2,1)S(1)}, u32[]{:S(2)}, u32[]{:S(2)}) async-start(bf16[8,32,16,128]{3,2,1,0:T(8,128)(2,1)} %filter_blocks.1._), calls=%async_computation | async-start | bytes 2097152 | tf_op jit(solution)/shard_map/all_to_all | solution.py:380
  10.7 14.6 %collective-permute-start = (bf16[256,256]{1,0:T(8,128)(2,1)S(1)}, bf16[256,256]{1,0:T(8,128)(2,1)S(1)}, u32[]{:S(2)}, u32[]{:S(2)}) collective-permute-start(bf16[256,256]{1,0:T(8,128)(2,1)S(1)} %get-tuple-element.30), channel_id=1, source_target_pairs={{0,2},{1,3},{2,0},{3,1},{4,6},{5,7},{6,4},{7,5},{8,10},{9,11},{10,... | collective-permute-start | bytes 393224 | tf_op jit(solution)/shard_map/ppermute | solution.py:370
  12.2 13.1 %collective-permute-start.1 = (bf16[256,256]{1,0:T(8,128)(2,1)S(1)}, bf16[256,256]{1,0:T(8,128)(2,1)S(1)}, u32[]{:S(2)}, u32[]{:S(2)}) collective-permute-start(bf16[256,256]{1,0:T(8,128)(2,1)S(1)} %get-tuple-element.31), channel_id=1, source_target_pairs={{0,3},{1,2},{2,1},{3,0},{4,7},{5,6},{6,5},{7,4},{8,11},{9,10},{10,... | collective-permute-start | bytes 393224 | tf_op jit(solution)/shard_map/ppermute | solution.py:370
  12.2 15.9 %collective-permute-start.9 = (bf16[256,256]{1,0:T(8,128)(2,1)S(1)}, bf16[256,256]{1,0:T(8,128)(2,1)S(1)}, u32[]{:S(2)}, u32[]{:S(2)}) collective-permute-start(bf16[256,256]{1,0:T(8,128)(2,1)S(1)} %get-tuple-element.43), channel_id=1, source_target_pairs={{0,1},{1,0},{2,3},{3,2},{4,5},{5,4},{6,7},{7,6},{8,9},{9,8},{10,11... | collective-permute-start | bytes 393224 | tf_op jit(solution)/shard_map/ppermute | solution.py:370
  12.9 36.0 %copy-start.2 = (bf16[256,256]{1,0:T(8,128)(2,1)S(1)}, bf16[256,256]{1,0:T(8,128)(2,1)}, u32[]{:S(2)}) copy-start(bf16[256,256]{1,0:T(8,128)(2,1)} %constant.19.b_fwd.refs_10_) | copy-start | bytes 393220
  12.9 36.0 %copy-start.5 = (bf16[256,128]{1,0:T(8,128)(2,1)S(1)}, bf16[256,128]{1,0:T(8,128)(2,1)}, u32[]{:S(2)}) copy-start(bf16[256,128]{1,0:T(8,128)(2,1)} %constant.18.a_fwd.refs_9_) | copy-start | bytes 196612
  12.9 36.0 %copy-start.6 = (f32[128,128]{1,0:T(8,128)S(1)}, f32[128,128]{1,0:T(8,128)}, u32[]{:S(2)}) copy-start(f32[128,128]{1,0:T(8,128)} %constant.17.clone.ts_ref.refs_14_) | copy-start | bytes 196612
  12.9 36.0 %copy-start.7 = (f32[128,128]{1,0:T(8,128)S(1)}, f32[128,128]{1,0:T(8,128)}, u32[]{:S(2)}) copy-start(f32[128,128]{1,0:T(8,128)} %constant.16.clone.tc_ref.refs_13_) | copy-start | bytes 196612
  21.7 33.2 %copy-start.4 = (bf16[32,16,128]{2,1,0:T(8,128)(2,1)S(1)}, bf16[32,16,128]{2,1,0:T(8,128)(2,1)}, u32[]{:S(2)}) copy-start(bf16[32,16,128]{2,1,0:T(8,128)(2,1)} %get-tuple-element.34.refs_0_.refs_2_) | copy-start | bytes 393220
  21.7 33.3 %copy-start.8 = (bf16[256,256]{1,0:T(8,128)(2,1)S(1)}, bf16[256,256]{1,0:T(8,128)(2,1)}, u32[]{:S(2)}) copy-start(bf16[256,256]{1,0:T(8,128)(2,1)} %constant.20.refs_11_) | copy-start | bytes 393220
  21.7 33.3 %copy-start.16 = (bf16[128,256]{1,0:T(8,128)(2,1)S(1)}, bf16[128,256]{1,0:T(8,128)(2,1)}, u32[]{:S(2)}) copy-start(bf16[128,256]{1,0:T(8,128)(2,1)} %constant.21.refs_12_) | copy-start | bytes 196612
  21.7 8.3 %collective-permute-start.2 = (bf16[32,16,128]{2,1,0:T(8,128)(2,1)}, bf16[32,16,128]{2,1,0:T(8,128)(2,1)S(1)}, u32[]{:S(2)}, u32[]{:S(2)}) collective-permute-start(bf16[32,16,128]{2,1,0:T(8,128)(2,1)} %get-tuple-element.35.refs_3_), channel_id=1, source_target_pairs={{0,4},{4,0},{8,12},{12,8},{16,20},{20,16},{24,28},{28,24},{1,5},{5... | collective-permute-start | bytes 393224 | tf_op jit(solution)/shard_map/ppermute | solution.py:370
  23.8 9.8 %collective-permute-start.3 = (bf16[32,16,128]{2,1,0:T(8,128)(2,1)}, bf16[32,16,128]{2,1,0:T(8,128)(2,1)S(1)}, u32[]{:S(2)}, u32[]{:S(2)}) collective-permute-start(bf16[32,16,128]{2,1,0:T(8,128)(2,1)} %get-tuple-element.36.refs_6_), channel_id=1, source_target_pairs={{0,8},{4,12},{8,0},{12,4},{16,24},{20,28},{24,16},{28,20},{1,9},{5... | collective-permute-start | bytes 393224 | tf_op jit(solution)/shard_map/ppermute | solution.py:370
  25.2 25.1 %collective-permute-start.4 = (bf16[32,16,128]{2,1,0:T(8,128)(2,1)}, bf16[32,16,128]{2,1,0:T(8,128)(2,1)S(1)}, u32[]{:S(2)}, u32[]{:S(2)}) collective-permute-start(bf16[32,16,128]{2,1,0:T(8,128)(2,1)} %get-tuple-element.37.refs_7_), channel_id=1, source_target_pairs={{0,12},{4,8},{8,4},{12,0},{16,28},{20,24},{24,20},{28,16},{1,13},{... | collective-permute-start | bytes 393224 | tf_op jit(solution)/shard_map/ppermute | solution.py:370
  25.3 26.3 %collective-permute-start.5 = (bf16[32,16,128]{2,1,0:T(8,128)(2,1)}, bf16[32,16,128]{2,1,0:T(8,128)(2,1)S(1)}, u32[]{:S(2)}, u32[]{:S(2)}) collective-permute-start(bf16[32,16,128]{2,1,0:T(8,128)(2,1)} %get-tuple-element.38.refs_4_), channel_id=1, source_target_pairs={{0,16},{4,20},{8,24},{12,28},{16,0},{20,4},{24,8},{28,12},{1,17},{... | collective-permute-start | bytes 393224 | tf_op jit(solution)/shard_map/ppermute | solution.py:370
  28.2 26.7 %collective-permute-start.6 = (bf16[32,16,128]{2,1,0:T(8,128)(2,1)}, bf16[32,16,128]{2,1,0:T(8,128)(2,1)S(1)}, u32[]{:S(2)}, u32[]{:S(2)}) collective-permute-start(bf16[32,16,128]{2,1,0:T(8,128)(2,1)} %get-tuple-element.39.refs_5_), channel_id=1, source_target_pairs={{0,20},{4,16},{8,28},{12,24},{16,4},{20,0},{24,12},{28,8},{1,21},{... | collective-permute-start | bytes 393224 | tf_op jit(solution)/shard_map/ppermute | solution.py:370
  30.0 24.9 %collective-permute-start.7 = (bf16[32,16,128]{2,1,0:T(8,128)(2,1)}, bf16[32,16,128]{2,1,0:T(8,128)(2,1)S(1)}, u32[]{:S(2)}, u32[]{:S(2)}) collective-permute-start(bf16[32,16,128]{2,1,0:T(8,128)(2,1)} %get-tuple-element.40.refs_2_), channel_id=1, source_target_pairs={{0,24},{4,28},{8,16},{12,20},{16,8},{20,12},{24,0},{28,4},{1,25},{... | collective-permute-start | bytes 393224 | tf_op jit(solution)/shard_map/ppermute | solution.py:370
  33.5 21.4 %collective-permute-start.8 = (bf16[32,16,128]{2,1,0:T(8,128)(2,1)}, bf16[32,16,128]{2,1,0:T(8,128)(2,1)S(1)}, u32[]{:S(2)}, u32[]{:S(2)}) collective-permute-start(bf16[32,16,128]{2,1,0:T(8,128)(2,1)} %get-tuple-element.41.refs_3_), channel_id=1, source_target_pairs={{0,28},{4,24},{8,20},{12,16},{16,12},{20,8},{24,4},{28,0},{1,29},{... | collective-permute-start | bytes 393224 | tf_op jit(solution)/shard_map/ppermute | solution.py:370
  50.3 26.0 %copy-start = (bf16[8,32,16,128]{3,2,1,0:T(8,128)(2,1)S(1)}, bf16[8,32,16,128]{3,2,1,0:T(8,128)(2,1)}, u32[]{:S(2)}) copy-start(bf16[8,32,16,128]{3,2,1,0:T(8,128)(2,1)} %get-tuple-element.32.gates) | copy-start | bytes 3145732
  50.3 26.0 %copy-start.12 = (bf16[32,16,128]{2,1,0:T(8,128)(2,1)S(1)}, bf16[32,16,128]{2,1,0:T(8,128)(2,1)}, u32[]{:S(2)}) copy-start(bf16[32,16,128]{2,1,0:T(8,128)(2,1)} %get-tuple-element.36.refs_6_) | copy-start | bytes 393220
  50.3 26.0 %copy-start.13 = (bf16[32,16,128]{2,1,0:T(8,128)(2,1)S(1)}, bf16[32,16,128]{2,1,0:T(8,128)(2,1)}, u32[]{:S(2)}) copy-start(bf16[32,16,128]{2,1,0:T(8,128)(2,1)} %get-tuple-element.37.refs_7_) | copy-start | bytes 393220
  50.3 26.0 %copy-start.14 = (bf16[32,16,128]{2,1,0:T(8,128)(2,1)S(1)}, bf16[32,16,128]{2,1,0:T(8,128)(2,1)}, u32[]{:S(2)}) copy-start(bf16[32,16,128]{2,1,0:T(8,128)(2,1)} %get-tuple-element.38.refs_4_) | copy-start | bytes 393220
  50.3 26.0 %copy-start.15 = (bf16[32,16,128]{2,1,0:T(8,128)(2,1)S(1)}, bf16[32,16,128]{2,1,0:T(8,128)(2,1)}, u32[]{:S(2)}) copy-start(bf16[32,16,128]{2,1,0:T(8,128)(2,1)} %get-tuple-element.39.refs_5_) | copy-start | bytes 393220
  54.9 28.9 %copy-start.11 = (bf16[32,16,128]{2,1,0:T(8,128)(2,1)S(1)}, bf16[32,16,128]{2,1,0:T(8,128)(2,1)}, u32[]{:S(2)}) copy-start(bf16[32,16,128]{2,1,0:T(8,128)(2,1)} %get-tuple-element.35.refs_3_) | copy-start | bytes 393220
  54.9 33.2 %copy-start.9 = (bf16[32,16,128]{2,1,0:T(8,128)(2,1)S(1)}, bf16[32,16,128]{2,1,0:T(8,128)(2,1)}, u32[]{:S(2)}) copy-start(bf16[32,16,128]{2,1,0:T(8,128)(2,1)} %get-tuple-element.40.refs_2_) | copy-start | bytes 393220
  55.0 33.2 %copy-start.10 = (bf16[32,16,128]{2,1,0:T(8,128)(2,1)S(1)}, bf16[32,16,128]{2,1,0:T(8,128)(2,1)}, u32[]{:S(2)}) copy-start(bf16[32,16,128]{2,1,0:T(8,128)(2,1)} %get-tuple-element.41.refs_3_) | copy-start | bytes 393220
  57.5 15.2 %collective-permute-start.14 = (bf16[32,16,128]{2,1,0:T(8,128)(2,1)S(1)}, bf16[32,16,128]{2,1,0:T(8,128)(2,1)S(1)}, u32[]{:S(2)}, u32[]{:S(2)}) collective-permute-start(bf16[32,16,128]{2,1,0:T(8,128)(2,1)S(1)} %get-tuple-element.49), channel_id=1, source_target_pairs={{0,16},{4,20},{8,24},{12,28},{16,0},{20,4},{24,8},{28,12},{1,17},{... | collective-permute-start | bytes 393224 | tf_op jit(solution)/shard_map/ppermute | solution.py:370
  62.7 12.0 %collective-permute-start.15 = (bf16[32,16,128]{2,1,0:T(8,128)(2,1)S(1)}, bf16[32,16,128]{2,1,0:T(8,128)(2,1)S(1)}, u32[]{:S(2)}, u32[]{:S(2)}) collective-permute-start(bf16[32,16,128]{2,1,0:T(8,128)(2,1)S(1)} %get-tuple-element.50), channel_id=1, source_target_pairs={{0,20},{4,16},{8,28},{12,24},{16,4},{20,0},{24,12},{28,8},{1,21},{... | collective-permute-start | bytes 393224 | tf_op jit(solution)/shard_map/ppermute | solution.py:370
  62.7 12.0 %collective-permute-start.16 = (bf16[32,16,128]{2,1,0:T(8,128)(2,1)S(1)}, bf16[32,16,128]{2,1,0:T(8,128)(2,1)S(1)}, u32[]{:S(2)}, u32[]{:S(2)}) collective-permute-start(bf16[32,16,128]{2,1,0:T(8,128)(2,1)S(1)} %get-tuple-element.51), channel_id=1, source_target_pairs={{0,8},{4,12},{8,0},{12,4},{16,24},{20,28},{24,16},{28,20},{1,9},{5... | collective-permute-start | bytes 393224 | tf_op jit(solution)/shard_map/ppermute | solution.py:370
  65.7 10.6 %collective-permute-start.17 = (bf16[32,16,128]{2,1,0:T(8,128)(2,1)S(1)}, bf16[32,16,128]{2,1,0:T(8,128)(2,1)S(1)}, u32[]{:S(2)}, u32[]{:S(2)}) collective-permute-start(bf16[32,16,128]{2,1,0:T(8,128)(2,1)S(1)} %get-tuple-element.52), channel_id=1, source_target_pairs={{0,12},{4,8},{8,4},{12,0},{16,28},{20,24},{24,20},{28,16},{1,13},{... | collective-permute-start | bytes 393224 | tf_op jit(solution)/shard_map/ppermute | solution.py:370
  76.9 13.0 %collective-permute-start.18 = (bf16[16,128,128]{2,1,0:T(8,128)(2,1)S(1)}, bf16[16,128,128]{2,1,0:T(8,128)(2,1)S(1)}, u32[]{:S(2)}, u32[]{:S(2)}) collective-permute-start(bf16[16,128,128]{2,1,0:T(8,128)(2,1)S(1)} %apply_gate.5.refs_3_), channel_id=1, source_target_pairs={{0,2},{1,3},{2,0},{3,1},{4,6},{5,7},{6,4},{7,5},{8,10},{9,11},{10,... | collective-permute-start | bytes 1572872 | tf_op jit(solution)/shard_map/ppermute | solution.py:370
  78.5 5.3 %collective-permute-start.10 = (bf16[32,16,128]{2,1,0:T(8,128)(2,1)S(1)}, bf16[32,16,128]{2,1,0:T(8,128)(2,1)S(1)}, u32[]{:S(2)}, u32[]{:S(2)}) collective-permute-start(bf16[32,16,128]{2,1,0:T(8,128)(2,1)S(1)} %get-tuple-element.45), channel_id=1, source_target_pairs={{0,4},{4,0},{8,12},{12,8},{16,20},{20,16},{24,28},{28,24},{1,5},{5... | collective-permute-start | bytes 393224 | tf_op jit(solution)/shard_map/ppermute | solution.py:370
  79.5 6.8 %collective-permute-start.12 = (bf16[32,16,128]{2,1,0:T(8,128)(2,1)S(1)}, bf16[32,16,128]{2,1,0:T(8,128)(2,1)S(1)}, u32[]{:S(2)}, u32[]{:S(2)}) collective-permute-start(bf16[32,16,128]{2,1,0:T(8,128)(2,1)S(1)} %get-tuple-element.46), channel_id=1, source_target_pairs={{0,24},{4,28},{8,16},{12,20},{16,8},{20,12},{24,0},{28,4},{1,25},{... | collective-permute-start | bytes 393224 | tf_op jit(solution)/shard_map/ppermute | solution.py:370
  80.3 7.9 %collective-permute-start.13 = (bf16[32,16,128]{2,1,0:T(8,128)(2,1)S(1)}, bf16[32,16,128]{2,1,0:T(8,128)(2,1)S(1)}, u32[]{:S(2)}, u32[]{:S(2)}) collective-permute-start(bf16[32,16,128]{2,1,0:T(8,128)(2,1)S(1)} %get-tuple-element.47), channel_id=1, source_target_pairs={{0,28},{4,24},{8,20},{12,16},{16,12},{20,8},{24,4},{28,0},{1,29},{... | collective-permute-start | bytes 393224 | tf_op jit(solution)/shard_map/ppermute | solution.py:370
  83.8 12.0 %collective-permute-start.21 = (bf16[16,128,128]{2,1,0:T(8,128)(2,1)S(1)}, bf16[16,128,128]{2,1,0:T(8,128)(2,1)S(1)}, u32[]{:S(2)}, u32[]{:S(2)}) collective-permute-start(bf16[16,128,128]{2,1,0:T(8,128)(2,1)S(1)} %apply_gate.5.refs_3_), channel_id=1, source_target_pairs={{0,1},{1,0},{2,3},{3,2},{4,5},{5,4},{6,7},{7,6},{8,9},{9,8},{10,11... | collective-permute-start | bytes 1572872 | tf_op jit(solution)/shard_map/ppermute | solution.py:370
  84.1 10.2 %collective-permute-start.11 = (bf16[16,64,128]{2,1,0:T(8,128)(2,1)S(1)}, bf16[16,64,128]{2,1,0:T(8,128)(2,1)S(1)}, u32[]{:S(2)}, u32[]{:S(2)}) collective-permute-start(bf16[16,64,128]{2,1,0:T(8,128)(2,1)S(1)} %apply_gate.3.refs_2_), channel_id=1, source_target_pairs={{0,2},{1,3},{2,0},{3,1},{4,6},{5,7},{6,4},{7,5},{8,10},{9,11},{10,... | collective-permute-start | bytes 786440 | tf_op jit(solution)/shard_map/ppermute | solution.py:370
  88.4 7.3 %collective-permute-start.22 = (bf16[16,64,128]{2,1,0:T(8,128)(2,1)S(1)}, bf16[16,64,128]{2,1,0:T(8,128)(2,1)S(1)}, u32[]{:S(2)}, u32[]{:S(2)}) collective-permute-start(bf16[16,64,128]{2,1,0:T(8,128)(2,1)S(1)} %apply_gate.4.refs_4_), channel_id=1, source_target_pairs={{0,1},{1,0},{2,3},{3,2},{4,5},{5,4},{6,7},{7,6},{8,9},{9,8},{10,11... | collective-permute-start | bytes 786440 | tf_op jit(solution)/shard_map/ppermute | solution.py:370
  90.0 11.3 %collective-permute-start.24 = (bf16[16,128,128]{2,1,0:T(8,128)(2,1)S(1)}, bf16[16,128,128]{2,1,0:T(8,128)(2,1)S(1)}, u32[]{:S(2)}, u32[]{:S(2)}) collective-permute-start(bf16[16,128,128]{2,1,0:T(8,128)(2,1)S(1)} %collective-permute-done.18.refs_3_), channel_id=1, source_target_pairs={{0,1},{1,0},{2,3},{3,2},{4,5},{5,4},{6,7},{7,6},{8,9},{9,8},{10,11... | collective-permute-start | bytes 1572872 | tf_op jit(solution)/shard_map/ppermute | solution.py:370
  90.0 5.8 %collective-permute-start.20 = (bf16[16,64,128]{2,1,0:T(8,128)(2,1)S(1)}, bf16[16,64,128]{2,1,0:T(8,128)(2,1)S(1)}, u32[]{:S(2)}, u32[]{:S(2)}) collective-permute-start(bf16[16,64,128]{2,1,0:T(8,128)(2,1)S(1)} %apply_gate.3.refs_2_), channel_id=1, source_target_pairs={{0,1},{1,0},{2,3},{3,2},{4,5},{5,4},{6,7},{7,6},{8,9},{9,8},{10,11... | collective-permute-start | bytes 786440 | tf_op jit(solution)/shard_map/ppermute | solution.py:370
  94.3 7.0 %collective-permute-start.19 = (bf16[16,64,128]{2,1,0:T(8,128)(2,1)S(1)}, bf16[16,64,128]{2,1,0:T(8,128)(2,1)S(1)}, u32[]{:S(2)}, u32[]{:S(2)}) collective-permute-start(bf16[16,64,128]{2,1,0:T(8,128)(2,1)S(1)} %apply_gate.4.refs_4_), channel_id=1, source_target_pairs={{0,2},{1,3},{2,0},{3,1},{4,6},{5,7},{6,4},{7,5},{8,10},{9,11},{10,... | collective-permute-start | bytes 786440 | tf_op jit(solution)/shard_map/ppermute | solution.py:370
  95.8 5.5 %collective-permute-start.23 = (bf16[16,64,128]{2,1,0:T(8,128)(2,1)S(1)}, bf16[16,64,128]{2,1,0:T(8,128)(2,1)S(1)}, u32[]{:S(2)}, u32[]{:S(2)}) collective-permute-start(bf16[16,64,128]{2,1,0:T(8,128)(2,1)S(1)} %collective-permute-done.11.refs_2_), channel_id=1, source_target_pairs={{0,1},{1,0},{2,3},{3,2},{4,5},{5,4},{6,7},{7,6},{8,9},{9,8},{10,11... | collective-permute-start | bytes 786440 | tf_op jit(solution)/shard_map/ppermute | solution.py:370
  101.3 1.5 %collective-permute-start.25 = (bf16[16,64,128]{2,1,0:T(8,128)(2,1)S(1)}, bf16[16,64,128]{2,1,0:T(8,128)(2,1)S(1)}, u32[]{:S(2)}, u32[]{:S(2)}) collective-permute-start(bf16[16,64,128]{2,1,0:T(8,128)(2,1)S(1)} %collective-permute-done.19.refs_4_), channel_id=1, source_target_pairs={{0,1},{1,0},{2,3},{3,2},{4,5},{5,4},{6,7},{7,6},{8,9},{9,8},{10,11... | collective-permute-start | bytes 786440 | tf_op jit(solution)/shard_map/ppermute | solution.py:370

commit v3 on v2

--- a/solution.py
+++ b/solution.py
@@ -10,7 +10,7 @@
 from jax.sharding import PartitionSpec as P
 
 LANES = 128
-GROUPS = ((0,1),(4,5,2,3),(6,7))
+GROUPS = ((4, 5, 0), (2, 3, 1), (6, 7))
 NEAR = (1, 2, 3)
 SMALL = 16
 LANES = 128

time: 105 us -> 103 us (0.981)
  waiting for transfers between devices: 42.4 us -> 40.9 us
    ppermute x26, waiting for transfers between devices: 29.7 us -> 28.2 us  [swap(): return lax.ppermute(value, axis, [(i, i ^ step) for i in range(size)])]
  transfers between devices with their start and end apart: 27 -> 27, of which waited for: 13 -> 14; matrix products, arithmetic and copies ran while one was open for 0% -> 0% of each run, Pallas kernels for 11% -> 12%
where the time goes in v3:
time: 103 us
  starting transfers between devices  42.5 us (41%)
  waiting for transfers between devices  40.9 us (40%)
  Pallas kernels  18.3 us (18%)
  local copies, waits for them, and re-layouts  1.29 us (1%)
    ppermute x26, starting transfers between devices, swap(): return lax.ppermute(value, axis, [(i, i ^ step) for i in range(size)])  35.2 us
    ppermute x26, waiting for transfers between devices, swap(): return lax.ppermute(value, axis, [(i, i ^ step) for i in range(size)])  28.2 us
    all_to_all x1, waiting for transfers between devices, on_device(): lax.all_to_all(filt_sends, 'seq', split_axis=0, concat_axis=0, tiled=True)  12.6 us
    pallas_call x1, Pallas kernels, project(): pl.pallas_call(functools.partial(project_kernel, seq), grid=(frames // ti...  8.77 us
    all_to_all x1, starting transfers between devices, on_device(): lax.all_to_all(filt_sends, 'seq', split_axis=0, concat_axis=0, tiled=True)  7.28 us
    pallas_call x1, Pallas kernels, convolve(): pl.pallas_call(functools.partial(conv_kernel, seq, len(ready)), in_specs=...  2.51 us
  transfers between devices with their start and end apart: 27, of which 14 were waited for; matrix products, arithmetic and copies ran while one was open for 0% of the time, Pallas kernels for 12%

profile of v3, /device:TPU:0, one launch (start us, length us, event | category | flops | bytes accessed | tf_op | source)
XLA Modules:
  0.0 103.2 jit_solution(11068841459140402094)
XLA Ops:
  0.0 1.2 %copy-done.1 = bf16[2048,256]{1,0:T(8,128)(2,1)S(1)} copy-done((bf16[2048,256]{1,0:T(8,128)(2,1)S(1)}, bf16[2048,256]{1,0:T(8,128)(2,1)}, u32[]{:S(2)}) %copy-start.1) | copy-done | bytes 1048600
  1.2 1.9 %filter_blocks.1._ = bf16[8,32,16,128]{3,2,1,0:T(8,128)(2,1)} custom-call(bf16[2048,256]{1,0:T(8,128)(2,1)S(1)} %copy-done.1), custom_call_target="tpu_custom_call" | custom-call | bytes 4194304 | tf_op jit(solution)/shard_map/filter_blocks/pallas_call | solution.py:84
  3.1 7.3 %all-to-all-start = ((bf16[8,32,16,128]{3,2,1,0:T(8,128)(2,1)}), bf16[8,32,16,128]{3,2,1,0:T(8,128)(2,1)S(1)}, u32[]{:S(2)}, u32[]{:S(2)}) async-start(bf16[8,32,16,128]{3,2,1,0:T(8,128)(2,1)} %filter_blocks.1._), calls=%async_computation | async-start | bytes 2097152 | tf_op jit(solution)/shard_map/all_to_all | solution.py:380
  10.4 0.3 out_weights.1
  10.7 1.6 %collective-permute-start = (bf16[256,256]{1,0:T(8,128)(2,1)S(1)}, bf16[256,256]{1,0:T(8,128)(2,1)S(1)}, u32[]{:S(2)}, u32[]{:S(2)}) collective-permute-start(bf16[256,256]{1,0:T(8,128)(2,1)S(1)} %get-tuple-element.30), channel_id=1, source_target_pairs={{0,2},{1,3},{2,0},{3,1},{4,6},{5,7},{6,4},{7,5},{8,10},{9,11},{10,... | collective-permute-start | bytes 393224 | tf_op jit(solution)/shard_map/ppermute | solution.py:370
  12.2 0.0 collective-permute-start.1
  12.2 0.6 collective-permute-start.9
  12.9 8.8 %project.1 = (bf16[8,32,16,128]{3,2,1,0:T(8,128)(2,1)}, bf16[32,16,128]{2,1,0:T(8,128)(2,1)}, bf16[32,16,128]{2,1,0:T(8,128)(2,1)}, bf16[32,16,128]{2,1,0:T(8,12...) custom-call(bf16[2048,1024]{1,0:T(8,128)(2,1)} %x_ref.1, ...), custom_call_target="tpu_custom_call" | custom-call | flops 3221225472 | bytes 16777216 | tf_op jit(solution)/shard_map/project/pallas_call | solution.py:128
  21.7 2.1 %collective-permute-start.2 = (bf16[32,16,128]{2,1,0:T(8,128)(2,1)}, bf16[32,16,128]{2,1,0:T(8,128)(2,1)S(1)}, u32[]{:S(2)}, u32[]{:S(2)}) collective-permute-start(bf16[32,16,128]{2,1,0:T(8,128)(2,1)} %get-tuple-element.35.refs_5_), channel_id=1, source_target_pairs={{0,4},{4,0},{8,12},{12,8},{16,20},{20,16},{24,28},{28,24},{1,5},{5... | collective-permute-start | bytes 393224 | tf_op jit(solution)/shard_map/ppermute | solution.py:370
  23.8 1.5 %collective-permute-start.3 = (bf16[32,16,128]{2,1,0:T(8,128)(2,1)}, bf16[32,16,128]{2,1,0:T(8,128)(2,1)S(1)}, u32[]{:S(2)}, u32[]{:S(2)}) collective-permute-start(bf16[32,16,128]{2,1,0:T(8,128)(2,1)} %get-tuple-element.36.refs_3_), channel_id=1, source_target_pairs={{0,8},{4,12},{8,0},{12,4},{16,24},{20,28},{24,16},{28,20},{1,9},{5... | collective-permute-start | bytes 393224 | tf_op jit(solution)/shard_map/ppermute | solution.py:370
  25.2 0.0 collective-permute-done.refs_17_.refs_0_
  25.2 0.1 collective-permute-start.4
  25.3 0.0 collective-permute-done.1.refs_18_.refs_1_
  25.3 2.8 %collective-permute-start.5 = (bf16[32,16,128]{2,1,0:T(8,128)(2,1)}, bf16[32,16,128]{2,1,0:T(8,128)(2,1)S(1)}, u32[]{:S(2)}, u32[]{:S(2)}) collective-permute-start(bf16[32,16,128]{2,1,0:T(8,128)(2,1)} %get-tuple-element.38.refs_3_), channel_id=1, source_target_pairs={{0,16},{4,20},{8,24},{12,28},{16,0},{20,4},{24,8},{28,12},{1,17},{... | collective-permute-start | bytes 393224 | tf_op jit(solution)/shard_map/ppermute | solution.py:370
  28.1 0.0 collective-permute-done.9.refs_16_.refs_1_
  28.2 1.5 %collective-permute-start.6 = (bf16[32,16,128]{2,1,0:T(8,128)(2,1)}, bf16[32,16,128]{2,1,0:T(8,128)(2,1)S(1)}, u32[]{:S(2)}, u32[]{:S(2)}) collective-permute-start(bf16[32,16,128]{2,1,0:T(8,128)(2,1)} %get-tuple-element.39.refs_4_), channel_id=1, source_target_pairs={{0,20},{4,16},{8,28},{12,24},{16,4},{20,0},{24,12},{28,8},{1,21},{... | collective-permute-start | bytes 393224 | tf_op jit(solution)/shard_map/ppermute | solution.py:370
  29.6 0.4 collective-permute-done.2.refs_1_
  30.0 3.5 %collective-permute-start.7 = (bf16[32,16,128]{2,1,0:T(8,128)(2,1)}, bf16[32,16,128]{2,1,0:T(8,128)(2,1)S(1)}, u32[]{:S(2)}, u32[]{:S(2)}) collective-permute-start(bf16[32,16,128]{2,1,0:T(8,128)(2,1)} %get-tuple-element.40.refs_2_), channel_id=1, source_target_pairs={{0,24},{4,28},{8,16},{12,20},{16,8},{20,12},{24,0},{28,4},{1,25},{... | collective-permute-start | bytes 393224 | tf_op jit(solution)/shard_map/ppermute | solution.py:370
  33.5 0.0 collective-permute-done.3.refs_2_
  33.5 2.7 %collective-permute-start.8 = (bf16[32,16,128]{2,1,0:T(8,128)(2,1)}, bf16[32,16,128]{2,1,0:T(8,128)(2,1)S(1)}, u32[]{:S(2)}, u32[]{:S(2)}) collective-permute-start(bf16[32,16,128]{2,1,0:T(8,128)(2,1)} %get-tuple-element.41.refs_3_), channel_id=1, source_target_pairs={{0,28},{4,24},{8,20},{12,16},{16,12},{20,8},{24,4},{28,0},{1,29},{... | collective-permute-start | bytes 393224 | tf_op jit(solution)/shard_map/ppermute | solution.py:370
  36.2 12.6 %all-to-all-done.f_ref = bf16[8,32,16,128]{3,2,1,0:T(8,128)(2,1)S(1)} async-done(((bf16[8,32,16,128]{3,2,1,0:T(8,128)(2,1)}), bf16[8,32,16,128]{3,2,1,0:T(8,128)(2,1)S(1)}, u32[]{:S(2)}, u32[]{:S(2)}) %all-to-all-start) | async-done | bytes 1048608 | tf_op jit(solution)/shard_map/all_to_all | solution.py:380
  48.9 1.4 %filter_spectra.1.refs_8_ = f32[32,128,256]{2,1,0:T(8,128)S(1)} custom-call(bf16[8,32,16,128]{3,2,1,0:T(8,128)(2,1)S(1)} %all-to-all-done.f_ref, bf16[256,128]{1,0:T(8,128)(2,1)S(1)} %copy-done.5, bf16[256,256]{1,0:T(8,128)(2,1)S(1)} %copy-done.3, f32[128,128]{1,0:T(8,128)S(1)} %copy-done.7, f32[128,128]{1,0:T(8,128)S(1)} %copy-done.6), custom_call_target="tpu_custom_call" | custom-call | flops 536870912 | bytes 5242880 | tf_op jit(solution)/shard_map/filter_spectra/pallas_call | solution.py:184
  50.3 0.0 collective-permute-done.4.refs_3_
  50.3 1.3 %collective-permute-done.5.refs_4_ = bf16[32,16,128]{2,1,0:T(8,128)(2,1)S(1)} collective-permute-done((bf16[32,16,128]{2,1,0:T(8,128)(2,1)}, bf16[32,16,128]{2,1,0:T(8,128)(2,1)S(1)}, u32[]{:S(2)}, u32[]{:S(2)}) %collective-permute-start.5) | collective-permute-done | bytes 131104 | tf_op jit(solution)/shard_map/ppermute | solution.py:370
  51.6 3.3 %collective-permute-done.6.refs_5_ = bf16[32,16,128]{2,1,0:T(8,128)(2,1)S(1)} collective-permute-done((bf16[32,16,128]{2,1,0:T(8,128)(2,1)}, bf16[32,16,128]{2,1,0:T(8,128)(2,1)S(1)}, u32[]{:S(2)}, u32[]{:S(2)}) %collective-permute-start.6) | collective-permute-done | bytes 131104 | tf_op jit(solution)/shard_map/ppermute | solution.py:370
  54.9 0.0 collective-permute-done.7.refs_6_
  54.9 0.0 collective-permute-done.8.refs_7_
  55.0 2.5 %convolve.1 = (bf16[32,16,128]{2,1,0:T(8,128)(2,1)S(1)}, bf16[32,16,128]{2,1,0:T(8,128)(2,1)S(1)}, bf16[32,16,128]{2,1,0:T(8,128)(2,1)S(1)}, bf16[32,16,128]{2,1...) custom-call(bf16[32,16,128]{2,1,0:T(8,128)(2,1)S(1)} %copy-done.2, ...), custom_call_target="tpu_custom_call" | custom-call | flops 1073741824 | bytes 6291456 | tf_op jit(solution)/shard_map/convolve/pallas_call | solution.py:236
  57.5 5.2 %collective-permute-start.15 = (bf16[32,16,128]{2,1,0:T(8,128)(2,1)S(1)}, bf16[32,16,128]{2,1,0:T(8,128)(2,1)S(1)}, u32[]{:S(2)}, u32[]{:S(2)}) collective-permute-start(bf16[32,16,128]{2,1,0:T(8,128)(2,1)S(1)} %get-tuple-element.50), channel_id=1, source_target_pairs={{0,8},{4,12},{8,0},{12,4},{16,24},{20,28},{24,16},{28,20},{1,9},{5... | collective-permute-start | bytes 393224 | tf_op jit(solution)/shard_map/ppermute | solution.py:370
  62.7 0.2 collective-permute-start.16
  62.8 1.4 %collective-permute-start.17 = (bf16[32,16,128]{2,1,0:T(8,128)(2,1)S(1)}, bf16[32,16,128]{2,1,0:T(8,128)(2,1)S(1)}, u32[]{:S(2)}, u32[]{:S(2)}) collective-permute-start(bf16[32,16,128]{2,1,0:T(8,128)(2,1)S(1)} %get-tuple-element.52), channel_id=1, source_target_pairs={{0,4},{4,0},{8,12},{12,8},{16,20},{20,16},{24,28},{28,24},{1,5},{5... | collective-permute-start | bytes 393224 | tf_op jit(solution)/shard_map/ppermute | solution.py:370
  64.2 1.9 %collective-permute-start.10 = (bf16[32,16,128]{2,1,0:T(8,128)(2,1)S(1)}, bf16[32,16,128]{2,1,0:T(8,128)(2,1)S(1)}, u32[]{:S(2)}, u32[]{:S(2)}) collective-permute-start(bf16[32,16,128]{2,1,0:T(8,128)(2,1)S(1)} %get-tuple-element.44), channel_id=1, source_target_pairs={{0,16},{4,20},{8,24},{12,28},{16,0},{20,4},{24,8},{28,12},{1,17},{... | collective-permute-start | bytes 393224 | tf_op jit(solution)/shard_map/ppermute | solution.py:370
  66.2 1.1 %collective-permute-start.11 = (bf16[32,16,128]{2,1,0:T(8,128)(2,1)S(1)}, bf16[32,16,128]{2,1,0:T(8,128)(2,1)S(1)}, u32[]{:S(2)}, u32[]{:S(2)}) collective-permute-start(bf16[32,16,128]{2,1,0:T(8,128)(2,1)S(1)} %get-tuple-element.45), channel_id=1, source_target_pairs={{0,20},{4,16},{8,28},{12,24},{16,4},{20,0},{24,12},{28,8},{1,21},{... | collective-permute-start | bytes 393224 | tf_op jit(solution)/shard_map/ppermute | solution.py:370
  67.2 1.0 collective-permute-done.15.refs_0_
  68.2 3.2 %collective-permute-done.16.refs_1_ = bf16[32,16,128]{2,1,0:T(8,128)(2,1)S(1)} collective-permute-done((bf16[32,16,128]{2,1,0:T(8,128)(2,1)S(1)}, bf16[32,16,128]{2,1,0:T(8,128)(2,1)S(1)}, u32[]{:S(2)}, u32[]{:S(2)}) %collective-permute-start.16) | collective-permute-done | bytes 131104 | tf_op jit(solution)/shard_map/ppermute | solution.py:370
  71.4 0.0 collective-permute-done.17.refs_2_
  71.4 0.5 apply_gate.5.refs_3_
  71.9 1.5 %collective-permute-start.18 = (bf16[16,96,128]{2,1,0:T(8,128)(2,1)S(1)}, bf16[16,96,128]{2,1,0:T(8,128)(2,1)S(1)}, u32[]{:S(2)}, u32[]{:S(2)}) collective-permute-start(bf16[16,96,128]{2,1,0:T(8,128)(2,1)S(1)} %apply_gate.5.refs_3_), channel_id=1, source_target_pairs={{0,2},{1,3},{2,0},{3,1},{4,6},{5,7},{6,4},{7,5},{8,10},{9,11},{10,... | collective-permute-start | bytes 1179656 | tf_op jit(solution)/shard_map/ppermute | solution.py:370
  73.4 3.4 %collective-permute-done.10.refs_0_ = bf16[32,16,128]{2,1,0:T(8,128)(2,1)S(1)} collective-permute-done((bf16[32,16,128]{2,1,0:T(8,128)(2,1)S(1)}, bf16[32,16,128]{2,1,0:T(8,128)(2,1)S(1)}, u32[]{:S(2)}, u32[]{:S(2)}) %collective-permute-start.10) | collective-permute-done | bytes 131104 | tf_op jit(solution)/shard_map/ppermute | solution.py:370
  76.8 1.8 %collective-permute-done.11.refs_1_ = bf16[32,16,128]{2,1,0:T(8,128)(2,1)S(1)} collective-permute-done((bf16[32,16,128]{2,1,0:T(8,128)(2,1)S(1)}, bf16[32,16,128]{2,1,0:T(8,128)(2,1)S(1)}, u32[]{:S(2)}, u32[]{:S(2)}) %collective-permute-start.11) | collective-permute-done | bytes 131104 | tf_op jit(solution)/shard_map/ppermute | solution.py:370
  78.6 0.5 apply_gate.3.refs_2_
  79.1 1.6 %collective-permute-start.12 = (bf16[16,96,128]{2,1,0:T(8,128)(2,1)S(1)}, bf16[16,96,128]{2,1,0:T(8,128)(2,1)S(1)}, u32[]{:S(2)}, u32[]{:S(2)}) collective-permute-start(bf16[16,96,128]{2,1,0:T(8,128)(2,1)S(1)} %apply_gate.3.refs_2_), channel_id=1, source_target_pairs={{0,2},{1,3},{2,0},{3,1},{4,6},{5,7},{6,4},{7,5},{8,10},{9,11},{10,... | collective-permute-start | bytes 1179656 | tf_op jit(solution)/shard_map/ppermute | solution.py:370
  80.6 1.2 %collective-permute-start.13 = (bf16[32,16,128]{2,1,0:T(8,128)(2,1)S(1)}, bf16[32,16,128]{2,1,0:T(8,128)(2,1)S(1)}, u32[]{:S(2)}, u32[]{:S(2)}) collective-permute-start(bf16[32,16,128]{2,1,0:T(8,128)(2,1)S(1)} %get-tuple-element.47), channel_id=1, source_target_pairs={{0,24},{4,28},{8,16},{12,20},{16,8},{20,12},{24,0},{28,4},{1,25},{... | collective-permute-start | bytes 393224 | tf_op jit(solution)/shard_map/ppermute | solution.py:370
  81.8 3.1 %collective-permute-start.14 = (bf16[32,16,128]{2,1,0:T(8,128)(2,1)S(1)}, bf16[32,16,128]{2,1,0:T(8,128)(2,1)S(1)}, u32[]{:S(2)}, u32[]{:S(2)}) collective-permute-start(bf16[32,16,128]{2,1,0:T(8,128)(2,1)S(1)} %get-tuple-element.48), channel_id=1, source_target_pairs={{0,28},{4,24},{8,20},{12,16},{16,12},{20,8},{24,4},{28,0},{1,29},{... | collective-permute-start | bytes 393224 | tf_op jit(solution)/shard_map/ppermute | solution.py:370
  84.9 3.4 %collective-permute-done.13.refs_0_ = bf16[32,16,128]{2,1,0:T(8,128)(2,1)S(1)} collective-permute-done((bf16[32,16,128]{2,1,0:T(8,128)(2,1)S(1)}, bf16[32,16,128]{2,1,0:T(8,128)(2,1)S(1)}, u32[]{:S(2)}, u32[]{:S(2)}) %collective-permute-start.13) | collective-permute-done | bytes 131104 | tf_op jit(solution)/shard_map/ppermute | solution.py:370
  88.3 1.5 %collective-permute-done.14.refs_1_ = bf16[32,16,128]{2,1,0:T(8,128)(2,1)S(1)} collective-permute-done((bf16[32,16,128]{2,1,0:T(8,128)(2,1)S(1)}, bf16[32,16,128]{2,1,0:T(8,128)(2,1)S(1)}, u32[]{:S(2)}, u32[]{:S(2)}) %collective-permute-start.14) | collective-permute-done | bytes 131104 | tf_op jit(solution)/shard_map/ppermute | solution.py:370
  89.8 0.3 apply_gate.4.refs_4_
  90.1 0.1 collective-permute-start.22
  90.2 0.5 collective-permute-start.21
  90.7 0.1 collective-permute-start.20
  90.8 0.0 collective-permute-done.18.refs_3_
  90.8 0.4 collective-permute-start.24
  91.2 0.0 collective-permute-done.12.refs_2_
  91.2 0.1 collective-permute-start.23
  91.3 0.4 collective-permute-done.22.refs_7_
  91.7 0.5 collective-permute-start.19
  92.3 0.0 collective-permute-done.21.refs_6_
  92.3 0.6 collective-permute-done.20.refs_5_
  92.9 0.7 mix_early.1.refs_8_
  93.6 6.5 %collective-permute-done.19.refs_4_ = bf16[16,64,128]{2,1,0:T(8,128)(2,1)S(1)} collective-permute-done((bf16[16,64,128]{2,1,0:T(8,128)(2,1)S(1)}, bf16[16,64,128]{2,1,0:T(8,128)(2,1)S(1)}, u32[]{:S(2)}, u32[]{:S(2)}) %collective-permute-start.19) | collective-permute-done | bytes 262176 | tf_op jit(solution)/shard_map/ppermute | solution.py:370
  100.1 0.0 collective-permute-done.24.refs_6_
  100.1 0.0 collective-permute-done.23.refs_5_
  100.1 1.5 %collective-permute-done.25.refs_7_ = bf16[16,64,128]{2,1,0:T(8,128)(2,1)S(1)} collective-permute-done((bf16[16,64,128]{2,1,0:T(8,128)(2,1)S(1)}, bf16[16,64,128]{2,1,0:T(8,128)(2,1)S(1)}, u32[]{:S(2)}, u32[]{:S(2)}) %collective-permute-start.25) | collective-permute-done | bytes 262176 | tf_op jit(solution)/shard_map/ppermute | solution.py:370
  101.6 1.6 %mix_last.1 = bf16[2048,256]{1,0:T(8,128)(2,1)} custom-call(bf16[256,256]{1,0:T(8,128)(2,1)S(1)} %collective-permute-done.refs_17_.refs_0_, bf16[256,256]{1,0:T(8,128)(2,1)S(1)} %collective-permute-done.1.refs_18_.refs_1_, bf16[16,96,128]{2,1,0:T(8,128)(2,1)S(1)} %collective-permute-done.12.refs_2_, ...), custom_call_target="tpu_custom_call" | custom-call | flops 536870912 | bytes 4194304 | tf_op jit(solution)/shard_map/mix_last/pallas_call | solution.py:357
  (36 shorter events, 0.1 us)
Async XLA Ops:
  0.0 1.2 %copy-start.1 = (bf16[2048,256]{1,0:T(8,128)(2,1)S(1)}, bf16[2048,256]{1,0:T(8,128)(2,1)}, u32[]{:S(2)}) copy-start(bf16[2048,256]{1,0:T(8,128)(2,1)} %f_ref.1) | copy-start | bytes 3145732
  1.2 9.1 %copy-start.4 = (bf16[256,1024]{1,0:T(8,128)(2,1)S(1)}, bf16[256,1024]{1,0:T(8,128)(2,1)}, u32[]{:S(2)}) copy-start(bf16[256,1024]{1,0:T(8,128)(2,1)} %w_ref.1) | copy-start | bytes 1572868
  1.2 9.2 %copy-start.17 = (f32[256]{0:T(256)S(1)}, f32[256]{0:T(256)}, u32[]{:S(2)}) copy-start(f32[256]{0:T(256)} %param.14) | copy-start | bytes 3076
  3.1 45.7 %all-to-all-start = ((bf16[8,32,16,128]{3,2,1,0:T(8,128)(2,1)}), bf16[8,32,16,128]{3,2,1,0:T(8,128)(2,1)S(1)}, u32[]{:S(2)}, u32[]{:S(2)}) async-start(bf16[8,32,16,128]{3,2,1,0:T(8,128)(2,1)} %filter_blocks.1._), calls=%async_computation | async-start | bytes 2097152 | tf_op jit(solution)/shard_map/all_to_all | solution.py:380
  10.7 14.6 %collective-permute-start = (bf16[256,256]{1,0:T(8,128)(2,1)S(1)}, bf16[256,256]{1,0:T(8,128)(2,1)S(1)}, u32[]{:S(2)}, u32[]{:S(2)}) collective-permute-start(bf16[256,256]{1,0:T(8,128)(2,1)S(1)} %get-tuple-element.30), channel_id=1, source_target_pairs={{0,2},{1,3},{2,0},{3,1},{4,6},{5,7},{6,4},{7,5},{8,10},{9,11},{10,... | collective-permute-start | bytes 393224 | tf_op jit(solution)/shard_map/ppermute | solution.py:370
  12.2 13.1 %collective-permute-start.1 = (bf16[256,256]{1,0:T(8,128)(2,1)S(1)}, bf16[256,256]{1,0:T(8,128)(2,1)S(1)}, u32[]{:S(2)}, u32[]{:S(2)}) collective-permute-start(bf16[256,256]{1,0:T(8,128)(2,1)S(1)} %get-tuple-element.31), channel_id=1, source_target_pairs={{0,3},{1,2},{2,1},{3,0},{4,7},{5,6},{6,5},{7,4},{8,11},{9,10},{10,... | collective-permute-start | bytes 393224 | tf_op jit(solution)/shard_map/ppermute | solution.py:370
  12.2 15.9 %collective-permute-start.9 = (bf16[256,256]{1,0:T(8,128)(2,1)S(1)}, bf16[256,256]{1,0:T(8,128)(2,1)S(1)}, u32[]{:S(2)}, u32[]{:S(2)}) collective-permute-start(bf16[256,256]{1,0:T(8,128)(2,1)S(1)} %get-tuple-element.43), channel_id=1, source_target_pairs={{0,1},{1,0},{2,3},{3,2},{4,5},{5,4},{6,7},{7,6},{8,9},{9,8},{10,11... | collective-permute-start | bytes 393224 | tf_op jit(solution)/shard_map/ppermute | solution.py:370
  12.9 36.0 %copy-start.3 = (bf16[256,256]{1,0:T(8,128)(2,1)S(1)}, bf16[256,256]{1,0:T(8,128)(2,1)}, u32[]{:S(2)}) copy-start(bf16[256,256]{1,0:T(8,128)(2,1)} %constant.19.b_fwd.refs_10_) | copy-start | bytes 393220
  12.9 36.0 %copy-start.5 = (bf16[256,128]{1,0:T(8,128)(2,1)S(1)}, bf16[256,128]{1,0:T(8,128)(2,1)}, u32[]{:S(2)}) copy-start(bf16[256,128]{1,0:T(8,128)(2,1)} %constant.18.a_fwd.refs_9_) | copy-start | bytes 196612
  12.9 36.0 %copy-start.6 = (f32[128,128]{1,0:T(8,128)S(1)}, f32[128,128]{1,0:T(8,128)}, u32[]{:S(2)}) copy-start(f32[128,128]{1,0:T(8,128)} %constant.17.clone.ts_ref.refs_14_) | copy-start | bytes 196612
  12.9 36.0 %copy-start.7 = (f32[128,128]{1,0:T(8,128)S(1)}, f32[128,128]{1,0:T(8,128)}, u32[]{:S(2)}) copy-start(f32[128,128]{1,0:T(8,128)} %constant.16.clone.tc_ref.refs_13_) | copy-start | bytes 196612
  21.7 33.2 %copy-start.2 = (bf16[32,16,128]{2,1,0:T(8,128)(2,1)S(1)}, bf16[32,16,128]{2,1,0:T(8,128)(2,1)}, u32[]{:S(2)}) copy-start(bf16[32,16,128]{2,1,0:T(8,128)(2,1)} %get-tuple-element.34.refs_0_.refs_5_) | copy-start | bytes 393220
  21.7 33.3 %copy-start.13 = (bf16[256,256]{1,0:T(8,128)(2,1)S(1)}, bf16[256,256]{1,0:T(8,128)(2,1)}, u32[]{:S(2)}) copy-start(bf16[256,256]{1,0:T(8,128)(2,1)} %constant.20.refs_11_) | copy-start | bytes 393220
  21.7 33.3 %copy-start.16 = (bf16[128,256]{1,0:T(8,128)(2,1)S(1)}, bf16[128,256]{1,0:T(8,128)(2,1)}, u32[]{:S(2)}) copy-start(bf16[128,256]{1,0:T(8,128)(2,1)} %constant.21.refs_12_) | copy-start | bytes 196612
  21.7 8.3 %collective-permute-start.2 = (bf16[32,16,128]{2,1,0:T(8,128)(2,1)}, bf16[32,16,128]{2,1,0:T(8,128)(2,1)S(1)}, u32[]{:S(2)}, u32[]{:S(2)}) collective-permute-start(bf16[32,16,128]{2,1,0:T(8,128)(2,1)} %get-tuple-element.35.refs_5_), channel_id=1, source_target_pairs={{0,4},{4,0},{8,12},{12,8},{16,20},{20,16},{24,28},{28,24},{1,5},{5... | collective-permute-start | bytes 393224 | tf_op jit(solution)/shard_map/ppermute | solution.py:370
  23.8 9.8 %collective-permute-start.3 = (bf16[32,16,128]{2,1,0:T(8,128)(2,1)}, bf16[32,16,128]{2,1,0:T(8,128)(2,1)S(1)}, u32[]{:S(2)}, u32[]{:S(2)}) collective-permute-start(bf16[32,16,128]{2,1,0:T(8,128)(2,1)} %get-tuple-element.36.refs_3_), channel_id=1, source_target_pairs={{0,8},{4,12},{8,0},{12,4},{16,24},{20,28},{24,16},{28,20},{1,9},{5... | collective-permute-start | bytes 393224 | tf_op jit(solution)/shard_map/ppermute | solution.py:370
  25.2 25.1 %collective-permute-start.4 = (bf16[32,16,128]{2,1,0:T(8,128)(2,1)}, bf16[32,16,128]{2,1,0:T(8,128)(2,1)S(1)}, u32[]{:S(2)}, u32[]{:S(2)}) collective-permute-start(bf16[32,16,128]{2,1,0:T(8,128)(2,1)} %get-tuple-element.37.refs_4_), channel_id=1, source_target_pairs={{0,12},{4,8},{8,4},{12,0},{16,28},{20,24},{24,20},{28,16},{1,13},{... | collective-permute-start | bytes 393224 | tf_op jit(solution)/shard_map/ppermute | solution.py:370
  25.3 26.3 %collective-permute-start.5 = (bf16[32,16,128]{2,1,0:T(8,128)(2,1)}, bf16[32,16,128]{2,1,0:T(8,128)(2,1)S(1)}, u32[]{:S(2)}, u32[]{:S(2)}) collective-permute-start(bf16[32,16,128]{2,1,0:T(8,128)(2,1)} %get-tuple-element.38.refs_3_), channel_id=1, source_target_pairs={{0,16},{4,20},{8,24},{12,28},{16,0},{20,4},{24,8},{28,12},{1,17},{... | collective-permute-start | bytes 393224 | tf_op jit(solution)/shard_map/ppermute | solution.py:370
  28.2 26.7 %collective-permute-start.6 = (bf16[32,16,128]{2,1,0:T(8,128)(2,1)}, bf16[32,16,128]{2,1,0:T(8,128)(2,1)S(1)}, u32[]{:S(2)}, u32[]{:S(2)}) collective-permute-start(bf16[32,16,128]{2,1,0:T(8,128)(2,1)} %get-tuple-element.39.refs_4_), channel_id=1, source_target_pairs={{0,20},{4,16},{8,28},{12,24},{16,4},{20,0},{24,12},{28,8},{1,21},{... | collective-permute-start | bytes 393224 | tf_op jit(solution)/shard_map/ppermute | solution.py:370
  30.0 24.9 %collective-permute-start.7 = (bf16[32,16,128]{2,1,0:T(8,128)(2,1)}, bf16[32,16,128]{2,1,0:T(8,128)(2,1)S(1)}, u32[]{:S(2)}, u32[]{:S(2)}) collective-permute-start(bf16[32,16,128]{2,1,0:T(8,128)(2,1)} %get-tuple-element.40.refs_2_), channel_id=1, source_target_pairs={{0,24},{4,28},{8,16},{12,20},{16,8},{20,12},{24,0},{28,4},{1,25},{... | collective-permute-start | bytes 393224 | tf_op jit(solution)/shard_map/ppermute | solution.py:370
  33.5 21.4 %collective-permute-start.8 = (bf16[32,16,128]{2,1,0:T(8,128)(2,1)}, bf16[32,16,128]{2,1,0:T(8,128)(2,1)S(1)}, u32[]{:S(2)}, u32[]{:S(2)}) collective-permute-start(bf16[32,16,128]{2,1,0:T(8,128)(2,1)} %get-tuple-element.41.refs_3_), channel_id=1, source_target_pairs={{0,28},{4,24},{8,20},{12,16},{16,12},{20,8},{24,4},{28,0},{1,29},{... | collective-permute-start | bytes 393224 | tf_op jit(solution)/shard_map/ppermute | solution.py:370
  50.3 21.1 %copy-start = (bf16[8,32,16,128]{3,2,1,0:T(8,128)(2,1)S(1)}, bf16[8,32,16,128]{3,2,1,0:T(8,128)(2,1)}, u32[]{:S(2)}) copy-start(bf16[8,32,16,128]{3,2,1,0:T(8,128)(2,1)} %get-tuple-element.32.gates) | copy-start | bytes 3145732
  50.3 21.1 %copy-start.10 = (bf16[32,16,128]{2,1,0:T(8,128)(2,1)S(1)}, bf16[32,16,128]{2,1,0:T(8,128)(2,1)}, u32[]{:S(2)}) copy-start(bf16[32,16,128]{2,1,0:T(8,128)(2,1)} %get-tuple-element.35.refs_5_) | copy-start | bytes 393220
  50.3 21.1 %copy-start.11 = (bf16[32,16,128]{2,1,0:T(8,128)(2,1)S(1)}, bf16[32,16,128]{2,1,0:T(8,128)(2,1)}, u32[]{:S(2)}) copy-start(bf16[32,16,128]{2,1,0:T(8,128)(2,1)} %get-tuple-element.36.refs_3_) | copy-start | bytes 393220
  50.3 21.1 %copy-start.12 = (bf16[32,16,128]{2,1,0:T(8,128)(2,1)S(1)}, bf16[32,16,128]{2,1,0:T(8,128)(2,1)}, u32[]{:S(2)}) copy-start(bf16[32,16,128]{2,1,0:T(8,128)(2,1)} %get-tuple-element.37.refs_4_) | copy-start | bytes 393220
  54.9 23.7 %copy-start.8 = (bf16[32,16,128]{2,1,0:T(8,128)(2,1)S(1)}, bf16[32,16,128]{2,1,0:T(8,128)(2,1)}, u32[]{:S(2)}) copy-start(bf16[32,16,128]{2,1,0:T(8,128)(2,1)} %get-tuple-element.38.refs_3_) | copy-start | bytes 393220
  54.9 23.6 %copy-start.9 = (bf16[32,16,128]{2,1,0:T(8,128)(2,1)S(1)}, bf16[32,16,128]{2,1,0:T(8,128)(2,1)}, u32[]{:S(2)}) copy-start(bf16[32,16,128]{2,1,0:T(8,128)(2,1)} %get-tuple-element.39.refs_4_) | copy-start | bytes 393220
  55.0 34.9 %copy-start.14 = (bf16[32,16,128]{2,1,0:T(8,128)(2,1)S(1)}, bf16[32,16,128]{2,1,0:T(8,128)(2,1)}, u32[]{:S(2)}) copy-start(bf16[32,16,128]{2,1,0:T(8,128)(2,1)} %get-tuple-element.40.refs_2_) | copy-start | bytes 393220
  55.0 34.9 %copy-start.15 = (bf16[32,16,128]{2,1,0:T(8,128)(2,1)S(1)}, bf16[32,16,128]{2,1,0:T(8,128)(2,1)}, u32[]{:S(2)}) copy-start(bf16[32,16,128]{2,1,0:T(8,128)(2,1)} %get-tuple-element.41.refs_3_) | copy-start | bytes 393220
  57.5 10.7 %collective-permute-start.15 = (bf16[32,16,128]{2,1,0:T(8,128)(2,1)S(1)}, bf16[32,16,128]{2,1,0:T(8,128)(2,1)S(1)}, u32[]{:S(2)}, u32[]{:S(2)}) collective-permute-start(bf16[32,16,128]{2,1,0:T(8,128)(2,1)S(1)} %get-tuple-element.50), channel_id=1, source_target_pairs={{0,8},{4,12},{8,0},{12,4},{16,24},{20,28},{24,16},{28,20},{1,9},{5... | collective-permute-start | bytes 393224 | tf_op jit(solution)/shard_map/ppermute | solution.py:370
  62.7 8.7 %collective-permute-start.16 = (bf16[32,16,128]{2,1,0:T(8,128)(2,1)S(1)}, bf16[32,16,128]{2,1,0:T(8,128)(2,1)S(1)}, u32[]{:S(2)}, u32[]{:S(2)}) collective-permute-start(bf16[32,16,128]{2,1,0:T(8,128)(2,1)S(1)} %get-tuple-element.51), channel_id=1, source_target_pairs={{0,12},{4,8},{8,4},{12,0},{16,28},{20,24},{24,20},{28,16},{1,13},{... | collective-permute-start | bytes 393224 | tf_op jit(solution)/shard_map/ppermute | solution.py:370
  62.8 8.5 %collective-permute-start.17 = (bf16[32,16,128]{2,1,0:T(8,128)(2,1)S(1)}, bf16[32,16,128]{2,1,0:T(8,128)(2,1)S(1)}, u32[]{:S(2)}, u32[]{:S(2)}) collective-permute-start(bf16[32,16,128]{2,1,0:T(8,128)(2,1)S(1)} %get-tuple-element.52), channel_id=1, source_target_pairs={{0,4},{4,0},{8,12},{12,8},{16,20},{20,16},{24,28},{28,24},{1,5},{5... | collective-permute-start | bytes 393224 | tf_op jit(solution)/shard_map/ppermute | solution.py:370
  64.2 12.6 %collective-permute-start.10 = (bf16[32,16,128]{2,1,0:T(8,128)(2,1)S(1)}, bf16[32,16,128]{2,1,0:T(8,128)(2,1)S(1)}, u32[]{:S(2)}, u32[]{:S(2)}) collective-permute-start(bf16[32,16,128]{2,1,0:T(8,128)(2,1)S(1)} %get-tuple-element.44), channel_id=1, source_target_pairs={{0,16},{4,20},{8,24},{12,28},{16,0},{20,4},{24,8},{28,12},{1,17},{... | collective-permute-start | bytes 393224 | tf_op jit(solution)/shard_map/ppermute | solution.py:370
  66.2 12.4 %collective-permute-start.11 = (bf16[32,16,128]{2,1,0:T(8,128)(2,1)S(1)}, bf16[32,16,128]{2,1,0:T(8,128)(2,1)S(1)}, u32[]{:S(2)}, u32[]{:S(2)}) collective-permute-start(bf16[32,16,128]{2,1,0:T(8,128)(2,1)S(1)} %get-tuple-element.45), channel_id=1, source_target_pairs={{0,20},{4,16},{8,28},{12,24},{16,4},{20,0},{24,12},{28,8},{1,21},{... | collective-permute-start | bytes 393224 | tf_op jit(solution)/shard_map/ppermute | solution.py:370
  71.9 18.9 %collective-permute-start.18 = (bf16[16,96,128]{2,1,0:T(8,128)(2,1)S(1)}, bf16[16,96,128]{2,1,0:T(8,128)(2,1)S(1)}, u32[]{:S(2)}, u32[]{:S(2)}) collective-permute-start(bf16[16,96,128]{2,1,0:T(8,128)(2,1)S(1)} %apply_gate.5.refs_3_), channel_id=1, source_target_pairs={{0,2},{1,3},{2,0},{3,1},{4,6},{5,7},{6,4},{7,5},{8,10},{9,11},{10,... | collective-permute-start | bytes 1179656 | tf_op jit(solution)/shard_map/ppermute | solution.py:370
  79.1 12.2 %collective-permute-start.12 = (bf16[16,96,128]{2,1,0:T(8,128)(2,1)S(1)}, bf16[16,96,128]{2,1,0:T(8,128)(2,1)S(1)}, u32[]{:S(2)}, u32[]{:S(2)}) collective-permute-start(bf16[16,96,128]{2,1,0:T(8,128)(2,1)S(1)} %apply_gate.3.refs_2_), channel_id=1, source_target_pairs={{0,2},{1,3},{2,0},{3,1},{4,6},{5,7},{6,4},{7,5},{8,10},{9,11},{10,... | collective-permute-start | bytes 1179656 | tf_op jit(solution)/shard_map/ppermute | solution.py:370
  80.6 7.7 %collective-permute-start.13 = (bf16[32,16,128]{2,1,0:T(8,128)(2,1)S(1)}, bf16[32,16,128]{2,1,0:T(8,128)(2,1)S(1)}, u32[]{:S(2)}, u32[]{:S(2)}) collective-permute-start(bf16[32,16,128]{2,1,0:T(8,128)(2,1)S(1)} %get-tuple-element.47), channel_id=1, source_target_pairs={{0,24},{4,28},{8,16},{12,20},{16,8},{20,12},{24,0},{28,4},{1,25},{... | collective-permute-start | bytes 393224 | tf_op jit(solution)/shard_map/ppermute | solution.py:370
  81.8 8.0 %collective-permute-start.14 = (bf16[32,16,128]{2,1,0:T(8,128)(2,1)S(1)}, bf16[32,16,128]{2,1,0:T(8,128)(2,1)S(1)}, u32[]{:S(2)}, u32[]{:S(2)}) collective-permute-start(bf16[32,16,128]{2,1,0:T(8,128)(2,1)S(1)} %get-tuple-element.48), channel_id=1, source_target_pairs={{0,28},{4,24},{8,20},{12,16},{16,12},{20,8},{24,4},{28,0},{1,29},{... | collective-permute-start | bytes 393224 | tf_op jit(solution)/shard_map/ppermute | solution.py:370
  90.1 1.6 %collective-permute-start.22 = (bf16[16,64,128]{2,1,0:T(8,128)(2,1)S(1)}, bf16[16,64,128]{2,1,0:T(8,128)(2,1)S(1)}, u32[]{:S(2)}, u32[]{:S(2)}) collective-permute-start(bf16[16,64,128]{2,1,0:T(8,128)(2,1)S(1)} %apply_gate.4.refs_4_), channel_id=1, source_target_pairs={{0,1},{1,0},{2,3},{3,2},{4,5},{5,4},{6,7},{7,6},{8,9},{9,8},{10,11... | collective-permute-start | bytes 786440 | tf_op jit(solution)/shard_map/ppermute | solution.py:370
  90.2 2.1 %collective-permute-start.21 = (bf16[16,96,128]{2,1,0:T(8,128)(2,1)S(1)}, bf16[16,96,128]{2,1,0:T(8,128)(2,1)S(1)}, u32[]{:S(2)}, u32[]{:S(2)}) collective-permute-start(bf16[16,96,128]{2,1,0:T(8,128)(2,1)S(1)} %apply_gate.5.refs_3_), channel_id=1, source_target_pairs={{0,1},{1,0},{2,3},{3,2},{4,5},{5,4},{6,7},{7,6},{8,9},{9,8},{10,11... | collective-permute-start | bytes 1179656 | tf_op jit(solution)/shard_map/ppermute | solution.py:370
  90.7 2.1 %collective-permute-start.20 = (bf16[16,96,128]{2,1,0:T(8,128)(2,1)S(1)}, bf16[16,96,128]{2,1,0:T(8,128)(2,1)S(1)}, u32[]{:S(2)}, u32[]{:S(2)}) collective-permute-start(bf16[16,96,128]{2,1,0:T(8,128)(2,1)S(1)} %apply_gate.3.refs_2_), channel_id=1, source_target_pairs={{0,1},{1,0},{2,3},{3,2},{4,5},{5,4},{6,7},{7,6},{8,9},{9,8},{10,11... | collective-permute-start | bytes 1179656 | tf_op jit(solution)/shard_map/ppermute | solution.py:370
  90.8 9.3 %collective-permute-start.24 = (bf16[16,96,128]{2,1,0:T(8,128)(2,1)S(1)}, bf16[16,96,128]{2,1,0:T(8,128)(2,1)S(1)}, u32[]{:S(2)}, u32[]{:S(2)}) collective-permute-start(bf16[16,96,128]{2,1,0:T(8,128)(2,1)S(1)} %collective-permute-done.18.refs_3_), channel_id=1, source_target_pairs={{0,1},{1,0},{2,3},{3,2},{4,5},{5,4},{6,7},{7,6},{8,9},{9,8},{10,11... | collective-permute-start | bytes 1179656 | tf_op jit(solution)/shard_map/ppermute | solution.py:370
  91.2 8.9 %collective-permute-start.23 = (bf16[16,96,128]{2,1,0:T(8,128)(2,1)S(1)}, bf16[16,96,128]{2,1,0:T(8,128)(2,1)S(1)}, u32[]{:S(2)}, u32[]{:S(2)}) collective-permute-start(bf16[16,96,128]{2,1,0:T(8,128)(2,1)S(1)} %collective-permute-done.12.refs_2_), channel_id=1, source_target_pairs={{0,1},{1,0},{2,3},{3,2},{4,5},{5,4},{6,7},{7,6},{8,9},{9,8},{10,11... | collective-permute-start | bytes 1179656 | tf_op jit(solution)/shard_map/ppermute | solution.py:370
  91.7 8.3 %collective-permute-start.19 = (bf16[16,64,128]{2,1,0:T(8,128)(2,1)S(1)}, bf16[16,64,128]{2,1,0:T(8,128)(2,1)S(1)}, u32[]{:S(2)}, u32[]{:S(2)}) collective-permute-start(bf16[16,64,128]{2,1,0:T(8,128)(2,1)S(1)} %apply_gate.4.refs_4_), channel_id=1, source_target_pairs={{0,2},{1,3},{2,0},{3,1},{4,6},{5,7},{6,4},{7,5},{8,10},{9,11},{10,... | collective-permute-start | bytes 786440 | tf_op jit(solution)/shard_map/ppermute | solution.py:370
  100.1 1.5 %collective-permute-start.25 = (bf16[16,64,128]{2,1,0:T(8,128)(2,1)S(1)}, bf16[16,64,128]{2,1,0:T(8,128)(2,1)S(1)}, u32[]{:S(2)}, u32[]{:S(2)}) collective-permute-start(bf16[16,64,128]{2,1,0:T(8,128)(2,1)S(1)} %collective-permute-done.19.refs_4_), channel_id=1, source_target_pairs={{0,1},{1,0},{2,3},{3,2},{4,5},{5,4},{6,7},{7,6},{8,9},{9,8},{10,11... | collective-permute-start | bytes 786440 | tf_op jit(solution)/shard_map/ppermute | solution.py:370

commit v4 on v3

--- a/solution.py
+++ b/solution.py
@@ -56,6 +56,10 @@
     return [jax.ShapeDtypeStruct((cpc, rows, LANES), BF16)] * seq
 
 
+def strided_scratch(chans, rows):
+    return pltpu.VMEM((chans * rows + rows, LANES), F32)
+
+
 def whole(shape):
     return pl.BlockSpec(tuple(shape), lambda i: (0,) * len(shape))
 
@@ -84,7 +88,7 @@
     return pl.pallas_call(
         functools.partial(filter_kernel, seq),
         out_shape=jax.ShapeDtypeStruct((seq, chans // seq, rows, LANES), BF16),
-        scratch_shapes=[pltpu.VMEM((chans * rows, LANES), F32)],
+        scratch_shapes=[strided_scratch(chans, rows)],
         compiler_params=params(12),
         cost_estimate=cost(0, 8 * frames * chans),
         name="filter_blocks",
@@ -135,7 +139,7 @@
         ],
         out_specs=[whole(v.shape) for v in out_shape],
         out_shape=out_shape,
-        scratch_shapes=[pltpu.VMEM((chans * rows, LANES), F32)] * 2,
+        scratch_shapes=[strided_scratch(chans, rows)] * 2,
         compiler_params=params(58),
         cost_estimate=cost(6 * frames * width * chans, 16 * 1024 * 1024),
         name="project",
@@ -265,7 +269,7 @@
     return pl.pallas_call(
         functools.partial(gate_kernel, group),
         out_shape=jax.ShapeDtypeStruct((rows, chans, LANES), BF16),
-        scratch_shapes=[pltpu.VMEM((chans * rows, LANES), F32)],
+        scratch_shapes=[strided_scratch(chans, rows)],
         compiler_params=params(SMALL),
         cost_estimate=cost(0, 10 * rows * chans * LANES),
         name="apply_gate",

time: 103 us -> 103 us (level)
  no operation moved by 1% of the time
where the time goes in v4:
time: 103 us
  starting transfers between devices  42.5 us (41%)
  waiting for transfers between devices  40.9 us (40%)
  Pallas kernels  18.3 us (18%)
  local copies, waits for them, and re-layouts  1.29 us (1%)
    ppermute x26, starting transfers between devices, swap(): return lax.ppermute(value, axis, [(i, i ^ step) for i in range(size)])  35.2 us
    ppermute x26, waiting for transfers between devices, swap(): return lax.ppermute(value, axis, [(i, i ^ step) for i in range(size)])  28.2 us
    all_to_all x1, waiting for transfers between devices, on_device(): lax.all_to_all(filt_sends, 'seq', split_axis=0, concat_axis=0, tiled=True)  12.6 us
    pallas_call x1, Pallas kernels, project(): pl.pallas_call(functools.partial(project_kernel, seq), grid=(frames // ti...  8.78 us
    all_to_all x1, starting transfers between devices, on_device(): lax.all_to_all(filt_sends, 'seq', split_axis=0, concat_axis=0, tiled=True)  7.28 us
    pallas_call x1, Pallas kernels, convolve(): pl.pallas_call(functools.partial(conv_kernel, seq, len(ready)), in_specs=...  2.51 us
  transfers between devices with their start and end apart: 27, of which 14 were waited for; matrix products, arithmetic and copies ran while one was open for 0% of the time, Pallas kernels for 12%

profile of v4, /device:TPU:0, one launch (start us, length us, event | category | flops | bytes accessed | tf_op | source)
XLA Modules:
  0.0 103.2 jit_solution(3692286119607805313)
XLA Ops:
  0.0 1.2 %copy-done.1 = bf16[2048,256]{1,0:T(8,128)(2,1)S(1)} copy-done((bf16[2048,256]{1,0:T(8,128)(2,1)S(1)}, bf16[2048,256]{1,0:T(8,128)(2,1)}, u32[]{:S(2)}) %copy-start.1) | copy-done | bytes 1048600
  1.2 1.9 %filter_blocks.1._ = bf16[8,32,16,128]{3,2,1,0:T(8,128)(2,1)} custom-call(bf16[2048,256]{1,0:T(8,128)(2,1)S(1)} %copy-done.1), custom_call_target="tpu_custom_call" | custom-call | bytes 4194304 | tf_op jit(solution)/shard_map/filter_blocks/pallas_call | solution.py:88
  3.1 7.3 %all-to-all-start = ((bf16[8,32,16,128]{3,2,1,0:T(8,128)(2,1)}), bf16[8,32,16,128]{3,2,1,0:T(8,128)(2,1)S(1)}, u32[]{:S(2)}, u32[]{:S(2)}) async-start(bf16[8,32,16,128]{3,2,1,0:T(8,128)(2,1)} %filter_blocks.1._), calls=%async_computation | async-start | bytes 2097152 | tf_op jit(solution)/shard_map/all_to_all | solution.py:384
  10.4 0.3 out_weights.1
  10.7 1.6 %collective-permute-start = (bf16[256,256]{1,0:T(8,128)(2,1)S(1)}, bf16[256,256]{1,0:T(8,128)(2,1)S(1)}, u32[]{:S(2)}, u32[]{:S(2)}) collective-permute-start(bf16[256,256]{1,0:T(8,128)(2,1)S(1)} %get-tuple-element.30), channel_id=1, source_target_pairs={{0,2},{1,3},{2,0},{3,1},{4,6},{5,7},{6,4},{7,5},{8,10},{9,11},{10,... | collective-permute-start | bytes 393224 | tf_op jit(solution)/shard_map/ppermute | solution.py:374
  12.2 0.0 collective-permute-start.1
  12.2 0.6 collective-permute-start.9
  12.9 8.8 %project.1 = (bf16[8,32,16,128]{3,2,1,0:T(8,128)(2,1)}, bf16[32,16,128]{2,1,0:T(8,128)(2,1)}, bf16[32,16,128]{2,1,0:T(8,128)(2,1)}, bf16[32,16,128]{2,1,0:T(8,12...) custom-call(bf16[2048,1024]{1,0:T(8,128)(2,1)} %x_ref.1, ...), custom_call_target="tpu_custom_call" | custom-call | flops 3221225472 | bytes 16777216 | tf_op jit(solution)/shard_map/project/pallas_call | solution.py:132
  21.7 2.1 %collective-permute-start.2 = (bf16[32,16,128]{2,1,0:T(8,128)(2,1)}, bf16[32,16,128]{2,1,0:T(8,128)(2,1)S(1)}, u32[]{:S(2)}, u32[]{:S(2)}) collective-permute-start(bf16[32,16,128]{2,1,0:T(8,128)(2,1)} %get-tuple-element.35.refs_5_), channel_id=1, source_target_pairs={{0,4},{4,0},{8,12},{12,8},{16,20},{20,16},{24,28},{28,24},{1,5},{5... | collective-permute-start | bytes 393224 | tf_op jit(solution)/shard_map/ppermute | solution.py:374
  23.8 1.5 %collective-permute-start.3 = (bf16[32,16,128]{2,1,0:T(8,128)(2,1)}, bf16[32,16,128]{2,1,0:T(8,128)(2,1)S(1)}, u32[]{:S(2)}, u32[]{:S(2)}) collective-permute-start(bf16[32,16,128]{2,1,0:T(8,128)(2,1)} %get-tuple-element.36.refs_3_), channel_id=1, source_target_pairs={{0,8},{4,12},{8,0},{12,4},{16,24},{20,28},{24,16},{28,20},{1,9},{5... | collective-permute-start | bytes 393224 | tf_op jit(solution)/shard_map/ppermute | solution.py:374
  25.2 0.0 collective-permute-done.refs_17_.refs_0_
  25.2 0.1 collective-permute-start.4
  25.3 0.0 collective-permute-done.1.refs_18_.refs_1_
  25.3 2.8 %collective-permute-start.5 = (bf16[32,16,128]{2,1,0:T(8,128)(2,1)}, bf16[32,16,128]{2,1,0:T(8,128)(2,1)S(1)}, u32[]{:S(2)}, u32[]{:S(2)}) collective-permute-start(bf16[32,16,128]{2,1,0:T(8,128)(2,1)} %get-tuple-element.38.refs_3_), channel_id=1, source_target_pairs={{0,16},{4,20},{8,24},{12,28},{16,0},{20,4},{24,8},{28,12},{1,17},{... | collective-permute-start | bytes 393224 | tf_op jit(solution)/shard_map/ppermute | solution.py:374
  28.2 0.0 collective-permute-done.9.refs_16_.refs_1_
  28.2 1.5 %collective-permute-start.6 = (bf16[32,16,128]{2,1,0:T(8,128)(2,1)}, bf16[32,16,128]{2,1,0:T(8,128)(2,1)S(1)}, u32[]{:S(2)}, u32[]{:S(2)}) collective-permute-start(bf16[32,16,128]{2,1,0:T(8,128)(2,1)} %get-tuple-element.39.refs_4_), channel_id=1, source_target_pairs={{0,20},{4,16},{8,28},{12,24},{16,4},{20,0},{24,12},{28,8},{1,21},{... | collective-permute-start | bytes 393224 | tf_op jit(solution)/shard_map/ppermute | solution.py:374
  29.6 0.4 collective-permute-done.2.refs_1_
  30.0 3.5 %collective-permute-start.7 = (bf16[32,16,128]{2,1,0:T(8,128)(2,1)}, bf16[32,16,128]{2,1,0:T(8,128)(2,1)S(1)}, u32[]{:S(2)}, u32[]{:S(2)}) collective-permute-start(bf16[32,16,128]{2,1,0:T(8,128)(2,1)} %get-tuple-element.40.refs_2_), channel_id=1, source_target_pairs={{0,24},{4,28},{8,16},{12,20},{16,8},{20,12},{24,0},{28,4},{1,25},{... | collective-permute-start | bytes 393224 | tf_op jit(solution)/shard_map/ppermute | solution.py:374
  33.5 0.0 collective-permute-done.3.refs_2_
  33.5 2.7 %collective-permute-start.8 = (bf16[32,16,128]{2,1,0:T(8,128)(2,1)}, bf16[32,16,128]{2,1,0:T(8,128)(2,1)S(1)}, u32[]{:S(2)}, u32[]{:S(2)}) collective-permute-start(bf16[32,16,128]{2,1,0:T(8,128)(2,1)} %get-tuple-element.41.refs_3_), channel_id=1, source_target_pairs={{0,28},{4,24},{8,20},{12,16},{16,12},{20,8},{24,4},{28,0},{1,29},{... | collective-permute-start | bytes 393224 | tf_op jit(solution)/shard_map/ppermute | solution.py:374
  36.2 12.6 %all-to-all-done.f_ref = bf16[8,32,16,128]{3,2,1,0:T(8,128)(2,1)S(1)} async-done(((bf16[8,32,16,128]{3,2,1,0:T(8,128)(2,1)}), bf16[8,32,16,128]{3,2,1,0:T(8,128)(2,1)S(1)}, u32[]{:S(2)}, u32[]{:S(2)}) %all-to-all-start) | async-done | bytes 1048608 | tf_op jit(solution)/shard_map/all_to_all | solution.py:384
  48.9 1.4 %filter_spectra.1.refs_8_ = f32[32,128,256]{2,1,0:T(8,128)S(1)} custom-call(bf16[8,32,16,128]{3,2,1,0:T(8,128)(2,1)S(1)} %all-to-all-done.f_ref, bf16[256,128]{1,0:T(8,128)(2,1)S(1)} %copy-done.5, bf16[256,256]{1,0:T(8,128)(2,1)S(1)} %copy-done.3, f32[128,128]{1,0:T(8,128)S(1)} %copy-done.7, f32[128,128]{1,0:T(8,128)S(1)} %copy-done.6), custom_call_target="tpu_custom_call" | custom-call | flops 536870912 | bytes 5242880 | tf_op jit(solution)/shard_map/filter_spectra/pallas_call | solution.py:188
  50.3 0.0 collective-permute-done.4.refs_3_
  50.3 1.3 %collective-permute-done.5.refs_4_ = bf16[32,16,128]{2,1,0:T(8,128)(2,1)S(1)} collective-permute-done((bf16[32,16,128]{2,1,0:T(8,128)(2,1)}, bf16[32,16,128]{2,1,0:T(8,128)(2,1)S(1)}, u32[]{:S(2)}, u32[]{:S(2)}) %collective-permute-start.5) | collective-permute-done | bytes 131104 | tf_op jit(solution)/shard_map/ppermute | solution.py:374
  51.7 3.2 %collective-permute-done.6.refs_5_ = bf16[32,16,128]{2,1,0:T(8,128)(2,1)S(1)} collective-permute-done((bf16[32,16,128]{2,1,0:T(8,128)(2,1)}, bf16[32,16,128]{2,1,0:T(8,128)(2,1)S(1)}, u32[]{:S(2)}, u32[]{:S(2)}) %collective-permute-start.6) | collective-permute-done | bytes 131104 | tf_op jit(solution)/shard_map/ppermute | solution.py:374
  54.9 0.0 collective-permute-done.7.refs_6_
  54.9 0.0 collective-permute-done.8.refs_7_
  55.0 2.5 %convolve.1 = (bf16[32,16,128]{2,1,0:T(8,128)(2,1)S(1)}, bf16[32,16,128]{2,1,0:T(8,128)(2,1)S(1)}, bf16[32,16,128]{2,1,0:T(8,128)(2,1)S(1)}, bf16[32,16,128]{2,1...) custom-call(bf16[32,16,128]{2,1,0:T(8,128)(2,1)S(1)} %copy-done.2, ...), custom_call_target="tpu_custom_call" | custom-call | flops 1073741824 | bytes 6291456 | tf_op jit(solution)/shard_map/convolve/pallas_call | solution.py:240
  57.5 5.2 %collective-permute-start.15 = (bf16[32,16,128]{2,1,0:T(8,128)(2,1)S(1)}, bf16[32,16,128]{2,1,0:T(8,128)(2,1)S(1)}, u32[]{:S(2)}, u32[]{:S(2)}) collective-permute-start(bf16[32,16,128]{2,1,0:T(8,128)(2,1)S(1)} %get-tuple-element.50), channel_id=1, source_target_pairs={{0,8},{4,12},{8,0},{12,4},{16,24},{20,28},{24,16},{28,20},{1,9},{5... | collective-permute-start | bytes 393224 | tf_op jit(solution)/shard_map/ppermute | solution.py:374
  62.7 0.2 collective-permute-start.16
  62.8 1.4 %collective-permute-start.17 = (bf16[32,16,128]{2,1,0:T(8,128)(2,1)S(1)}, bf16[32,16,128]{2,1,0:T(8,128)(2,1)S(1)}, u32[]{:S(2)}, u32[]{:S(2)}) collective-permute-start(bf16[32,16,128]{2,1,0:T(8,128)(2,1)S(1)} %get-tuple-element.52), channel_id=1, source_target_pairs={{0,4},{4,0},{8,12},{12,8},{16,20},{20,16},{24,28},{28,24},{1,5},{5... | collective-permute-start | bytes 393224 | tf_op jit(solution)/shard_map/ppermute | solution.py:374
  64.2 1.9 %collective-permute-start.10 = (bf16[32,16,128]{2,1,0:T(8,128)(2,1)S(1)}, bf16[32,16,128]{2,1,0:T(8,128)(2,1)S(1)}, u32[]{:S(2)}, u32[]{:S(2)}) collective-permute-start(bf16[32,16,128]{2,1,0:T(8,128)(2,1)S(1)} %get-tuple-element.44), channel_id=1, source_target_pairs={{0,16},{4,20},{8,24},{12,28},{16,0},{20,4},{24,8},{28,12},{1,17},{... | collective-permute-start | bytes 393224 | tf_op jit(solution)/shard_map/ppermute | solution.py:374
  66.1 1.1 %collective-permute-start.11 = (bf16[32,16,128]{2,1,0:T(8,128)(2,1)S(1)}, bf16[32,16,128]{2,1,0:T(8,128)(2,1)S(1)}, u32[]{:S(2)}, u32[]{:S(2)}) collective-permute-start(bf16[32,16,128]{2,1,0:T(8,128)(2,1)S(1)} %get-tuple-element.45), channel_id=1, source_target_pairs={{0,20},{4,16},{8,28},{12,24},{16,4},{20,0},{24,12},{28,8},{1,21},{... | collective-permute-start | bytes 393224 | tf_op jit(solution)/shard_map/ppermute | solution.py:374
  67.2 1.0 collective-permute-done.15.refs_0_
  68.2 3.2 %collective-permute-done.16.refs_1_ = bf16[32,16,128]{2,1,0:T(8,128)(2,1)S(1)} collective-permute-done((bf16[32,16,128]{2,1,0:T(8,128)(2,1)S(1)}, bf16[32,16,128]{2,1,0:T(8,128)(2,1)S(1)}, u32[]{:S(2)}, u32[]{:S(2)}) %collective-permute-start.16) | collective-permute-done | bytes 131104 | tf_op jit(solution)/shard_map/ppermute | solution.py:374
  71.4 0.0 collective-permute-done.17.refs_2_
  71.4 0.5 apply_gate.5.refs_3_
  71.9 1.6 %collective-permute-start.18 = (bf16[16,96,128]{2,1,0:T(8,128)(2,1)S(1)}, bf16[16,96,128]{2,1,0:T(8,128)(2,1)S(1)}, u32[]{:S(2)}, u32[]{:S(2)}) collective-permute-start(bf16[16,96,128]{2,1,0:T(8,128)(2,1)S(1)} %apply_gate.5.refs_3_), channel_id=1, source_target_pairs={{0,2},{1,3},{2,0},{3,1},{4,6},{5,7},{6,4},{7,5},{8,10},{9,11},{10,... | collective-permute-start | bytes 1179656 | tf_op jit(solution)/shard_map/ppermute | solution.py:374
  73.4 3.4 %collective-permute-done.10.refs_0_ = bf16[32,16,128]{2,1,0:T(8,128)(2,1)S(1)} collective-permute-done((bf16[32,16,128]{2,1,0:T(8,128)(2,1)S(1)}, bf16[32,16,128]{2,1,0:T(8,128)(2,1)S(1)}, u32[]{:S(2)}, u32[]{:S(2)}) %collective-permute-start.10) | collective-permute-done | bytes 131104 | tf_op jit(solution)/shard_map/ppermute | solution.py:374
  76.8 1.8 %collective-permute-done.11.refs_1_ = bf16[32,16,128]{2,1,0:T(8,128)(2,1)S(1)} collective-permute-done((bf16[32,16,128]{2,1,0:T(8,128)(2,1)S(1)}, bf16[32,16,128]{2,1,0:T(8,128)(2,1)S(1)}, u32[]{:S(2)}, u32[]{:S(2)}) %collective-permute-start.11) | collective-permute-done | bytes 131104 | tf_op jit(solution)/shard_map/ppermute | solution.py:374
  78.6 0.5 apply_gate.3.refs_2_
  79.1 1.6 %collective-permute-start.12 = (bf16[16,96,128]{2,1,0:T(8,128)(2,1)S(1)}, bf16[16,96,128]{2,1,0:T(8,128)(2,1)S(1)}, u32[]{:S(2)}, u32[]{:S(2)}) collective-permute-start(bf16[16,96,128]{2,1,0:T(8,128)(2,1)S(1)} %apply_gate.3.refs_2_), channel_id=1, source_target_pairs={{0,2},{1,3},{2,0},{3,1},{4,6},{5,7},{6,4},{7,5},{8,10},{9,11},{10,... | collective-permute-start | bytes 1179656 | tf_op jit(solution)/shard_map/ppermute | solution.py:374
  80.6 1.2 %collective-permute-start.13 = (bf16[32,16,128]{2,1,0:T(8,128)(2,1)S(1)}, bf16[32,16,128]{2,1,0:T(8,128)(2,1)S(1)}, u32[]{:S(2)}, u32[]{:S(2)}) collective-permute-start(bf16[32,16,128]{2,1,0:T(8,128)(2,1)S(1)} %get-tuple-element.47), channel_id=1, source_target_pairs={{0,24},{4,28},{8,16},{12,20},{16,8},{20,12},{24,0},{28,4},{1,25},{... | collective-permute-start | bytes 393224 | tf_op jit(solution)/shard_map/ppermute | solution.py:374
  81.8 3.1 %collective-permute-start.14 = (bf16[32,16,128]{2,1,0:T(8,128)(2,1)S(1)}, bf16[32,16,128]{2,1,0:T(8,128)(2,1)S(1)}, u32[]{:S(2)}, u32[]{:S(2)}) collective-permute-start(bf16[32,16,128]{2,1,0:T(8,128)(2,1)S(1)} %get-tuple-element.48), channel_id=1, source_target_pairs={{0,28},{4,24},{8,20},{12,16},{16,12},{20,8},{24,4},{28,0},{1,29},{... | collective-permute-start | bytes 393224 | tf_op jit(solution)/shard_map/ppermute | solution.py:374
  84.9 3.4 %collective-permute-done.13.refs_0_ = bf16[32,16,128]{2,1,0:T(8,128)(2,1)S(1)} collective-permute-done((bf16[32,16,128]{2,1,0:T(8,128)(2,1)S(1)}, bf16[32,16,128]{2,1,0:T(8,128)(2,1)S(1)}, u32[]{:S(2)}, u32[]{:S(2)}) %collective-permute-start.13) | collective-permute-done | bytes 131104 | tf_op jit(solution)/shard_map/ppermute | solution.py:374
  88.3 1.5 %collective-permute-done.14.refs_1_ = bf16[32,16,128]{2,1,0:T(8,128)(2,1)S(1)} collective-permute-done((bf16[32,16,128]{2,1,0:T(8,128)(2,1)S(1)}, bf16[32,16,128]{2,1,0:T(8,128)(2,1)S(1)}, u32[]{:S(2)}, u32[]{:S(2)}) %collective-permute-start.14) | collective-permute-done | bytes 131104 | tf_op jit(solution)/shard_map/ppermute | solution.py:374
  89.8 0.3 apply_gate.4.refs_4_
  90.1 0.1 collective-permute-start.22
  90.2 0.5 collective-permute-start.21
  90.7 0.1 collective-permute-start.20
  90.8 0.0 collective-permute-done.18.refs_3_
  90.8 0.4 collective-permute-start.24
  91.2 0.0 collective-permute-done.12.refs_2_
  91.2 0.1 collective-permute-start.23
  91.3 0.4 collective-permute-done.22.refs_7_
  91.7 0.5 collective-permute-start.19
  92.3 0.0 collective-permute-done.21.refs_6_
  92.3 0.6 collective-permute-done.20.refs_5_
  92.9 0.7 mix_early.1.refs_8_
  93.6 6.5 %collective-permute-done.19.refs_4_ = bf16[16,64,128]{2,1,0:T(8,128)(2,1)S(1)} collective-permute-done((bf16[16,64,128]{2,1,0:T(8,128)(2,1)S(1)}, bf16[16,64,128]{2,1,0:T(8,128)(2,1)S(1)}, u32[]{:S(2)}, u32[]{:S(2)}) %collective-permute-start.19) | collective-permute-done | bytes 262176 | tf_op jit(solution)/shard_map/ppermute | solution.py:374
  100.1 0.0 collective-permute-done.24.refs_6_
  100.1 0.0 collective-permute-done.23.refs_5_
  100.1 1.5 %collective-permute-done.25.refs_7_ = bf16[16,64,128]{2,1,0:T(8,128)(2,1)S(1)} collective-permute-done((bf16[16,64,128]{2,1,0:T(8,128)(2,1)S(1)}, bf16[16,64,128]{2,1,0:T(8,128)(2,1)S(1)}, u32[]{:S(2)}, u32[]{:S(2)}) %collective-permute-start.25) | collective-permute-done | bytes 262176 | tf_op jit(solution)/shard_map/ppermute | solution.py:374
  101.6 1.6 %mix_last.1 = bf16[2048,256]{1,0:T(8,128)(2,1)} custom-call(bf16[256,256]{1,0:T(8,128)(2,1)S(1)} %collective-permute-done.refs_17_.refs_0_, bf16[256,256]{1,0:T(8,128)(2,1)S(1)} %collective-permute-done.1.refs_18_.refs_1_, bf16[16,96,128]{2,1,0:T(8,128)(2,1)S(1)} %collective-permute-done.12.refs_2_, ...), custom_call_target="tpu_custom_call" | custom-call | flops 536870912 | bytes 4194304 | tf_op jit(solution)/shard_map/mix_last/pallas_call | solution.py:361
  (36 shorter events, 0.1 us)
Async XLA Ops:
  0.0 1.2 %copy-start.1 = (bf16[2048,256]{1,0:T(8,128)(2,1)S(1)}, bf16[2048,256]{1,0:T(8,128)(2,1)}, u32[]{:S(2)}) copy-start(bf16[2048,256]{1,0:T(8,128)(2,1)} %f_ref.1) | copy-start | bytes 3145732
  1.2 9.1 %copy-start.4 = (bf16[256,1024]{1,0:T(8,128)(2,1)S(1)}, bf16[256,1024]{1,0:T(8,128)(2,1)}, u32[]{:S(2)}) copy-start(bf16[256,1024]{1,0:T(8,128)(2,1)} %w_ref.1) | copy-start | bytes 1572868
  1.2 9.2 %copy-start.17 = (f32[256]{0:T(256)S(1)}, f32[256]{0:T(256)}, u32[]{:S(2)}) copy-start(f32[256]{0:T(256)} %param.14) | copy-start | bytes 3076
  3.1 45.8 %all-to-all-start = ((bf16[8,32,16,128]{3,2,1,0:T(8,128)(2,1)}), bf16[8,32,16,128]{3,2,1,0:T(8,128)(2,1)S(1)}, u32[]{:S(2)}, u32[]{:S(2)}) async-start(bf16[8,32,16,128]{3,2,1,0:T(8,128)(2,1)} %filter_blocks.1._), calls=%async_computation | async-start | bytes 2097152 | tf_op jit(solution)/shard_map/all_to_all | solution.py:384
  10.7 14.6 %collective-permute-start = (bf16[256,256]{1,0:T(8,128)(2,1)S(1)}, bf16[256,256]{1,0:T(8,128)(2,1)S(1)}, u32[]{:S(2)}, u32[]{:S(2)}) collective-permute-start(bf16[256,256]{1,0:T(8,128)(2,1)S(1)} %get-tuple-element.30), channel_id=1, source_target_pairs={{0,2},{1,3},{2,0},{3,1},{4,6},{5,7},{6,4},{7,5},{8,10},{9,11},{10,... | collective-permute-start | bytes 393224 | tf_op jit(solution)/shard_map/ppermute | solution.py:374
  12.2 13.1 %collective-permute-start.1 = (bf16[256,256]{1,0:T(8,128)(2,1)S(1)}, bf16[256,256]{1,0:T(8,128)(2,1)S(1)}, u32[]{:S(2)}, u32[]{:S(2)}) collective-permute-start(bf16[256,256]{1,0:T(8,128)(2,1)S(1)} %get-tuple-element.31), channel_id=1, source_target_pairs={{0,3},{1,2},{2,1},{3,0},{4,7},{5,6},{6,5},{7,4},{8,11},{9,10},{10,... | collective-permute-start | bytes 393224 | tf_op jit(solution)/shard_map/ppermute | solution.py:374
  12.2 15.9 %collective-permute-start.9 = (bf16[256,256]{1,0:T(8,128)(2,1)S(1)}, bf16[256,256]{1,0:T(8,128)(2,1)S(1)}, u32[]{:S(2)}, u32[]{:S(2)}) collective-permute-start(bf16[256,256]{1,0:T(8,128)(2,1)S(1)} %get-tuple-element.43), channel_id=1, source_target_pairs={{0,1},{1,0},{2,3},{3,2},{4,5},{5,4},{6,7},{7,6},{8,9},{9,8},{10,11... | collective-permute-start | bytes 393224 | tf_op jit(solution)/shard_map/ppermute | solution.py:374
  12.9 36.0 %copy-start.3 = (bf16[256,256]{1,0:T(8,128)(2,1)S(1)}, bf16[256,256]{1,0:T(8,128)(2,1)}, u32[]{:S(2)}) copy-start(bf16[256,256]{1,0:T(8,128)(2,1)} %constant.19.b_fwd.refs_10_) | copy-start | bytes 393220
  12.9 36.0 %copy-start.5 = (bf16[256,128]{1,0:T(8,128)(2,1)S(1)}, bf16[256,128]{1,0:T(8,128)(2,1)}, u32[]{:S(2)}) copy-start(bf16[256,128]{1,0:T(8,128)(2,1)} %constant.18.a_fwd.refs_9_) | copy-start | bytes 196612
  12.9 36.0 %copy-start.6 = (f32[128,128]{1,0:T(8,128)S(1)}, f32[128,128]{1,0:T(8,128)}, u32[]{:S(2)}) copy-start(f32[128,128]{1,0:T(8,128)} %constant.17.clone.ts_ref.refs_14_) | copy-start | bytes 196612
  12.9 36.0 %copy-start.7 = (f32[128,128]{1,0:T(8,128)S(1)}, f32[128,128]{1,0:T(8,128)}, u32[]{:S(2)}) copy-start(f32[128,128]{1,0:T(8,128)} %constant.16.clone.tc_ref.refs_13_) | copy-start | bytes 196612
  21.7 33.2 %copy-start.2 = (bf16[32,16,128]{2,1,0:T(8,128)(2,1)S(1)}, bf16[32,16,128]{2,1,0:T(8,128)(2,1)}, u32[]{:S(2)}) copy-start(bf16[32,16,128]{2,1,0:T(8,128)(2,1)} %get-tuple-element.34.refs_0_.refs_5_) | copy-start | bytes 393220
  21.7 33.2 %copy-start.13 = (bf16[256,256]{1,0:T(8,128)(2,1)S(1)}, bf16[256,256]{1,0:T(8,128)(2,1)}, u32[]{:S(2)}) copy-start(bf16[256,256]{1,0:T(8,128)(2,1)} %constant.20.refs_11_) | copy-start | bytes 393220
  21.7 33.3 %copy-start.16 = (bf16[128,256]{1,0:T(8,128)(2,1)S(1)}, bf16[128,256]{1,0:T(8,128)(2,1)}, u32[]{:S(2)}) copy-start(bf16[128,256]{1,0:T(8,128)(2,1)} %constant.21.refs_12_) | copy-start | bytes 196612
  21.7 8.3 %collective-permute-start.2 = (bf16[32,16,128]{2,1,0:T(8,128)(2,1)}, bf16[32,16,128]{2,1,0:T(8,128)(2,1)S(1)}, u32[]{:S(2)}, u32[]{:S(2)}) collective-permute-start(bf16[32,16,128]{2,1,0:T(8,128)(2,1)} %get-tuple-element.35.refs_5_), channel_id=1, source_target_pairs={{0,4},{4,0},{8,12},{12,8},{16,20},{20,16},{24,28},{28,24},{1,5},{5... | collective-permute-start | bytes 393224 | tf_op jit(solution)/shard_map/ppermute | solution.py:374
  23.8 9.8 %collective-permute-start.3 = (bf16[32,16,128]{2,1,0:T(8,128)(2,1)}, bf16[32,16,128]{2,1,0:T(8,128)(2,1)S(1)}, u32[]{:S(2)}, u32[]{:S(2)}) collective-permute-start(bf16[32,16,128]{2,1,0:T(8,128)(2,1)} %get-tuple-element.36.refs_3_), channel_id=1, source_target_pairs={{0,8},{4,12},{8,0},{12,4},{16,24},{20,28},{24,16},{28,20},{1,9},{5... | collective-permute-start | bytes 393224 | tf_op jit(solution)/shard_map/ppermute | solution.py:374
  25.2 25.1 %collective-permute-start.4 = (bf16[32,16,128]{2,1,0:T(8,128)(2,1)}, bf16[32,16,128]{2,1,0:T(8,128)(2,1)S(1)}, u32[]{:S(2)}, u32[]{:S(2)}) collective-permute-start(bf16[32,16,128]{2,1,0:T(8,128)(2,1)} %get-tuple-element.37.refs_4_), channel_id=1, source_target_pairs={{0,12},{4,8},{8,4},{12,0},{16,28},{20,24},{24,20},{28,16},{1,13},{... | collective-permute-start | bytes 393224 | tf_op jit(solution)/shard_map/ppermute | solution.py:374
  25.3 26.3 %collective-permute-start.5 = (bf16[32,16,128]{2,1,0:T(8,128)(2,1)}, bf16[32,16,128]{2,1,0:T(8,128)(2,1)S(1)}, u32[]{:S(2)}, u32[]{:S(2)}) collective-permute-start(bf16[32,16,128]{2,1,0:T(8,128)(2,1)} %get-tuple-element.38.refs_3_), channel_id=1, source_target_pairs={{0,16},{4,20},{8,24},{12,28},{16,0},{20,4},{24,8},{28,12},{1,17},{... | collective-permute-start | bytes 393224 | tf_op jit(solution)/shard_map/ppermute | solution.py:374
  28.2 26.7 %collective-permute-start.6 = (bf16[32,16,128]{2,1,0:T(8,128)(2,1)}, bf16[32,16,128]{2,1,0:T(8,128)(2,1)S(1)}, u32[]{:S(2)}, u32[]{:S(2)}) collective-permute-start(bf16[32,16,128]{2,1,0:T(8,128)(2,1)} %get-tuple-element.39.refs_4_), channel_id=1, source_target_pairs={{0,20},{4,16},{8,28},{12,24},{16,4},{20,0},{24,12},{28,8},{1,21},{... | collective-permute-start | bytes 393224 | tf_op jit(solution)/shard_map/ppermute | solution.py:374
  30.0 24.9 %collective-permute-start.7 = (bf16[32,16,128]{2,1,0:T(8,128)(2,1)}, bf16[32,16,128]{2,1,0:T(8,128)(2,1)S(1)}, u32[]{:S(2)}, u32[]{:S(2)}) collective-permute-start(bf16[32,16,128]{2,1,0:T(8,128)(2,1)} %get-tuple-element.40.refs_2_), channel_id=1, source_target_pairs={{0,24},{4,28},{8,16},{12,20},{16,8},{20,12},{24,0},{28,4},{1,25},{... | collective-permute-start | bytes 393224 | tf_op jit(solution)/shard_map/ppermute | solution.py:374
  33.5 21.4 %collective-permute-start.8 = (bf16[32,16,128]{2,1,0:T(8,128)(2,1)}, bf16[32,16,128]{2,1,0:T(8,128)(2,1)S(1)}, u32[]{:S(2)}, u32[]{:S(2)}) collective-permute-start(bf16[32,16,128]{2,1,0:T(8,128)(2,1)} %get-tuple-element.41.refs_3_), channel_id=1, source_target_pairs={{0,28},{4,24},{8,20},{12,16},{16,12},{20,8},{24,4},{28,0},{1,29},{... | collective-permute-start | bytes 393224 | tf_op jit(solution)/shard_map/ppermute | solution.py:374
  50.3 21.1 %copy-start = (bf16[8,32,16,128]{3,2,1,0:T(8,128)(2,1)S(1)}, bf16[8,32,16,128]{3,2,1,0:T(8,128)(2,1)}, u32[]{:S(2)}) copy-start(bf16[8,32,16,128]{3,2,1,0:T(8,128)(2,1)} %get-tuple-element.32.gates) | copy-start | bytes 3145732
  50.3 21.1 %copy-start.10 = (bf16[32,16,128]{2,1,0:T(8,128)(2,1)S(1)}, bf16[32,16,128]{2,1,0:T(8,128)(2,1)}, u32[]{:S(2)}) copy-start(bf16[32,16,128]{2,1,0:T(8,128)(2,1)} %get-tuple-element.35.refs_5_) | copy-start | bytes 393220
  50.3 21.1 %copy-start.11 = (bf16[32,16,128]{2,1,0:T(8,128)(2,1)S(1)}, bf16[32,16,128]{2,1,0:T(8,128)(2,1)}, u32[]{:S(2)}) copy-start(bf16[32,16,128]{2,1,0:T(8,128)(2,1)} %get-tuple-element.36.refs_3_) | copy-start | bytes 393220
  50.3 21.1 %copy-start.12 = (bf16[32,16,128]{2,1,0:T(8,128)(2,1)S(1)}, bf16[32,16,128]{2,1,0:T(8,128)(2,1)}, u32[]{:S(2)}) copy-start(bf16[32,16,128]{2,1,0:T(8,128)(2,1)} %get-tuple-element.37.refs_4_) | copy-start | bytes 393220
  54.9 23.7 %copy-start.8 = (bf16[32,16,128]{2,1,0:T(8,128)(2,1)S(1)}, bf16[32,16,128]{2,1,0:T(8,128)(2,1)}, u32[]{:S(2)}) copy-start(bf16[32,16,128]{2,1,0:T(8,128)(2,1)} %get-tuple-element.38.refs_3_) | copy-start | bytes 393220
  54.9 23.7 %copy-start.9 = (bf16[32,16,128]{2,1,0:T(8,128)(2,1)S(1)}, bf16[32,16,128]{2,1,0:T(8,128)(2,1)}, u32[]{:S(2)}) copy-start(bf16[32,16,128]{2,1,0:T(8,128)(2,1)} %get-tuple-element.39.refs_4_) | copy-start | bytes 393220
  55.0 34.9 %copy-start.14 = (bf16[32,16,128]{2,1,0:T(8,128)(2,1)S(1)}, bf16[32,16,128]{2,1,0:T(8,128)(2,1)}, u32[]{:S(2)}) copy-start(bf16[32,16,128]{2,1,0:T(8,128)(2,1)} %get-tuple-element.40.refs_2_) | copy-start | bytes 393220
  55.0 34.9 %copy-start.15 = (bf16[32,16,128]{2,1,0:T(8,128)(2,1)S(1)}, bf16[32,16,128]{2,1,0:T(8,128)(2,1)}, u32[]{:S(2)}) copy-start(bf16[32,16,128]{2,1,0:T(8,128)(2,1)} %get-tuple-element.41.refs_3_) | copy-start | bytes 393220
  57.5 10.7 %collective-permute-start.15 = (bf16[32,16,128]{2,1,0:T(8,128)(2,1)S(1)}, bf16[32,16,128]{2,1,0:T(8,128)(2,1)S(1)}, u32[]{:S(2)}, u32[]{:S(2)}) collective-permute-start(bf16[32,16,128]{2,1,0:T(8,128)(2,1)S(1)} %get-tuple-element.50), channel_id=1, source_target_pairs={{0,8},{4,12},{8,0},{12,4},{16,24},{20,28},{24,16},{28,20},{1,9},{5... | collective-permute-start | bytes 393224 | tf_op jit(solution)/shard_map/ppermute | solution.py:374
  62.7 8.7 %collective-permute-start.16 = (bf16[32,16,128]{2,1,0:T(8,128)(2,1)S(1)}, bf16[32,16,128]{2,1,0:T(8,128)(2,1)S(1)}, u32[]{:S(2)}, u32[]{:S(2)}) collective-permute-start(bf16[32,16,128]{2,1,0:T(8,128)(2,1)S(1)} %get-tuple-element.51), channel_id=1, source_target_pairs={{0,12},{4,8},{8,4},{12,0},{16,28},{20,24},{24,20},{28,16},{1,13},{... | collective-permute-start | bytes 393224 | tf_op jit(solution)/shard_map/ppermute | solution.py:374
  62.8 8.5 %collective-permute-start.17 = (bf16[32,16,128]{2,1,0:T(8,128)(2,1)S(1)}, bf16[32,16,128]{2,1,0:T(8,128)(2,1)S(1)}, u32[]{:S(2)}, u32[]{:S(2)}) collective-permute-start(bf16[32,16,128]{2,1,0:T(8,128)(2,1)S(1)} %get-tuple-element.52), channel_id=1, source_target_pairs={{0,4},{4,0},{8,12},{12,8},{16,20},{20,16},{24,28},{28,24},{1,5},{5... | collective-permute-start | bytes 393224 | tf_op jit(solution)/shard_map/ppermute | solution.py:374
  64.2 12.6 %collective-permute-start.10 = (bf16[32,16,128]{2,1,0:T(8,128)(2,1)S(1)}, bf16[32,16,128]{2,1,0:T(8,128)(2,1)S(1)}, u32[]{:S(2)}, u32[]{:S(2)}) collective-permute-start(bf16[32,16,128]{2,1,0:T(8,128)(2,1)S(1)} %get-tuple-element.44), channel_id=1, source_target_pairs={{0,16},{4,20},{8,24},{12,28},{16,0},{20,4},{24,8},{28,12},{1,17},{... | collective-permute-start | bytes 393224 | tf_op jit(solution)/shard_map/ppermute | solution.py:374
  66.1 12.4 %collective-permute-start.11 = (bf16[32,16,128]{2,1,0:T(8,128)(2,1)S(1)}, bf16[32,16,128]{2,1,0:T(8,128)(2,1)S(1)}, u32[]{:S(2)}, u32[]{:S(2)}) collective-permute-start(bf16[32,16,128]{2,1,0:T(8,128)(2,1)S(1)} %get-tuple-element.45), channel_id=1, source_target_pairs={{0,20},{4,16},{8,28},{12,24},{16,4},{20,0},{24,12},{28,8},{1,21},{... | collective-permute-start | bytes 393224 | tf_op jit(solution)/shard_map/ppermute | solution.py:374
  71.9 18.9 %collective-permute-start.18 = (bf16[16,96,128]{2,1,0:T(8,128)(2,1)S(1)}, bf16[16,96,128]{2,1,0:T(8,128)(2,1)S(1)}, u32[]{:S(2)}, u32[]{:S(2)}) collective-permute-start(bf16[16,96,128]{2,1,0:T(8,128)(2,1)S(1)} %apply_gate.5.refs_3_), channel_id=1, source_target_pairs={{0,2},{1,3},{2,0},{3,1},{4,6},{5,7},{6,4},{7,5},{8,10},{9,11},{10,... | collective-permute-start | bytes 1179656 | tf_op jit(solution)/shard_map/ppermute | solution.py:374
  79.1 12.2 %collective-permute-start.12 = (bf16[16,96,128]{2,1,0:T(8,128)(2,1)S(1)}, bf16[16,96,128]{2,1,0:T(8,128)(2,1)S(1)}, u32[]{:S(2)}, u32[]{:S(2)}) collective-permute-start(bf16[16,96,128]{2,1,0:T(8,128)(2,1)S(1)} %apply_gate.3.refs_2_), channel_id=1, source_target_pairs={{0,2},{1,3},{2,0},{3,1},{4,6},{5,7},{6,4},{7,5},{8,10},{9,11},{10,... | collective-permute-start | bytes 1179656 | tf_op jit(solution)/shard_map/ppermute | solution.py:374
  80.6 7.7 %collective-permute-start.13 = (bf16[32,16,128]{2,1,0:T(8,128)(2,1)S(1)}, bf16[32,16,128]{2,1,0:T(8,128)(2,1)S(1)}, u32[]{:S(2)}, u32[]{:S(2)}) collective-permute-start(bf16[32,16,128]{2,1,0:T(8,128)(2,1)S(1)} %get-tuple-element.47), channel_id=1, source_target_pairs={{0,24},{4,28},{8,16},{12,20},{16,8},{20,12},{24,0},{28,4},{1,25},{... | collective-permute-start | bytes 393224 | tf_op jit(solution)/shard_map/ppermute | solution.py:374
  81.8 8.0 %collective-permute-start.14 = (bf16[32,16,128]{2,1,0:T(8,128)(2,1)S(1)}, bf16[32,16,128]{2,1,0:T(8,128)(2,1)S(1)}, u32[]{:S(2)}, u32[]{:S(2)}) collective-permute-start(bf16[32,16,128]{2,1,0:T(8,128)(2,1)S(1)} %get-tuple-element.48), channel_id=1, source_target_pairs={{0,28},{4,24},{8,20},{12,16},{16,12},{20,8},{24,4},{28,0},{1,29},{... | collective-permute-start | bytes 393224 | tf_op jit(solution)/shard_map/ppermute | solution.py:374
  90.1 1.6 %collective-permute-start.22 = (bf16[16,64,128]{2,1,0:T(8,128)(2,1)S(1)}, bf16[16,64,128]{2,1,0:T(8,128)(2,1)S(1)}, u32[]{:S(2)}, u32[]{:S(2)}) collective-permute-start(bf16[16,64,128]{2,1,0:T(8,128)(2,1)S(1)} %apply_gate.4.refs_4_), channel_id=1, source_target_pairs={{0,1},{1,0},{2,3},{3,2},{4,5},{5,4},{6,7},{7,6},{8,9},{9,8},{10,11... | collective-permute-start | bytes 786440 | tf_op jit(solution)/shard_map/ppermute | solution.py:374
  90.2 2.1 %collective-permute-start.21 = (bf16[16,96,128]{2,1,0:T(8,128)(2,1)S(1)}, bf16[16,96,128]{2,1,0:T(8,128)(2,1)S(1)}, u32[]{:S(2)}, u32[]{:S(2)}) collective-permute-start(bf16[16,96,128]{2,1,0:T(8,128)(2,1)S(1)} %apply_gate.5.refs_3_), channel_id=1, source_target_pairs={{0,1},{1,0},{2,3},{3,2},{4,5},{5,4},{6,7},{7,6},{8,9},{9,8},{10,11... | collective-permute-start | bytes 1179656 | tf_op jit(solution)/shard_map/ppermute | solution.py:374
  90.7 2.1 %collective-permute-start.20 = (bf16[16,96,128]{2,1,0:T(8,128)(2,1)S(1)}, bf16[16,96,128]{2,1,0:T(8,128)(2,1)S(1)}, u32[]{:S(2)}, u32[]{:S(2)}) collective-permute-start(bf16[16,96,128]{2,1,0:T(8,128)(2,1)S(1)} %apply_gate.3.refs_2_), channel_id=1, source_target_pairs={{0,1},{1,0},{2,3},{3,2},{4,5},{5,4},{6,7},{7,6},{8,9},{9,8},{10,11... | collective-permute-start | bytes 1179656 | tf_op jit(solution)/shard_map/ppermute | solution.py:374
  90.8 9.3 %collective-permute-start.24 = (bf16[16,96,128]{2,1,0:T(8,128)(2,1)S(1)}, bf16[16,96,128]{2,1,0:T(8,128)(2,1)S(1)}, u32[]{:S(2)}, u32[]{:S(2)}) collective-permute-start(bf16[16,96,128]{2,1,0:T(8,128)(2,1)S(1)} %collective-permute-done.18.refs_3_), channel_id=1, source_target_pairs={{0,1},{1,0},{2,3},{3,2},{4,5},{5,4},{6,7},{7,6},{8,9},{9,8},{10,11... | collective-permute-start | bytes 1179656 | tf_op jit(solution)/shard_map/ppermute | solution.py:374
  91.2 8.9 %collective-permute-start.23 = (bf16[16,96,128]{2,1,0:T(8,128)(2,1)S(1)}, bf16[16,96,128]{2,1,0:T(8,128)(2,1)S(1)}, u32[]{:S(2)}, u32[]{:S(2)}) collective-permute-start(bf16[16,96,128]{2,1,0:T(8,128)(2,1)S(1)} %collective-permute-done.12.refs_2_), channel_id=1, source_target_pairs={{0,1},{1,0},{2,3},{3,2},{4,5},{5,4},{6,7},{7,6},{8,9},{9,8},{10,11... | collective-permute-start | bytes 1179656 | tf_op jit(solution)/shard_map/ppermute | solution.py:374
  91.7 8.3 %collective-permute-start.19 = (bf16[16,64,128]{2,1,0:T(8,128)(2,1)S(1)}, bf16[16,64,128]{2,1,0:T(8,128)(2,1)S(1)}, u32[]{:S(2)}, u32[]{:S(2)}) collective-permute-start(bf16[16,64,128]{2,1,0:T(8,128)(2,1)S(1)} %apply_gate.4.refs_4_), channel_id=1, source_target_pairs={{0,2},{1,3},{2,0},{3,1},{4,6},{5,7},{6,4},{7,5},{8,10},{9,11},{10,... | collective-permute-start | bytes 786440 | tf_op jit(solution)/shard_map/ppermute | solution.py:374
  100.1 1.5 %collective-permute-start.25 = (bf16[16,64,128]{2,1,0:T(8,128)(2,1)S(1)}, bf16[16,64,128]{2,1,0:T(8,128)(2,1)S(1)}, u32[]{:S(2)}, u32[]{:S(2)}) collective-permute-start(bf16[16,64,128]{2,1,0:T(8,128)(2,1)S(1)} %collective-permute-done.19.refs_4_), channel_id=1, source_target_pairs={{0,1},{1,0},{2,3},{3,2},{4,5},{5,4},{6,7},{7,6},{8,9},{9,8},{10,11... | collective-permute-start | bytes 786440 | tf_op jit(solution)/shard_map/ppermute | solution.py:374
